TPU v7x, 32 devices: a whole 2x2x4 slice. The times are simulated.
32 devices in a mesh: seq: 8 (over z, y), fsdp: 4 (over x, core).
Axes of the slice: x: 2, y: 2, z: 4, core: 2. Of those that a mesh axis runs over, the one named last changes fastest.
Arguments:
- tokens: bfloat16 [8, 4096, 768], P('fsdp', 'seq'), may hold values from -6 to 6
- norm_gain_attn: bfloat16 [768], P('fsdp'), may hold values from 0.5 to 1.5
- qkv_weight: bfloat16 [768, 2304], P('fsdp'), may hold values from -0.21875 to 0.21875
- attn_out_weight: bfloat16 [768, 768], P('fsdp'), may hold values from -2.5 to 2.5
- norm_gain_mlp: bfloat16 [768], P('fsdp'), may hold values from 0.5 to 1.5
- mlp_in_weight: bfloat16 [768, 2304], P('fsdp'), may hold values from -0.21875 to 0.21875
- mlp_out_weight: bfloat16 [1152, 768], P('fsdp'), may hold values from -0.1875 to 0.1875
- grad_out: bfloat16 [8, 4096, 768], P('fsdp', 'seq'), may hold values from -16 to 16
Outputs:
- block_out: bfloat16 [8, 4096, 768], P('fsdp', 'seq')
- tokens_grad: float32 [8, 4096, 768], P('fsdp', 'seq')
- norm_gain_attn_grad: float32 [768], P('fsdp')
- qkv_weight_grad: float32 [768, 2304], P('fsdp')
- attn_out_weight_grad: float32 [768, 768], P('fsdp')
- norm_gain_mlp_grad: float32 [768], P('fsdp')
- mlp_in_weight_grad: float32 [768, 2304], P('fsdp')
- mlp_out_weight_grad: float32 [1152, 768], P('fsdp')
All inputs are finite; a program needn't handle non-finite values.
Results may differ from a plain program's by a relative error of at most 0.018.
Values may be sent and summed in bfloat16 or wider, within the bound.
A program may use at most 256 MiB of HBM per device.

v0:
```python
import math

import jax
import jax.numpy as jnp
from jax import lax
from jax.sharding import PartitionSpec as P

HEADS = 12
HEAD_DIM = 64
FF = 1152
WIN = 64


epsilon = 1e-05
rope_base = 10000.0
negative = -1e30


def padded(block, sides, width):
    for axis, dim in sides:
        count = lax.axis_size(axis)
        forward = [(i, i + 1) for i in range(count - 1)]
        backward = [(target, source) for source, target in forward]
        low = lax.ppermute(
            lax.slice_in_dim(block, block.shape[dim] - width, None, axis=dim), axis, forward
        )
        high = lax.ppermute(lax.slice_in_dim(block, 0, width, axis=dim), axis, backward)
        block = jnp.concatenate([low, block, high], axis=dim)
    return block


def from_behind(block, axis, distance):
    devices = range(lax.axis_size(axis))
    route = [(i - distance, i) for i in devices if i - distance in devices]
    return lax.ppermute(block, axis, route)


def norm_forward(values, gain_row):
    center = values - jnp.mean(values, axis=-1, keepdims=True)
    inverse = lax.rsqrt(jnp.mean(center * center, axis=-1, keepdims=True) + epsilon)
    unit_rows = center * inverse
    return (unit_rows * gain_row, unit_rows, inverse)


def norm_backward(upstream, unit_rows, inverse, gain_row):
    scaled = upstream * gain_row
    gain_grad = jnp.sum(upstream * unit_rows, axis=(0, 1))
    inner = (
        scaled
        - jnp.mean(scaled, axis=-1, keepdims=True)
        - unit_rows * jnp.mean(scaled * unit_rows, axis=-1, keepdims=True)
    )
    return (inner * inverse, gain_grad)


def rope_tables(positions):
    half_dim = HEAD_DIM // 2
    freqs = rope_base ** (-(jnp.arange(half_dim, dtype=jnp.float32) * 2.0 / HEAD_DIM))
    angles = positions[:, None] * freqs[None, :]
    angles = jnp.concatenate([angles, angles], axis=-1)
    return (jnp.cos(angles), jnp.sin(angles))


def rotate(values, cosine, sine):
    half_dim = HEAD_DIM // 2
    turned = jnp.concatenate([-values[..., half_dim:], values[..., :half_dim]], axis=-1)
    return values * cosine[:, None, :] + turned * sine[:, None, :]


def rotate_back(upstream, cosine, sine):
    half_dim = HEAD_DIM // 2
    turned = upstream * sine[:, None, :]
    moved = jnp.concatenate([turned[..., half_dim:], -turned[..., :half_dim]], axis=-1)
    return upstream * cosine[:, None, :] + moved


def gated(first_half, second_half):
    return jax.nn.gelu(first_half, approximate=False) * second_half


def band_scores(query, key_block, inside):
    score_scale = 1.0 / math.sqrt(HEAD_DIM)
    scores = (
        jnp.einsum("sqhd,skhd->shqk", query, key_block, preferred_element_type=jnp.float32)
        * score_scale
    )
    return jnp.where(inside[None, None], scores, negative)


def shards(
    tokens,
    norm_gain_attn,
    qkv_weight,
    attn_out_weight,
    norm_gain_mlp,
    mlp_in_weight,
    mlp_out_weight,
    grad_out,
):
    seq_count, piece_len, model_width = tokens.shape
    key_span = piece_len + 2 * WIN
    score_scale = 1.0 / math.sqrt(HEAD_DIM)
    gain_low, weight_qkv, weight_attn, gain_mid, weight_in, weight_out = (
        lax.all_gather(norm_gain_attn, "fsdp", axis=0, tiled=True),
        lax.all_gather(qkv_weight, "fsdp", axis=0, tiled=True),
        lax.all_gather(attn_out_weight, "fsdp", axis=0, tiled=True),
        lax.all_gather(norm_gain_mlp, "fsdp", axis=0, tiled=True),
        lax.all_gather(mlp_in_weight, "fsdp", axis=0, tiled=True),
        lax.all_gather(mlp_out_weight, "fsdp", axis=0, tiled=True),
    )
    gain_attn = gain_low.astype(jnp.float32)
    gain_mlp = gain_mid.astype(jnp.float32)
    piece_start = lax.axis_index("seq") * piece_len
    full_length = piece_len * lax.axis_size("seq")
    position_ids = piece_start + jnp.arange(piece_len, dtype=jnp.int32)
    key_positions = piece_start - WIN + jnp.arange(key_span, dtype=jnp.int32)
    inside = (
        (jnp.abs(position_ids[:, None] - key_positions[None, :]) <= WIN)
        & (key_positions[None, :] >= 0)
        & (key_positions[None, :] < full_length)
    )
    cosine, sine = rope_tables(position_ids.astype(jnp.float32))
    inputs = tokens.astype(jnp.float32)
    normed_full, unit_attn, inverse_attn = norm_forward(inputs, gain_attn)
    normed = normed_full.astype(jnp.bfloat16)
    projected = jnp.dot(normed, weight_qkv, preferred_element_type=jnp.float32).reshape(
        seq_count, piece_len, 3, HEADS, HEAD_DIM
    )
    query = rotate(projected[:, :, 0], cosine, sine).astype(jnp.bfloat16)
    key_local = rotate(projected[:, :, 1], cosine, sine).astype(jnp.bfloat16)
    value_local = projected[:, :, 2].astype(jnp.bfloat16)
    key_value = jnp.concatenate(
        [
            key_local.reshape(seq_count, piece_len, model_width),
            value_local.reshape(seq_count, piece_len, model_width),
        ],
        axis=-1,
    )
    extended = padded(key_value, (("seq", 1),), WIN)
    key_block = extended[..., :model_width].reshape(seq_count, key_span, HEADS, HEAD_DIM)
    value_block = extended[..., model_width:].reshape(seq_count, key_span, HEADS, HEAD_DIM)
    scores = band_scores(query, key_block, inside)
    highest = jnp.max(scores, axis=-1, keepdims=True)
    raised = jnp.exp(scores - highest)
    summed = jnp.sum(raised, axis=-1, keepdims=True)
    weights = (raised / summed).astype(jnp.bfloat16)
    log_total = highest + jnp.log(summed)
    attended = jnp.einsum(
        "shqk,skhd->sqhd", weights, value_block, preferred_element_type=jnp.float32
    )
    attended = attended.reshape(seq_count, piece_len, model_width).astype(jnp.bfloat16)
    middle = inputs + jnp.dot(attended, weight_attn, preferred_element_type=jnp.float32)
    normed_mlp_full, unit_mlp, inverse_mlp = norm_forward(middle, gain_mlp)
    normed_mlp = normed_mlp_full.astype(jnp.bfloat16)
    widened = jnp.dot(normed_mlp, weight_in, preferred_element_type=jnp.float32)
    hidden_full, gated_back = jax.vjp(gated, widened[..., :FF], widened[..., FF:])
    hidden = hidden_full.astype(jnp.bfloat16)
    block_out = (middle + jnp.dot(hidden, weight_out, preferred_element_type=jnp.float32)).astype(
        jnp.bfloat16
    )
    upstream = grad_out.astype(jnp.float32)
    out_grad = jnp.einsum("spf,spd->fd", hidden, grad_out, preferred_element_type=jnp.float32)
    hidden_grad = jnp.einsum(
        "spd,fd->spf", grad_out, weight_out, preferred_element_type=jnp.float32
    )
    first_grad, second_grad = gated_back(hidden_grad)
    widened_grad = jnp.concatenate([first_grad, second_grad], axis=-1).astype(jnp.bfloat16)
    in_grad = jnp.einsum(
        "spd,spf->df", normed_mlp, widened_grad, preferred_element_type=jnp.float32
    )
    normed_mlp_grad = jnp.einsum(
        "spf,df->spd", widened_grad, weight_in, preferred_element_type=jnp.float32
    )
    mlp_norm_part, gain_mlp_grad = norm_backward(normed_mlp_grad, unit_mlp, inverse_mlp, gain_mlp)
    middle_grad = upstream + mlp_norm_part
    middle_low = middle_grad.astype(jnp.bfloat16)
    attn_grad = jnp.einsum("spd,spe->de", attended, middle_low, preferred_element_type=jnp.float32)
    attended_grad = jnp.einsum(
        "spe,de->spd", middle_low, weight_attn, preferred_element_type=jnp.float32
    )
    attended_grad = attended_grad.astype(jnp.bfloat16).reshape(
        seq_count, piece_len, HEADS, HEAD_DIM
    )
    key_back, value_back = (key_block, value_block)
    scores_back = band_scores(query, key_back, inside)
    probs = jnp.exp(scores_back - log_total)
    prob_grad = jnp.einsum(
        "sqhd,skhd->shqk", attended_grad, value_back, preferred_element_type=jnp.float32
    )
    centered = prob_grad - jnp.sum(probs * prob_grad, axis=-1, keepdims=True)
    score_grad = (probs * centered).astype(jnp.bfloat16)
    query_grad = (
        jnp.einsum("shqk,skhd->sqhd", score_grad, key_back, preferred_element_type=jnp.float32)
        * score_scale
    )
    key_grad = (
        jnp.einsum("shqk,sqhd->skhd", score_grad, query, preferred_element_type=jnp.float32)
        * score_scale
    )
    value_grad = jnp.einsum(
        "shqk,sqhd->skhd",
        probs.astype(jnp.bfloat16),
        attended_grad,
        preferred_element_type=jnp.float32,
    )
    edge_grad = jnp.concatenate(
        [
            key_grad.reshape(seq_count, key_span, model_width),
            value_grad.reshape(seq_count, key_span, model_width),
        ],
        axis=-1,
    )
    from_right = from_behind(edge_grad[:, :WIN].astype(jnp.bfloat16), "seq", -1).astype(jnp.float32)
    from_left = from_behind(edge_grad[:, piece_len + WIN :].astype(jnp.bfloat16), "seq", 1).astype(
        jnp.float32
    )
    own_grad = edge_grad[:, WIN : WIN + piece_len]
    own_grad = own_grad + jnp.pad(from_left, ((0, 0), (0, piece_len - WIN), (0, 0)))
    own_grad = own_grad + jnp.pad(from_right, ((0, 0), (piece_len - WIN, 0), (0, 0)))
    key_own = own_grad[..., :model_width].reshape(seq_count, piece_len, HEADS, HEAD_DIM)
    value_own = own_grad[..., model_width:].reshape(seq_count, piece_len, HEADS, HEAD_DIM)
    projected_grad = jnp.stack(
        [rotate_back(query_grad, cosine, sine), rotate_back(key_own, cosine, sine), value_own],
        axis=2,
    )
    projected_grad = projected_grad.reshape(seq_count, piece_len, 3 * model_width).astype(
        jnp.bfloat16
    )
    qkv_grad = jnp.einsum("spd,spe->de", normed, projected_grad, preferred_element_type=jnp.float32)
    normed_grad = jnp.einsum(
        "spe,de->spd", projected_grad, weight_qkv, preferred_element_type=jnp.float32
    )
    attn_norm_part, gain_attn_grad = norm_backward(normed_grad, unit_attn, inverse_attn, gain_attn)
    tokens_grad = middle_grad + attn_norm_part
    shares = (
        lax.psum_scatter(
            gain_attn_grad.astype(jnp.bfloat16), "fsdp", scatter_dimension=0, tiled=True
        ).astype(jnp.float32),
        lax.psum_scatter(
            qkv_grad.astype(jnp.bfloat16), "fsdp", scatter_dimension=0, tiled=True
        ).astype(jnp.float32),
        lax.psum_scatter(
            attn_grad.astype(jnp.bfloat16), "fsdp", scatter_dimension=0, tiled=True
        ).astype(jnp.float32),
        lax.psum_scatter(
            gain_mlp_grad.astype(jnp.bfloat16), "fsdp", scatter_dimension=0, tiled=True
        ).astype(jnp.float32),
        lax.psum_scatter(
            in_grad.astype(jnp.bfloat16), "fsdp", scatter_dimension=0, tiled=True
        ).astype(jnp.float32),
        lax.psum_scatter(
            out_grad.astype(jnp.bfloat16), "fsdp", scatter_dimension=0, tiled=True
        ).astype(jnp.float32),
    )
    finals = lax.psum((shares[0], shares[1], shares[2], shares[3], shares[4], shares[5]), "seq")
    return (
        block_out,
        tokens_grad,
        finals[0],
        finals[1],
        finals[2],
        finals[3],
        finals[4],
        finals[5],
    )


def solution(mesh):
    return jax.shard_map(
        shards,
        mesh=mesh,
        in_specs=(
            P("fsdp", "seq", None),
            P("fsdp"),
            P("fsdp", None),
            P("fsdp", None),
            P("fsdp"),
            P("fsdp", None),
            P("fsdp", None),
            P("fsdp", "seq", None),
        ),
        out_specs=(
            P("fsdp", "seq", None),
            P("fsdp", "seq", None),
            P("fsdp"),
            P("fsdp", None),
            P("fsdp", None),
            P("fsdp"),
            P("fsdp", None),
            P("fsdp", None),
        ),
        check_vma=False,
    )
```

profile of v0, /device:TPU:0, one launch (start us, length us, event | category | flops | bytes accessed | tf_op | source)
XLA Modules:
  0.0 591.8 jit_solution(6652997142125301378)
XLA Ops:
  13.8 8.3 %all-reduce.8 = (bf16[768]{0:T(1024)(128)(2,1)S(1)}, bf16[768]{0:T(1024)(128)(2,1)S(1)}) all-reduce(bf16[768]{0:T(1024)(128)(2,1)S(1)} %dynamic-update-slice, bf16[768]{0:T(1024)(128)(2,1)S(1)} %dynamic-update-slice.1), channel_id=1, replica_groups=mesh['seq'=8,'fsdp'=4] {'fsdp'}, use_global_device_ids=true, to_apply=%add.2 | all-reduce | flops 1536 | bytes 6144
  24.1 18.9 %all-gather.5.cloned.1.call-done = bf16[768,2304]{1,0:T(8,128)(2,1)} async-done(((bf16[192,2304]{1,0:T(8,128)(2,1)}), bf16[768,2304]{1,0:T(8,128)(2,1)}) %all-gather.5.cloned.1.call-update) | async-done | bytes 3538960 | tf_op jit(solution)/shard_map/all_gather | solution.py:105
  43.1 6.0 %fusion.29 = f32[2,512,2304]{1,2,0:T(8,128)S(1)} fusion(bf16[768,2304]{1,0:T(8,128)(2,1)} %all-gather.5.cloned.1.call-done, bf16[2,512,768]{2,1,0:T(8,128)(2,1)S(1)} %copy-done.6, f32[768]{0:T(1024)S(1)} %convert_element_type.117, f32[2,512]{1,0:T(2,128)S(1)} %add_rsqrt_fusion.1, f32[2,512]{1,0:T(2,128)S(1)} %broadcast_multiply_fusion.9), kind=kOutput, calls=%fused_computation.59 | convolution fusion | flops 3627810816 | bytes 14560256 | tf_op jit(solution)/shard_map/dot_general | solution.py:126
  77.6 6.2 %collective-permute-done = bf16[2,64,1536]{2,1,0:T(8,128)(2,1)} collective-permute-done((bf16[2,64,1536]{2,1,0:T(8,128)(2,1)}, bf16[2,64,1536]{2,1,0:T(8,128)(2,1)}, u32[]{:S(2)}, u32[]{:S(2)}) %collective-permute-start) | collective-permute-done | bytes 393248 | tf_op jit(solution)/shard_map/ppermute | solution.py:24
  90.9 13.9 %fusion.74 = (f32[2,12,512]{2,1,0:T(8,128)S(1)}, f32[2,12,512,640]{3,2,1,0:T(8,128)}) fusion(bf16[2,512,12,64]{1,3,2,0:T(8,128)(2,1)S(1)} %fusion.40, bf16[2,640,12,64]{1,3,2,0:T(8,128)(2,1)S(1)} %bitcast.116, pred[512,640]{1,0:T(8,128)(4,1)S(1)} %fusion.55), kind=kOutput, calls=%fused_computation.150 | convolution fusion | flops 1030213632 | bytes 35373056 | tf_op jit(solution)/shard_map/sqhd,skhd->shqk/dot_general | solution.py:84
  104.8 13.8 %fusion = f32[2,12,512]{2,1,0:T(8,128)S(1)} fusion(f32[2,12,512,640]{3,2,1,0:T(8,128)} %get-tuple-element.52, f32[2,12,512]{2,1,0:T(8,128)S(1)} %get-tuple-element.51), kind=kLoop, calls=%fused_computation.6 | loop fusion | flops 15716352 | bytes 31555584 | tf_op jit(solution)/shard_map/reduce_sum | solution.py:145
  118.6 13.3 %fusion.49 = bf16[2,12,64,512]{3,2,1,0:T(8,128)(2,1)S(1)} fusion(bf16[2,640,12,64]{1,3,2,0:T(8,128)(2,1)S(1)} %bitcast.121, f32[2,12,512,640]{3,2,1,0:T(8,128)} %get-tuple-element.52, f32[2,12,512]{2,1,0:T(8,128)S(1)} %fusion, f32[2,12,512]{2,1,0:T(8,128)S(1)} %get-tuple-element.51), kind=kOutput, calls=%fused_computation.101 | convolution fusion | flops 1031012352 | bytes 35094528 | tf_op jit(solution)/shard_map/shqk,skhd->sqhd/dot_general | solution.py:148
  137.6 10.6 %fusion.25 = f32[2,512,2304]{2,1,0:T(8,128)} fusion(bf16[768,2304]{1,0:T(8,128)(2,1)} %all-gather.9.cloned.1.call-done, f32[2,512,768]{2,1,0:T(8,128)} %copy-done.13, f32[768]{0:T(1024)S(1)} %convert_element_type.127, f32[2,512]{1,0:T(2,128)S(1)} %add_rsqrt_fusion, f32[2,512]{1,0:T(2,128)S(1)} %broadcast_multiply_fusion.8), kind=kOutput, calls=%fused_computation.55 | convolution fusion | flops 3627024384 | bytes 16133120 | tf_op jit(solution)/shard_map/dot_general | solution.py:155
  148.1 16.1 %add_convert_fusion = (bf16[2,512,1152]{2,1,0:T(8,128)(2,1)}, f32[2,512,1152]{2,1,0:T(8,128)S(1)}, f32[2,512,1152]{2,1,0:T(8,128)S(1)}) fusion(f32[2,512,2304]{2,1,0:T(8,128)} %fusion.25, bf16[2,512,768]{2,1,0:T(8,128)(2,1)S(1)} %copy-done.28, bf16[1152,768]{1,0:T(8,128)(2,1)} %all-gather.11.cloned.1.call-done), kind=kOutput, calls=%fused_computation.28 | convolution fusion | flops 1898053632 | bytes 24576000 | tf_op jit(solution)/shard_map/spd,fd->spf/dot_general | solution.py:163
  168.9 6.6 %multiply_reduce_fusion.1 = (bf16[768]{0:T(1024)(128)(2,1)}, f32[2,512]{1,0:T(2,128)S(1)}, f32[2,512]{1,0:T(2,128)S(1)}, f32[2,512,768]{2,1,0:T(8,128)S(1)}) fusion(f32[2,512,768]{2,1,0:T(8,128)S(1)} %copy-done.14, f32[2,512]{1,0:T(2,128)S(1)} %add_rsqrt_fusion, f32[2,512]{1,0:T(2,128)S(1)} %broadcast_multiply_fusion.8, f32[768]{0:T(1024)S(1)} %convert_element_type.127, ...), kind=kOutput, calls=%fused_computation.86 | convolution fusion | flops 3639604480 | bytes 14569984 | tf_op jit(solution)/shard_map/spf,df->spd/dot_general | solution.py:171
  191.2 9.2 %bitcast_convert_fusion = bf16[768,2304]{1,0:T(8,128)(2,1)} fusion(bf16[2,512,1152]{2,1,0:T(8,128)(2,1)} %copy-done.22, bf16[2,512,1152]{2,1,0:T(8,128)(2,1)} %get-tuple-element.24, f32[2,512,768]{2,1,0:T(8,128)} %copy-done.13, f32[768]{0:T(1024)S(1)} %convert_element_type.127, f32[2,512]{1,0:T(2,128)S(1)} %add_rsqrt_fusion, ...), kind=kOutput, calls=%fused_computation.15 | convolution fusion | flops 3638231040 | bytes 11414528 | tf_op jit(solution)/shard_map/spd,spf->df/dot_general | solution.py:168
  201.9 23.2 %multiply_reduce_fusion = (f32[2,12,512]{2,1,0:T(8,128)}, f32[2,12,512,640]{3,2,1,0:T(8,128)}) fusion(f32[2,12,512,640]{3,2,1,0:T(8,128)} %get-tuple-element.52, f32[2,12,512]{2,1,0:T(8,128)} %log_add_fusion, bf16[2,512,12,64]{1,3,2,0:T(8,128)(2,1)S(1)} %bitcast.114, bf16[2,640,12,64]{1,3,2,0:T(8,128)(2,1)S(1)} %bitcast.122), kind=kOutput, calls=%fused_computation.1 | convolution fusion | flops 1030213632 | bytes 66551808 | tf_op jit(solution)/shard_map/sqhd,skhd->shqk/dot_general | solution.py:187
  225.2 28.0 %multiply_convert_fusion = bf16[2,12,512,640]{3,2,1,0:T(8,128)(2,1)} fusion(f32[2,12,512,640]{3,2,1,0:T(8,128)} %get-tuple-element.58, f32[2,12,512,640]{3,2,1,0:T(8,128)} %get-tuple-element.52, f32[2,12,512]{2,1,0:T(8,128)} %get-tuple-element.57, f32[2,12,512]{2,1,0:T(8,128)} %log_add_fusion), kind=kLoop, calls=%fused_computation | loop fusion | flops 31457280 | bytes 78741504 | tf_op jit(solution)/shard_map/convert_element_type | solution.py:191
  253.1 14.6 %fusion.2 = f32[2,12,64,640]{3,2,1,0:T(8,128)} fusion(bf16[2,512,12,64]{1,3,2,0:T(8,128)(2,1)S(1)} %bitcast.115, f32[2,12,512,640]{3,2,1,0:T(8,128)} %get-tuple-element.52, f32[2,12,512]{2,1,0:T(8,128)S(1)} %copy-done.23), kind=kOutput, calls=%fused_computation.8 | convolution fusion | flops 1022361600 | bytes 37011456 | tf_op jit(solution)/shard_map/shqk,sqhd->skhd/dot_general | solution.py:200
  267.8 5.7 copy.45
  273.5 10.2 %convolution_multiply_fusion = f32[2,12,64,640]{3,2,1,0:T(8,128)} fusion(bf16[2,512,12,64]{1,3,2,0:T(8,128)(2,1)S(1)} %copy-done.5, bf16[2,12,512,640]{3,2,1,0:T(8,128)(2,1)} %multiply_convert_fusion), kind=kOutput, calls=%fused_computation.96 | convolution fusion | flops 1007616000 | bytes 21233664 | tf_op jit(solution)/shard_map/shqk,sqhd->skhd/dot_general | solution.py:197
  283.6 5.6 copy.44
  298.9 13.1 %bitcast_multiply_fusion = (f32[2,512,12,64]{1,3,2,0:T(8,128)}, f32[2,12,64,512]{3,2,1,0:T(8,128)}) fusion(f32[512,64]{0,1:T(8,128)S(1)} %copy-done.30, bf16[2,640,12,64]{1,3,2,0:T(8,128)(2,1)S(1)} %bitcast.117, bf16[2,12,512,640]{3,2,1,0:T(8,128)(2,1)} %multiply_convert_fusion), kind=kOutput, calls=%fused_computation.80 | convolution fusion | flops 1007419392 | bytes 24117248 | tf_op jit(solution)/shard_map/shqk,skhd->sqhd/dot_general | solution.py:193
  335.6 6.4 %bitcast_convert_fusion.1 = bf16[768,2304]{1,0:T(8,128)(2,1)} fusion(bf16[2,512,2304]{1,2,0:T(8,128)(2,1)S(1)} %bitcast.129, bf16[2,512,768]{2,1,0:T(8,128)(2,1)S(1)} %copy-done.7, f32[768]{0:T(1024)S(1)} %copy-done.35, f32[2,512]{1,0:T(2,128)S(1)} %copy-done.37, f32[2,512]{1,0:T(2,128)S(1)} %copy-done.33), kind=kOutput, calls=%fused_computation.16 | convolution fusion | flops 3629580288 | bytes 9841664 | tf_op jit(solution)/shard_map/spd,spe->de/dot_general | solution.py:229
  343.5 6.1 %add_convert_fusion.1 = bf16[2,512,768]{2,1,0:T(8,128)(2,1)} fusion(f32[2,512,768]{2,1,0:T(8,128)} %copy-done.13, bf16[2,512,1152]{2,1,0:T(8,128)(2,1)} %get-tuple-element.27, bf16[1152,768]{1,0:T(8,128)(2,1)S(1)} %copy-done.41), kind=kOutput, calls=%fused_computation.89 | convolution fusion | flops 1813512192 | bytes 8847360 | tf_op jit(solution)/shard_map/dot_general | solution.py:158
  349.6 6.2 %fusion.37 = (bf16[768]{0:T(1024)(128)(2,1)S(1)}, f32[2,512]{1,0:T(2,128)S(1)}, f32[2,512]{1,0:T(2,128)S(1)}, f32[2,512,768]{2,1,0:T(8,128)}) fusion(bf16[2,512,768]{2,1,0:T(8,128)(2,1)S(1)} %copy-done.7, f32[2,512]{1,0:T(2,128)S(1)} %copy-done.37, f32[2,512]{1,0:T(2,128)S(1)} %copy-done.33, f32[768]{0:T(1024)S(1)} %copy-done.35, ...), kind=kOutput, calls=%fused_computation.67 | convolution fusion | flops 3630953728 | bytes 12997120 | tf_op jit(solution)/shard_map/spe,de->spd/dot_general | solution.py:230
  355.8 5.8 all-reduce.7
  366.8 17.9 %reduce-scatter.5.cloned.1.call-done = bf16[192,2304]{1,0:T(8,128)(2,1)} async-done(((bf16[768,2304]{1,0:T(8,128)(2,1)}), bf16[192,2304]{1,0:T(8,128)(2,1)}) %reduce-scatter.5.cloned.1.call-update) | async-done | bytes 884752 | tf_op jit(solution)/shard_map/reduce_scatter | solution.py:239
  384.7 199.7 %all-reduce.10 = (f32[192]{0:T(256)}, f32[192,2304]{1,0:T(8,128)}, f32[192,768]{1,0:T(8,128)}, f32[192]{0:T(256)}, f32[192,2304]{1,0:T(8,128)}, /*index=5*/f32[288,768]{1,0:T(8,128)}) all-reduce(f32[192]{0:T(256)S(1)} %dynamic-slice_convert_fusion.1, ...), channel_id=1, replica_groups=mesh['seq'=8,'fsdp'=4] {'seq'}, use_global_device_ids=true, to_apply=%region_13.14 | all-reduce | flops 1253760 | bytes 7523328 | tf_op jit(solution)/shard_map/psum | solution.py:255
  (183 shorter events, 109.7 us)
Async XLA Ops:
  7.2 15.0 %copy-start.6 = (bf16[2,512,768]{2,1,0:T(8,128)(2,1)S(1)}, bf16[2,512,768]{2,1,0:T(8,128)(2,1)}, u32[]{:S(2)}) copy-start(bf16[2,512,768]{2,1,0:T(8,128)(2,1)} %param.8) | copy-start | bytes 4718596
  7.2 35.9 %all-gather.5.cloned.1.call-start = ((), (), s32[]{:S(2)}) async-start(), calls=%async_computation.4 | async-start | bytes 4423680 | tf_op jit(solution)/shard_map/all_gather | solution.py:105
  7.9 124.0 %all-gather.7.cloned.1.call-start = ((), (), s32[]{:S(2)}) async-start(), calls=%async_computation.5 | async-start | bytes 1474560 | tf_op jit(solution)/shard_map/all_gather | solution.py:106
  8.7 128.9 %all-gather.9.cloned.1.call-start = ((), (), s32[]{:S(2)}) async-start(), calls=%async_computation.6 | async-start | bytes 4423680 | tf_op jit(solution)/shard_map/all_gather | solution.py:108
  9.4 138.7 %all-gather.11.cloned.1.call-start = ((), (), s32[]{:S(2)}) async-start(), calls=%async_computation.7 | async-start | bytes 2211840 | tf_op jit(solution)/shard_map/all_gather | solution.py:109
  10.0 356.8 %reduce-scatter.7.cloned.1.call-start = ((), (), s32[]{:S(2)}) async-start(), calls=%async_computation.9 | async-start | bytes 1474560 | tf_op jit(solution)/shard_map/reduce_scatter | solution.py:242
  22.1 27.0 %copy-start.34 = (f32[768]{0:T(1024)}, f32[768]{0:T(1024)S(1)}, u32[]{:S(2)}) copy-start(f32[768]{0:T(1024)S(1)} %convert_element_type.117) | copy-start | bytes 9220
  22.4 26.7 %copy-start.32 = (f32[2,512]{1,0:T(2,128)}, f32[2,512]{1,0:T(2,128)S(1)}, u32[]{:S(2)}) copy-start(f32[2,512]{1,0:T(2,128)S(1)} %broadcast_multiply_fusion.9) | copy-start | bytes 12292
  23.0 26.1 %copy-start.36 = (f32[2,512]{1,0:T(2,128)}, f32[2,512]{1,0:T(2,128)S(1)}, u32[]{:S(2)}) copy-start(f32[2,512]{1,0:T(2,128)S(1)} %add_rsqrt_fusion.1) | copy-start | bytes 12292
  24.1 33.1 %copy-start.26 = (f32[512,64]{0,1:T(8,128)}, f32[512,64]{0,1:T(8,128)S(1)}, u32[]{:S(2)}) copy-start(f32[512,64]{0,1:T(8,128)S(1)} %get-tuple-element.47) | copy-start | bytes 393220
  24.1 33.3 %copy-start.24 = (f32[512,64]{0,1:T(8,128)}, f32[512,64]{0,1:T(8,128)S(1)}, u32[]{:S(2)}) copy-start(f32[512,64]{0,1:T(8,128)S(1)} %get-tuple-element.48) | copy-start | bytes 393220
  62.0 13.5 %collective-permute-start.1 = (bf16[2,64,1536]{2,1,0:T(8,128)(2,1)}, bf16[2,64,1536]{2,1,0:T(8,128)(2,1)}, u32[]{:S(2)}, u32[]{:S(2)}) collective-permute-start(bf16[2,64,1536]{2,1,0:T(8,128)(2,1)} %copy.38), channel_id=1, source_target_pairs={{4,0},{8,4},{12,8},{16,12},{20,16},{24,20},{28,24},{5,1},{9,5},{13... | collective-permute-start | bytes 1179656 | tf_op jit(solution)/shard_map/ppermute | solution.py:27
  63.3 20.5 %collective-permute-start = (bf16[2,64,1536]{2,1,0:T(8,128)(2,1)}, bf16[2,64,1536]{2,1,0:T(8,128)(2,1)}, u32[]{:S(2)}, u32[]{:S(2)}) collective-permute-start(bf16[2,64,1536]{2,1,0:T(8,128)(2,1)} %copy.37), channel_id=1, source_target_pairs={{0,4},{4,8},{8,12},{12,16},{16,20},{20,24},{24,28},{1,5},{5,9},{9,... | collective-permute-start | bytes 1179656 | tf_op jit(solution)/shard_map/ppermute | solution.py:24
  73.8 17.2 %copy-start.4 = (bf16[2,512,12,64]{1,3,2,0:T(8,128)(2,1)}, bf16[2,512,12,64]{1,3,2,0:T(8,128)(2,1)S(1)}, u32[]{:S(2)}) copy-start(bf16[2,512,12,64]{1,3,2,0:T(8,128)(2,1)S(1)} %fusion.40) | copy-start | bytes 4718596
  90.9 13.9 %copy-start.2 = (bf16[2,640,768]{1,2,0:T(8,128)(2,1)}, bf16[2,640,768]{1,2,0:T(8,128)(2,1)S(1)}, u32[]{:S(2)}) copy-start(bf16[2,640,768]{1,2,0:T(8,128)(2,1)S(1)} %get-tuple-element.33) | copy-start | bytes 5898244
  90.9 27.7 %copy-start.10 = (bf16[2,640,768]{1,2,0:T(8,128)(2,1)}, bf16[2,640,768]{1,2,0:T(8,128)(2,1)S(1)}, u32[]{:S(2)}) copy-start(bf16[2,640,768]{1,2,0:T(8,128)(2,1)S(1)} %get-tuple-element.34) | copy-start | bytes 5898244
  137.5 10.6 %copy-start.28 = (bf16[2,512,768]{2,1,0:T(8,128)(2,1)S(1)}, bf16[2,512,768]{2,1,0:T(8,128)(2,1)}, u32[]{:S(2)}) copy-start(bf16[2,512,768]{2,1,0:T(8,128)(2,1)} %param.15) | copy-start | bytes 4718596
  148.1 16.1 %copy-start.17 = (f32[2,512,2304]{2,1,0:T(8,128)S(1)}, f32[2,512,2304]{2,1,0:T(8,128)}, u32[]{:S(2)}) copy-start(f32[2,512,2304]{2,1,0:T(8,128)} %fusion.25) | copy-start | bytes 28311556
  179.4 187.3 %reduce-scatter.11.cloned.1.call-start = ((), (), s32[]{:S(2)}) async-start(), calls=%async_computation.11 | async-start | bytes 2211840 | tf_op jit(solution)/shard_map/reduce_scatter | solution.py:251
  184.9 181.9 %reduce-scatter.9.cloned.1.call-start = ((), (), s32[]{:S(2)}) async-start(), calls=%async_computation.10 | async-start | bytes 4423680 | tf_op jit(solution)/shard_map/reduce_scatter | solution.py:248
  200.4 184.3 %reduce-scatter.5.cloned.1.call-start = ((), (), s32[]{:S(2)}) async-start(), calls=%async_computation.8 | async-start | bytes 4423680 | tf_op jit(solution)/shard_map/reduce_scatter | solution.py:239
  225.2 28.0 %copy-start.23 = (f32[2,12,512]{2,1,0:T(8,128)S(1)}, f32[2,12,512]{2,1,0:T(8,128)}, u32[]{:S(2)}) copy-start(f32[2,12,512]{2,1,0:T(8,128)} %log_add_fusion) | copy-start | bytes 147460
  293.1 23.8 %collective-permute-start.2 = (bf16[2,64,1536]{2,1,0:T(8,128)(2,1)S(1)}, bf16[2,64,1536]{2,1,0:T(8,128)(2,1)S(1)}, u32[]{:S(2)}, u32[]{:S(2)}) collective-permute-start(bf16[2,64,1536]{2,1,0:T(8,128)(2,1)S(1)} %get-tuple-element.31), channel_id=1, source_target_pairs={{0,4},{4,8},{8,12},{12,16},{16,20},{20,24},{24,28},{1,5},{5,9},{9,... | collective-permute-start | bytes 1179656 | tf_op jit(solution)/shard_map/ppermute | solution.py:35
  297.6 19.4 %collective-permute-start.3 = (bf16[2,64,1536]{2,1,0:T(8,128)(2,1)S(1)}, bf16[2,64,1536]{2,1,0:T(8,128)(2,1)}, u32[]{:S(2)}, u32[]{:S(2)}) collective-permute-start(bf16[2,64,1536]{2,1,0:T(8,128)(2,1)S(1)} %get-tuple-element.32), channel_id=1, source_target_pairs={{4,0},{8,4},{12,8},{16,12},{20,16},{24,20},{28,24},{5,1},{9,5},{13... | collective-permute-start | bytes 1179656 | tf_op jit(solution)/shard_map/ppermute | solution.py:35
  (32 other events, 131.1 us)
Sparse Core Ops, SparseCore 0:
  9.6 33.4 all-gather.4
  44.6 17.4 all-gather.6
  63.7 30.7 all-gather.8
  95.9 20.7 all-gather.10
  179.6 27.0 reduce-scatter.6
  209.9 29.3 reduce-scatter.10
  241.9 40.3 reduce-scatter.8
  342.2 42.5 reduce-scatter.4
where the time goes:
time: 601 us; the launch traced here: 592 us
  blocking collectives  214 us (36%)
  matrix products  171 us (28%)
  other arithmetic  81 us (13%)
  local copies, waits for them, and re-layouts  49.3 us (8%)
  waiting for transfers between devices  47.5 us (8%)
  between operations  16.7 us (3%)
  starting transfers between devices  12.8 us (2%)
    psum x1, blocking collectives, shards(): lax.psum((shares[0], shares[1], shares[2], shares[3], shares[4], shares[5...  200 us
    convert_element_type x1, other arithmetic, shards(): score_grad = (probs * centered).astype(jnp.bfloat16)  28 us
    dot_general x1, matrix products, shards(): jnp.einsum('sqhd,skhd->shqk', attended_grad, value_back, preferred_elemen...  23.2 us
    all_gather x1, waiting for transfers between devices, shards(): lax.all_gather(qkv_weight, 'fsdp', axis=0, tiled=True)  18.9 us
    unnamed x93, local copies, waits for them, and re-layouts  18.6 us
    reduce_scatter x1, waiting for transfers between devices, shards(): lax.psum_scatter(qkv_grad.astype(jnp.bfloat16), 'fsdp', scatter_dimension...  17.9 us
    dot_general x1, matrix products, shards(): jnp.einsum('spd,fd->spf', grad_out, weight_out, preferred_element_type=jn...  16.1 us
    dot_general x1, matrix products, shards(): jnp.einsum('shqk,sqhd->skhd', probs.astype(jnp.bfloat16), attended_grad,...  14.6 us
  transfers between devices with their start and end apart: 12, of which 4 were waited for; matrix products, arithmetic and copies ran while one was open for 43% of the time, Pallas kernels for 0%

commit v1 on v0

v1 whole, which is shorter than its diff:
```python
import math

import jax
import jax.numpy as jnp
from jax import lax
from jax.experimental import pallas as pl
from jax.experimental.pallas import tpu as pltpu
from jax.sharding import PartitionSpec as P

HEADS = 12
HEAD_DIM = 64
FF = 1152
WIN = 64
PAIR = 128
BLOCK = 128

epsilon = 1e-05
rope_base = 10000.0
negative = -1e30
f32 = jnp.float32
bf16 = jnp.bfloat16
LIMIT = 56 * 1024 * 1024

NN = (((1,), (0,)), ((), ()))
NT = (((1,), (1,)), ((), ()))
TN = (((0,), (0,)), ((), ()))


def mm(a, b, dims=NN):
    return lax.dot_general(a, b, dims, preferred_element_type=f32)


def unit_rows(x):
    center = x - jnp.mean(x, axis=-1, keepdims=True)
    inverse = lax.rsqrt(jnp.mean(center * center, axis=-1, keepdims=True) + epsilon)
    return center * inverse, inverse


def turn(x, cos, low, high):
    return x * cos + pltpu.roll(x, PAIR - 32, 1) * low + pltpu.roll(x, 32, 1) * high


def qkv_kernel(tok_ref, gain_ref, w_ref, cos_ref, low_ref, high_ref, q_ref, kv_ref):
    unit, _ = unit_rows(tok_ref[...].astype(f32))
    normed = (unit * gain_ref[...]).astype(bf16)
    cos, low, high = cos_ref[...], low_ref[...], high_ref[...]
    width = q_ref.shape[1]
    step = 2 * PAIR
    for j in range(3 * width // step):
        part = mm(normed, w_ref[:, j * step : (j + 1) * step])
        for h in range(2):
            at = j * step + h * PAIR
            piece = part[:, h * PAIR : (h + 1) * PAIR]
            if at < width:
                q_ref[:, at : at + PAIR] = (
                    turn(piece, cos, low, high) * (1.0 / math.sqrt(HEAD_DIM))
                ).astype(bf16)
            elif at < 2 * width:
                kv_ref[:, at - width : at - width + PAIR] = turn(piece, cos, low, high).astype(bf16)
            else:
                kv_ref[:, at - width : at - width + PAIR] = piece.astype(bf16)


def head_masks():
    lane = lax.broadcasted_iota(jnp.int32, (1, PAIR), 1)
    first = (lane < HEAD_DIM).astype(f32)
    return first.astype(bf16), (1.0 - first).astype(bf16), lane < HEAD_DIM


def fill(dst, left, mid, right):
    n = mid.shape[1]
    dst[0:WIN] = left[0]
    dst[WIN : WIN + n] = mid[0]
    dst[WIN + n : 2 * WIN + n] = right[0]


def attend_kernel(q_ref, k_ref, v_ref, lk_ref, lv_ref, rk_ref, rv_ref, bias_ref, att_ref, p_ref, ke, ve):
    fill(ke, lk_ref, k_ref, rk_ref)
    fill(ve, lv_ref, v_ref, rv_ref)
    first, second, is_first = head_masks()
    for i in range(q_ref.shape[1] // BLOCK):
        rows = slice(i * BLOCK, (i + 1) * BLOCK)
        span = slice(i * BLOCK, (i + 1) * BLOCK + 2 * WIN)
        query, key, value = q_ref[0, rows], ke[span], ve[span]
        outs = []
        for h, mask in enumerate((first, second)):
            scores = mm(query * mask, key, NT) + bias_ref[i]
            raised = jnp.exp(scores - jnp.max(scores, axis=-1, keepdims=True))
            total = jnp.sum(raised, axis=-1, keepdims=True)
            probs = (raised * (1.0 / total)).astype(bf16)
            p_ref[0, h, rows] = probs
            outs.append(mm(probs, value))
        att_ref[0, rows] = jnp.where(is_first, outs[0], outs[1]).astype(bf16)


def attend_back_kernel(
    q_ref, k_ref, v_ref, lk_ref, lv_ref, rk_ref, rv_ref, p_ref, ag_ref, cos_ref, low_ref, high_ref,
    dq_ref, dk_ref, dv_ref, dl_ref, dr_ref, ke, ve, ka, va,
):
    fill(ke, lk_ref, k_ref, rk_ref)
    fill(ve, lv_ref, v_ref, rv_ref)
    ka[...] = jnp.zeros_like(ka)
    va[...] = jnp.zeros_like(va)
    first, second, is_first = head_masks()
    count = q_ref.shape[1]
    scale = 1.0 / math.sqrt(HEAD_DIM)
    for i in range(count // BLOCK):
        rows = slice(i * BLOCK, (i + 1) * BLOCK)
        span = slice(i * BLOCK, (i + 1) * BLOCK + 2 * WIN)
        query, key, value, upstream = q_ref[0, rows], ke[span], ve[span], ag_ref[0, rows]
        dqs, dks, dvs = [], [], []
        for h, mask in enumerate((first, second)):
            low_probs = p_ref[0, h, rows]
            probs = low_probs.astype(f32)
            back = mm(upstream * mask, value, NT)
            weighted = probs * back
            delta = jnp.sum(weighted, axis=-1, keepdims=True)
            grad = (weighted - probs * delta).astype(bf16)
            dqs.append(mm(grad, key))
            dks.append(mm(grad, query, TN))
            dvs.append(mm(low_probs, upstream, TN))
        dq = jnp.where(is_first, dqs[0], dqs[1]) * scale
        at = slice(WIN + i * BLOCK, WIN + (i + 1) * BLOCK)
        dq_ref[0, rows] = turn(dq, cos_ref[at], -low_ref[at], -high_ref[at]).astype(bf16)
        ka[span] += jnp.where(is_first, dks[0], dks[1])
        va[span] += jnp.where(is_first, dvs[0], dvs[1])
    dk = turn(ka[...], cos_ref[...], -low_ref[...], -high_ref[...])
    dl_ref[0, 0] = dk[:WIN].astype(bf16)
    dk_ref[0] = dk[WIN : WIN + count].astype(bf16)
    dr_ref[0, 0] = dk[WIN + count :].astype(bf16)
    dl_ref[0, 1] = va[:WIN].astype(bf16)
    dv_ref[0] = va[WIN : WIN + count].astype(bf16)
    dr_ref[0, 1] = va[WIN + count :].astype(bf16)


def mlp_kernel(
    tok_ref, att_ref, go_ref, gain_ref, wo_ref, win_ref, wout_ref,
    out_ref, mg_ref, ag_ref, dwo_ref, dwin_ref, dwout_ref, dgain_ref,
    awo, awin, awout, wg_buf, hid_buf,
):
    step = pl.program_id(0)

    @pl.when(step == 0)
    def _():
        awo[...] = jnp.zeros_like(awo)
        awin[...] = jnp.zeros_like(awin)
        awout[...] = jnp.zeros_like(awout)
        dgain_ref[...] = jnp.zeros_like(dgain_ref)

    attended, go = att_ref[...], go_ref[...]
    middle = tok_ref[...].astype(f32) + mm(attended, wo_ref[...])
    gain = gain_ref[...]
    unit, inverse = unit_rows(middle)
    normed = (unit * gain).astype(bf16)
    chunk = 384
    for c in range(FF // chunk):
        cols = slice(c * chunk, (c + 1) * chunk)
        gate = slice(FF + c * chunk, FF + (c + 1) * chunk)
        a = mm(normed, win_ref[:, cols])
        b = mm(normed, win_ref[:, gate])
        hg = mm(go, wout_ref[cols, :], NT)
        cdf = 0.5 * (1.0 + lax.erf(a * (1.0 / math.sqrt(2.0))))
        gelu = a * cdf
        slope = cdf + a * (jnp.exp(-0.5 * a * a) * (1.0 / math.sqrt(2.0 * math.pi)))
        hid_buf[:, cols] = (gelu * b).astype(bf16)
        wg_buf[:, cols] = (hg * b * slope).astype(bf16)
        wg_buf[:, gate] = (hg * gelu).astype(bf16)
    hidden, wg = hid_buf[...], wg_buf[...]
    out_ref[...] = (middle + mm(hidden, wout_ref[...])).astype(bf16)
    back = mm(wg, win_ref[...], NT)
    dgain_ref[...] += jnp.sum(back * unit, axis=0, keepdims=True)
    e = back * gain
    part = e - jnp.mean(e, axis=-1, keepdims=True) - unit * jnp.mean(e * unit, axis=-1, keepdims=True)
    mg = go.astype(f32) + inverse * part
    mg_ref[...] = mg
    low = mg.astype(bf16)
    ag_ref[...] = mm(low, wo_ref[...], NT).astype(bf16)
    awout[...] += mm(hidden, go, TN)
    awin[...] += mm(normed, wg, TN)
    awo[...] += mm(attended, low, TN)

    @pl.when(step == pl.num_programs(0) - 1)
    def _():
        dwo_ref[...] = awo[...].astype(bf16)
        dwin_ref[...] = awin[...].astype(bf16)
        dwout_ref[...] = awout[...].astype(bf16)


def qkv_back_kernel(
    tok_ref, mg_ref, dq_ref, dk_ref, dv_ref, fl_ref, fr_ref, gain_ref, w_ref,
    tg_ref, dw_ref, dgain_ref, acc, buf,
):
    step = pl.program_id(0)

    @pl.when(step == 0)
    def _():
        acc[...] = jnp.zeros_like(acc)
        dgain_ref[...] = jnp.zeros_like(dgain_ref)

    width = tok_ref.shape[2]
    count = tok_ref.shape[1]
    buf[:, :width] = dq_ref[0]
    for j, ref in enumerate((dk_ref, dv_ref)):
        cols = slice((j + 1) * width, (j + 2) * width)
        buf[:, cols] = ref[0]
        buf[:WIN, cols] = (ref[0, :WIN].astype(f32) + fl_ref[0, j].astype(f32)).astype(bf16)
        buf[count - WIN :, cols] = (
            ref[0, count - WIN :].astype(f32) + fr_ref[0, j].astype(f32)
        ).astype(bf16)
    gain = gain_ref[...]
    unit, inverse = unit_rows(tok_ref[0].astype(f32))
    normed = (unit * gain).astype(bf16)
    grads = buf[...]
    back = mm(grads, w_ref[...], NT)
    dgain_ref[...] += jnp.sum(back * unit, axis=0, keepdims=True)
    e = back * gain
    part = e - jnp.mean(e, axis=-1, keepdims=True) - unit * jnp.mean(e * unit, axis=-1, keepdims=True)
    tg_ref[0] = mg_ref[0] + inverse * part
    acc[...] += mm(normed, grads, TN)

    @pl.when(step == pl.num_programs(0) - 1)
    def _():
        dw_ref[...] = acc[...].astype(bf16)


def sds(shape, dtype):
    return jax.ShapeDtypeStruct(shape, dtype)


def whole(shape):
    return pl.BlockSpec(shape, lambda *_: (0,) * len(shape), pipeline_mode=pl.Buffered(1))


def tables(start, count):
    half = HEAD_DIM // 2
    freqs = rope_base ** (-(jnp.arange(half, dtype=f32) * 2.0 / HEAD_DIM))
    positions = (start + jnp.arange(count, dtype=jnp.int32)).astype(f32)
    angles = positions[:, None] * freqs[None, :]
    cos, sin = jnp.cos(angles), jnp.sin(angles)
    none = jnp.zeros_like(sin)
    return (
        jnp.concatenate([cos] * 4, axis=-1),
        jnp.concatenate([-sin, none] * 2, axis=-1),
        jnp.concatenate([none, sin] * 2, axis=-1),
    )


def shards(tokens, norm_gain_attn, qkv_weight, attn_out_weight, norm_gain_mlp, mlp_in_weight, mlp_out_weight, grad_out):
    seqs, piece, width = tokens.shape
    rows = seqs * piece
    span = piece + 2 * WIN
    pairs = width // PAIR
    seq_size = lax.axis_size("seq")
    forward = [(i, i + 1) for i in range(seq_size - 1)]
    backward = [(j, i) for i, j in forward]
    gather = lambda x: lax.all_gather(x, "fsdp", axis=0, tiled=True)
    w_qkv = gather(qkv_weight)
    gains = lax.all_gather(jnp.stack([norm_gain_attn, norm_gain_mlp]), "fsdp", axis=1, tiled=True)
    w_attn = gather(attn_out_weight)
    w_in = gather(mlp_in_weight)
    w_out = gather(mlp_out_weight)
    gain_attn = gains[0:1].astype(f32)
    gain_mlp = gains[1:2].astype(f32)
    start = lax.axis_index("seq") * piece
    cos, low, high = tables(start - WIN, span)
    q_at = start + jnp.arange(piece, dtype=jnp.int32).reshape(-1, BLOCK)[:, :, None]
    k_at = (
        start - WIN
        + jnp.arange(piece // BLOCK, dtype=jnp.int32)[:, None, None] * BLOCK
        + jnp.arange(BLOCK + 2 * WIN, dtype=jnp.int32)[None, None, :]
    )
    inside = (jnp.abs(q_at - k_at) <= WIN) & (k_at >= 0) & (k_at < piece * seq_size)
    bias = jnp.where(inside, 0.0, negative).astype(f32)

    tile = 256
    per = piece // tile
    flat = lambda x: x.reshape(rows, x.shape[-1])
    row_spec = lambda w: pl.BlockSpec((tile, w), lambda i: (i, 0))
    table_spec = pl.BlockSpec((tile, PAIR), lambda i: (lax.rem(i, per), 0))
    params = lambda n: pltpu.CompilerParams(dimension_semantics=("arbitrary",) * n, vmem_limit_bytes=LIMIT)
    tok = flat(tokens)
    mid = slice(WIN, WIN + piece)
    q, kv = pl.pallas_call(
        qkv_kernel,
        grid=(rows // tile,),
        in_specs=[row_spec(width), whole((1, width)), whole(w_qkv.shape), table_spec, table_spec, table_spec],
        out_specs=[row_spec(width), row_spec(2 * width)],
        out_shape=[sds((rows, width), bf16), sds((rows, 2 * width), bf16)],
        compiler_params=params(1),
        cost_estimate=pl.CostEstimate(flops=6 * rows * width * width, bytes_accessed=12 * rows * width, transcendentals=0),
        name="qkv_forward",
    )(tok, gain_attn, w_qkv, cos[mid], low[mid], high[mid])
    q = q.reshape(seqs, piece, width)
    kv = kv.reshape(seqs, piece, 2 * width)
    left = lax.ppermute(kv[:, piece - WIN :], "seq", forward)
    right = lax.ppermute(kv[:, :WIN], "seq", backward)

    def lanes(n, off=0):
        return pl.BlockSpec((1, n, PAIR), lambda s, p: (s, 0, p + off))

    kv_specs = [
        lanes(piece), lanes(piece, pairs), lanes(WIN), lanes(WIN, pairs), lanes(WIN), lanes(WIN, pairs),
    ]
    kv_args = (kv, kv, left, left, right, right)
    p_spec = pl.BlockSpec((1, 2, piece, BLOCK + 2 * WIN), lambda s, p: (s, p, 0, 0))
    p_shape = (seqs, HEADS, piece, BLOCK + 2 * WIN)
    ext = pltpu.VMEM((span, PAIR), bf16)
    unit_flops = 2 * seqs * HEADS * piece * (BLOCK + 2 * WIN) * HEAD_DIM
    p_bytes = 2 * math.prod(p_shape)
    attended, probs = pl.pallas_call(
        attend_kernel,
        grid=(seqs, pairs),
        in_specs=[lanes(piece)] + kv_specs + [whole(bias.shape)],
        out_specs=[lanes(piece), p_spec],
        out_shape=[sds((seqs, piece, width), bf16), sds(p_shape, bf16)],
        scratch_shapes=[ext, ext],
        compiler_params=params(2),
        cost_estimate=pl.CostEstimate(flops=8 * unit_flops, bytes_accessed=p_bytes + 8 * rows * width, transcendentals=p_bytes // 2),
        name="attend_forward",
    )(q, *kv_args, bias)

    out, mg, ag, d_wo, d_win, d_wout, d_gain_mlp = pl.pallas_call(
        mlp_kernel,
        grid=(rows // tile,),
        in_specs=[row_spec(width)] * 3 + [whole((1, width)), whole(w_attn.shape), whole(w_in.shape), whole(w_out.shape)],
        out_specs=[row_spec(width)] * 3
        + [whole(w_attn.shape), whole(w_in.shape), whole(w_out.shape), whole((1, width))],
        out_shape=[
            sds((rows, width), bf16), sds((rows, width), f32), sds((rows, width), bf16),
            sds(w_attn.shape, bf16), sds(w_in.shape, bf16), sds(w_out.shape, bf16), sds((1, width), f32),
        ],
        scratch_shapes=[
            pltpu.VMEM(w_attn.shape, f32), pltpu.VMEM(w_in.shape, f32), pltpu.VMEM(w_out.shape, f32),
            pltpu.VMEM((tile, 2 * FF), bf16), pltpu.VMEM((tile, FF), bf16),
        ],
        compiler_params=params(1),
        cost_estimate=pl.CostEstimate(flops=6 * rows * width * (width + 3 * FF), bytes_accessed=40 * 2**20, transcendentals=0),
        name="mlp_both_ways",
    )(tok, flat(attended), flat(grad_out), gain_mlp, w_attn, w_in, w_out)

    def reduce(x, dim=0):
        mine = lax.psum_scatter(x, "fsdp", scatter_dimension=dim, tiled=True)
        return mine

    s_win, s_wout, s_wo = reduce(d_win), reduce(d_wout), reduce(d_wo)
    s_win, s_wout, s_wo = lax.psum((s_win, s_wout, s_wo), "seq")

    table_full = pl.BlockSpec((span, PAIR), lambda s, p: (0, 0))
    edge = pl.BlockSpec((1, 2, WIN, PAIR), lambda s, p: (s, 0, 0, p))
    edge_shape = sds((seqs, 2, WIN, width), bf16)
    own = sds((seqs, piece, width), bf16)
    total = pltpu.VMEM((span, PAIR), f32)
    dq, dk, dv, dl, dr = pl.pallas_call(
        attend_back_kernel,
        grid=(seqs, pairs),
        in_specs=[lanes(piece)] + kv_specs + [p_spec, lanes(piece), table_full, table_full, table_full],
        out_specs=[lanes(piece)] * 3 + [edge, edge],
        out_shape=[own] * 3 + [edge_shape] * 2,
        scratch_shapes=[ext, ext, total, total],
        compiler_params=params(2),
        cost_estimate=pl.CostEstimate(flops=16 * unit_flops, bytes_accessed=p_bytes + 16 * rows * width, transcendentals=0),
        name="attend_backward",
    )(q, *kv_args, probs, ag.reshape(seqs, piece, width), cos, low, high)
    from_left = lax.ppermute(dr, "seq", forward)
    from_right = lax.ppermute(dl, "seq", backward)

    seq_spec = pl.BlockSpec((1, piece, width), lambda s: (s, 0, 0))
    edge_in = pl.BlockSpec((1, 2, WIN, width), lambda s: (s, 0, 0, 0))
    tokens_grad, d_wqkv, d_gain_attn = pl.pallas_call(
        qkv_back_kernel,
        grid=(seqs,),
        in_specs=[seq_spec] * 5 + [edge_in] * 2 + [whole((1, width)), whole(w_qkv.shape)],
        out_specs=[seq_spec, whole(w_qkv.shape), whole((1, width))],
        out_shape=[sds((seqs, piece, width), f32), sds(w_qkv.shape, bf16), sds((1, width), f32)],
        scratch_shapes=[pltpu.VMEM(w_qkv.shape, f32), pltpu.VMEM((piece, 3 * width), bf16)],
        compiler_params=params(1),
        cost_estimate=pl.CostEstimate(flops=12 * rows * width * width, bytes_accessed=20 * rows * width, transcendentals=0),
        name="qkv_backward",
    )(tokens, mg.reshape(seqs, piece, width), dq, dk, dv, from_left, from_right, gain_attn, w_qkv)

    s_gains = lax.psum_scatter(
        jnp.concatenate([d_gain_attn, d_gain_mlp]).astype(bf16), "fsdp", scatter_dimension=1, tiled=True
    ).astype(f32)
    s_wqkv = reduce(d_wqkv)
    s_gains, s_wqkv = lax.psum((s_gains, s_wqkv), "seq")
    return (
        out.reshape(seqs, piece, width),
        tokens_grad,
        s_gains[0],
        s_wqkv.astype(f32),
        s_wo.astype(f32),
        s_gains[1],
        s_win.astype(f32),
        s_wout.astype(f32),
    )


def solution(mesh):
    return jax.shard_map(
        shards,
        mesh=mesh,
        in_specs=(
            P("fsdp", "seq", None),
            P("fsdp"),
            P("fsdp", None),
            P("fsdp", None),
            P("fsdp"),
            P("fsdp", None),
            P("fsdp", None),
            P("fsdp", "seq", None),
        ),
        out_specs=(
            P("fsdp", "seq", None),
            P("fsdp", "seq", None),
            P("fsdp"),
            P("fsdp", None),
            P("fsdp", None),
            P("fsdp"),
            P("fsdp", None),
            P("fsdp", None),
        ),
        check_vma=False,
    )
```

time: 601 us -> 451 us (0.75); the launches traced: 592 us -> 451 us
  waiting for transfers between devices: 47.5 us -> 265 us
  blocking collectives: 214 us -> 27.8 us
  matrix products: 171 us -> 0 us
  Pallas kernels: 0 us -> 113 us
  other arithmetic: 81 us -> 10.7 us
  local copies, waits for them, and re-layouts: 49.3 us -> 8.12 us
    psum x1, blocking collectives: 200 us -> 21.8 us  [shards(): s_gains, s_wqkv = lax.psum((s_gains, s_wqkv), 'seq')]
    dot_general x18 -> x0, matrix products: 171 us -> none  [the longest x1 23.2 us: shards(): jnp.einsum('sqhd,skhd->shqk', attended_grad, value_back, preferred_elemen...]
    pallas_call x0 -> x5, Pallas kernels: none -> 113 us  [the longest x1 37.1 us: shards(): pl.pallas_call(attend_back_kernel, grid=(seqs, pairs), in_specs=[lanes(pi...]
    psum x0 -> x1, waiting for transfers between devices: none -> 94.4 us  [shards(): s_gains, s_wqkv = lax.psum((s_gains, s_wqkv), 'seq')]
    reduce_scatter x4, waiting for transfers between devices: 18 us -> 67.1 us  [reduce(): mine = lax.psum_scatter(x, 'fsdp', scatter_dimension=dim, tiled=True)]
    all_gather x4, waiting for transfers between devices: 19 us -> 46.8 us  [shards(): gather = lambda x: lax.all_gather(x, 'fsdp', axis=0, tiled=True)]
    convert_element_type x8 -> x6, other arithmetic: 33.8 us -> 7.33 us  [the longest x1 2.57 us: shards(): s_wqkv.astype(f32)]
    unnamed x8 -> x11, waiting for transfers between devices: 2.65 us -> 26.6 us
  transfers between devices with their start and end apart: 12 -> 14, of which waited for: 4 -> 9; matrix products, arithmetic and copies ran while one was open for 43% -> 2% of each run, Pallas kernels for 0% -> 17%
where the time goes in v1:
time: 451 us
  waiting for transfers between devices  265 us (59%)
  Pallas kernels  113 us (25%)
  blocking collectives  27.8 us (6%)
  between operations  14.4 us (3%)
  starting transfers between devices  11.3 us (3%)
  other arithmetic  10.7 us (2%)
  local copies, waits for them, and re-layouts  8.12 us (2%)
    psum x1, waiting for transfers between devices, shards(): s_gains, s_wqkv = lax.psum((s_gains, s_wqkv), 'seq')  94.4 us
    reduce_scatter x4, waiting for transfers between devices, reduce(): mine = lax.psum_scatter(x, 'fsdp', scatter_dimension=dim, tiled=True)  67.1 us
    all_gather x4, waiting for transfers between devices, shards(): gather = lambda x: lax.all_gather(x, 'fsdp', axis=0, tiled=True)  46.8 us
    pallas_call x1, Pallas kernels, shards(): pl.pallas_call(attend_back_kernel, grid=(seqs, pairs), in_specs=[lanes(pi...  37.1 us
    pallas_call x1, Pallas kernels, shards(): pl.pallas_call(mlp_kernel, grid=(rows // tile,), in_specs=[row_spec(width...  35.3 us
    unnamed x11, waiting for transfers between devices  26.6 us
    psum x1, blocking collectives, shards(): s_gains, s_wqkv = lax.psum((s_gains, s_wqkv), 'seq')  21.8 us
    pallas_call x1, Pallas kernels, shards(): pl.pallas_call(attend_kernel, grid=(seqs, pairs), in_specs=[lanes(piece)]...  16.2 us
  transfers between devices with their start and end apart: 14, of which 9 were waited for; matrix products, arithmetic and copies ran while one was open for 2% of the time, Pallas kernels for 17%

profile of v1, /device:TPU:0, one launch (start us, length us, event | category | flops | bytes accessed | tf_op | source)
XLA Modules:
  0.0 450.8 jit_solution(7861188302191227239)
XLA Ops:
  10.1 6.0 %all-gather = bf16[4,192,2]{1,2,0:T(2,128)(2,1)S(1)} all-gather(bf16[1,192,2]{1,2,0:T(2,128)(2,1)S(1)} %maximum_bitcast_fusion), channel_id=1, replica_groups=mesh['seq'=8,'fsdp'=4] {'fsdp'}, dimensions={0}, use_global_device_ids=true | all-gather | bytes 3840 | tf_op jit(solution)/shard_map/all_gather | solution.py:258
  16.2 1.2 multiply_sine_fusion
  21.3 21.8 %all-gather.6.cloned.1.call-done.w_ref = bf16[768,2304]{1,0:T(8,128)(2,1)} async-done(((bf16[192,2304]{1,0:T(8,128)(2,1)}), bf16[768,2304]{1,0:T(8,128)(2,1)}) %all-gather.6.cloned.1.call-update) | async-done | bytes 3538960 | tf_op jit(solution)/shard_map/all_gather | solution.py:256
  43.1 8.8 %qkv_forward.1 = (bf16[1024,768]{1,0:T(8,128)(2,1)}, bf16[1024,1536]{1,0:T(8,128)(2,1)}) custom-call(bf16[1024,768]{1,0:T(8,128)(2,1)} %bitcast.30, f32[1,768]{1,0:T(1,128)} %get-tuple-element.58.gain_ref, bf16[768,2304]{1,0:T(8,128)(2,1)} %all-gather.6.cloned.1.call-done.w_ref, f32[512,128]{1,0:T(8,128)} %slice.37.cos_ref, f32[512,128]{1,0:T(8,128)} %slice.38.low_ref, ...), custom_call_target="tpu_custom_call" | custom-call | flops 3623878656 | bytes 9437184 | tf_op jit(solution)/shard_map/qkv_forward/pallas_call | solution.py:283
  53.1 1.3 collective-permute-start.1
  54.4 4.8 %collective-permute-start = (bf16[2,64,1536]{2,1,0:T(8,128)(2,1)S(1)}, bf16[2,64,1536]{2,1,0:T(8,128)(2,1)S(1)}, u32[]{:S(2)}, u32[]{:S(2)}) collective-permute-start(bf16[2,64,1536]{2,1,0:T(8,128)(2,1)S(1)} %get-tuple-element.51), channel_id=1, source_target_pairs={{0,4},{4,8},{8,12},{12,16},{16,20},{20,24},{24,28},{1,5},{5,9},{9,... | collective-permute-start | bytes 1179656 | tf_op jit(solution)/shard_map/ppermute | solution.py:295
  60.3 6.0 %collective-permute-done.1.rk_ref.rv_ref = bf16[2,64,1536]{2,1,0:T(8,128)(2,1)S(1)} collective-permute-done((bf16[2,64,1536]{2,1,0:T(8,128)(2,1)S(1)}, bf16[2,64,1536]{2,1,0:T(8,128)(2,1)S(1)}, u32[]{:S(2)}, u32[]{:S(2)}) %collective-permute-start.1) | collective-permute-done | bytes 393248 | tf_op jit(solution)/shard_map/ppermute | solution.py:296
  66.3 8.5 %collective-permute-done.lk_ref.lv_ref = bf16[2,64,1536]{2,1,0:T(8,128)(2,1)S(1)} collective-permute-done((bf16[2,64,1536]{2,1,0:T(8,128)(2,1)S(1)}, bf16[2,64,1536]{2,1,0:T(8,128)(2,1)S(1)}, u32[]{:S(2)}, u32[]{:S(2)}) %collective-permute-start) | collective-permute-done | bytes 393248 | tf_op jit(solution)/shard_map/ppermute | solution.py:295
  75.5 16.2 %attend_forward.1 = (bf16[2,512,768]{2,1,0:T(8,128)(2,1)}, bf16[2,12,512,256]{3,2,1,0:T(8,128)(2,1)}) custom-call(bf16[2,512,768]{2,1,0:T(8,128)(2,1)} %bitcast.34, bf16[2,512,1536]{2,1,0:T(8,128)(2,1)} %bitcast.21, bf16[2,512,1536]{2,1,0:T(8,128)(2,1)} %bitcast.22, bf16[2,64,1536]{2,1,0:T(8,128)(2,1)} %copy-done.8, bf16[2,64,1536]{2,1,0:T(8,128)(2,1)} %copy-done.8, ...), custom_call_target="tpu_custom_call" | custom-call | flops 3221225472 | bytes 12582912 | tf_op jit(solution)/shard_map/attend_forward/pallas_call | solution.py:310
  91.8 25.0 %all-gather.10.cloned.1.call-done.win_ref = bf16[768,2304]{1,0:T(8,128)(2,1)} async-done(((bf16[192,2304]{1,0:T(8,128)(2,1)}), bf16[768,2304]{1,0:T(8,128)(2,1)}) %all-gather.10.cloned.1.call-update) | async-done | bytes 3538960 | tf_op jit(solution)/shard_map/all_gather | solution.py:256
  116.7 35.3 %mlp_both_ways.1 = (bf16[1024,768]{1,0:T(8,128)(2,1)}, f32[1024,768]{1,0:T(8,128)}, bf16[1024,768]{1,0:T(8,128)(2,1)}, bf16[768,768]{1,0:T(8,128)(2,1)}, bf16[76...) custom-call(bf16[1024,768]{1,0:T(8,128)(2,1)} %bitcast.31, bf16[1024,768]{1,0:T(8,128)(2,1)} %bitcast.37, ...), custom_call_target="tpu_custom_call" | custom-call | flops 19931332608 | bytes 41943040 | tf_op jit(solution)/shard_map/mlp_both_ways/pallas_call | solution.py:322
  153.5 37.1 %attend_backward.1 = (bf16[2,512,768]{2,1,0:T(8,128)(2,1)}, bf16[2,512,768]{2,1,0:T(8,128)(2,1)}, bf16[2,512,768]{2,1,0:T(8,128)(2,1)}, bf16[2,2,64,768]{3,2,1,0:T(8,128)(2,1)}, bf16[2,2,64,768]{3,2,1,0:T(8,128)(2,1)}) custom-call(bf16[2,512,768]{2,1,0:T(8,128)(2,1)} %bitcast.35, bf16[2,512,1536]{2,1,0:T(8,128)(2,1)} %bitcast.23, ...), custom_call_target="tpu_custom_call" | custom-call | flops 6442450944 | bytes 18874368 | tf_op jit(solution)/shard_map/attend_backward/pallas_call | solution.py:353
  190.6 3.4 collective-permute-start.2
  194.0 1.5 collective-permute-start.3
  195.5 15.9 %collective-permute-done.2.fl_ref = bf16[2,2,64,768]{3,2,1,0:T(8,128)(2,1)S(1)} collective-permute-done((bf16[2,2,64,768]{3,2,1,0:T(8,128)(2,1)}, bf16[2,2,64,768]{3,2,1,0:T(8,128)(2,1)S(1)}, u32[]{:S(2)}, u32[]{:S(2)}) %collective-permute-start.2) | collective-permute-done | bytes 393248 | tf_op jit(solution)/shard_map/ppermute | solution.py:364
  212.3 15.8 %qkv_backward.1 = (f32[2,512,768]{2,1,0:T(8,128)}, bf16[768,2304]{1,0:T(8,128)(2,1)}, f32[1,768]{1,0:T(1,128)}) custom-call(bf16[2,512,768]{2,1,0:T(8,128)(2,1)} %tok_ref.1, f32[2,512,768]{2,1,0:T(8,128)} %bitcast.32, bf16[2,512,768]{2,1,0:T(8,128)(2,1)} %get-tuple-element.34.dq_ref, bf16[2,512,768]{2,1,0:T(8,128)(2,1)} %get-tuple-element.35.dk_ref, ...), custom_call_target="tpu_custom_call" | custom-call | flops 7247757312 | bytes 15728640 | tf_op jit(solution)/shard_map/qkv_backward/pallas_call | solution.py:369
  229.8 23.9 %reduce-scatter.12.cloned.1.call-done = bf16[192,2304]{1,0:T(8,128)(2,1)} async-done(((bf16[768,2304]{1,0:T(8,128)(2,1)}), bf16[192,2304]{1,0:T(8,128)(2,1)}) %reduce-scatter.12.cloned.1.call-update) | async-done | bytes 884752 | tf_op jit(solution)/shard_map/reduce_scatter | solution.py:342
  253.7 43.2 %reduce-scatter.8.cloned.1.call-done = bf16[192,2304]{1,0:T(8,128)(2,1)} async-done(((bf16[768,2304]{1,0:T(8,128)(2,1)}), bf16[192,2304]{1,0:T(8,128)(2,1)}) %reduce-scatter.8.cloned.1.call-update) | async-done | bytes 884752 | tf_op jit(solution)/shard_map/reduce_scatter | solution.py:342
  296.9 22.7 %reduce-scatter.16.cloned.1.call-done = bf16[192,2]{1,0:T(8,128)(2,1)} async-done(((bf16[768,2]{1,0:T(8,128)(2,1)}), bf16[192,2]{1,0:T(8,128)(2,1)}) %reduce-scatter.16.cloned.1.call-update) | async-done | bytes 784
  320.5 21.8 %psum.35 = f32[2,192]{1,0:T(2,128)S(1)} all-reduce(bf16[2,192]{1,0:T(2,128)(2,1)S(1)} %copy.19), channel_id=1, replica_groups=mesh['seq'=8,'fsdp'=4] {'seq'}, use_global_device_ids=true, to_apply=%region_1.2 | all-reduce | flops 384 | bytes 2304 | tf_op jit(solution)/shard_map/psum | solution.py:385
  342.8 94.4 %all-reduce.3.cloned.1.call-done = (bf16[192,2304]{1,0:T(8,128)(2,1)}, bf16[192,768]{1,0:T(8,128)(2,1)}, bf16[192,2304]{1,0:T(8,128)(2,1)}, bf16[288,768]{1,0:T(8,128)(2,1)}) async-done(((bf16[192,2304]{1,0:T(8,128)(2,1)}, bf16[192,768]{1,0:T(8,128)(2,1)}, bf16[192,2304]{1,0:T(8,128)(2,1)}, bf16[288,768]{1,0:T(8,128)(2,1)}), (bf16[192,2304]{1,0:T(8,128)(2,1)}, bf16[192,768]{1,0:T(8,128)(2,1)}, ...) | async-done | bytes 2506768 | tf_op jit(solution)/shard_map/psum | solution.py:385
  437.2 1.9 convert_element_type.34
  439.1 2.6 convert_element_type.33
  442.7 1.3 convert_element_type.35
  (78 shorter events, 16.2 us)
Async XLA Ops:
  7.2 2.9 copy-start.11
  7.2 2.9 copy-start.12
  7.2 35.9 %all-gather.6.cloned.1.call-start = ((), (), s32[]{:S(2)}) async-start(), calls=%async_computation.5 | async-start | bytes 4423680 | tf_op jit(solution)/shard_map/all_gather | solution.py:256
  7.9 83.8 %all-gather.8.cloned.1.call-start = ((), (), s32[]{:S(2)}) async-start(), calls=%async_computation.6 | async-start | bytes 1474560 | tf_op jit(solution)/shard_map/all_gather | solution.py:256
  8.7 83.1 %all-gather.12.cloned.1.call-start = ((), (), s32[]{:S(2)}) async-start(), calls=%async_computation.8 | async-start | bytes 2211840 | tf_op jit(solution)/shard_map/all_gather | solution.py:256
  9.4 107.3 %all-gather.10.cloned.1.call-start = ((), (), s32[]{:S(2)}) async-start(), calls=%async_computation.7 | async-start | bytes 4423680 | tf_op jit(solution)/shard_map/all_gather | solution.py:256
  10.0 219.8 %reduce-scatter.10.cloned.1.call-start = ((), (), s32[]{:S(2)}) async-start(), calls=%async_computation.10 | async-start | bytes 1474560 | tf_op jit(solution)/shard_map/reduce_scatter | solution.py:342
  18.0 33.9 %copy-start.1 = (f32[640,128]{1,0:T(8,128)}, f32[640,128]{1,0:T(8,128)S(1)}, u32[]{:S(2)}) copy-start(f32[640,128]{1,0:T(8,128)S(1)} %get-tuple-element.52.high_ref) | copy-start | bytes 983044
  18.0 33.9 %copy-start.2 = (f32[640,128]{1,0:T(8,128)}, f32[640,128]{1,0:T(8,128)S(1)}, u32[]{:S(2)}) copy-start(f32[640,128]{1,0:T(8,128)S(1)} %get-tuple-element.53.low_ref) | copy-start | bytes 983044
  19.9 32.0 %copy-start = (f32[640,128]{1,0:T(8,128)}, f32[640,128]{1,0:T(8,128)S(1)}, u32[]{:S(2)}) copy-start(f32[640,128]{1,0:T(8,128)S(1)} %pad_maximum_fusion.cos_ref) | copy-start | bytes 983044
  53.1 13.2 %collective-permute-start.1 = (bf16[2,64,1536]{2,1,0:T(8,128)(2,1)S(1)}, bf16[2,64,1536]{2,1,0:T(8,128)(2,1)S(1)}, u32[]{:S(2)}, u32[]{:S(2)}) collective-permute-start(bf16[2,64,1536]{2,1,0:T(8,128)(2,1)S(1)} %get-tuple-element.50), channel_id=1, source_target_pairs={{4,0},{8,4},{12,8},{16,12},{20,16},{24,20},{28,24},{5,1},{9,5},{13... | collective-permute-start | bytes 1179656 | tf_op jit(solution)/shard_map/ppermute | solution.py:296
  54.4 20.3 %collective-permute-start = (bf16[2,64,1536]{2,1,0:T(8,128)(2,1)S(1)}, bf16[2,64,1536]{2,1,0:T(8,128)(2,1)S(1)}, u32[]{:S(2)}, u32[]{:S(2)}) collective-permute-start(bf16[2,64,1536]{2,1,0:T(8,128)(2,1)S(1)} %get-tuple-element.51), channel_id=1, source_target_pairs={{0,4},{4,8},{8,12},{12,16},{16,20},{20,24},{24,28},{1,5},{5,9},{9,... | collective-permute-start | bytes 1179656 | tf_op jit(solution)/shard_map/ppermute | solution.py:295
  66.3 8.5 %copy-start.7 = (bf16[2,64,1536]{2,1,0:T(8,128)(2,1)}, bf16[2,64,1536]{2,1,0:T(8,128)(2,1)S(1)}, u32[]{:S(2)}) copy-start(bf16[2,64,1536]{2,1,0:T(8,128)(2,1)S(1)} %collective-permute-done.1.rk_ref.rv_ref) | copy-start | bytes 1179652
  74.8 0.7 copy-start.8
  152.1 77.7 %reduce-scatter.14.cloned.1.call-start = ((), (), s32[]{:S(2)}) async-start(), calls=%async_computation.12 | async-start | bytes 2211840 | tf_op jit(solution)/shard_map/reduce_scatter | solution.py:342
  152.7 101.0 %reduce-scatter.12.cloned.1.call-start = ((), (), s32[]{:S(2)}) async-start(), calls=%async_computation.11 | async-start | bytes 4423680 | tf_op jit(solution)/shard_map/reduce_scatter | solution.py:342
  153.4 143.4 %reduce-scatter.8.cloned.1.call-start = ((), (), s32[]{:S(2)}) async-start(), calls=%async_computation.9 | async-start | bytes 4423680 | tf_op jit(solution)/shard_map/reduce_scatter | solution.py:342
  190.6 20.9 %collective-permute-start.2 = (bf16[2,2,64,768]{3,2,1,0:T(8,128)(2,1)}, bf16[2,2,64,768]{3,2,1,0:T(8,128)(2,1)S(1)}, u32[]{:S(2)}, u32[]{:S(2)}) collective-permute-start(bf16[2,2,64,768]{3,2,1,0:T(8,128)(2,1)} %get-tuple-element.37), channel_id=1, source_target_pairs={{0,4},{4,8},{8,12},{12,16},{16,20},{20,24},{24,28},{1,5},{5,9},{9,... | collective-permute-start | bytes 1179656 | tf_op jit(solution)/shard_map/ppermute | solution.py:364
  194.0 17.5 %collective-permute-start.3 = (bf16[2,2,64,768]{3,2,1,0:T(8,128)(2,1)}, bf16[2,2,64,768]{3,2,1,0:T(8,128)(2,1)S(1)}, u32[]{:S(2)}, u32[]{:S(2)}) collective-permute-start(bf16[2,2,64,768]{3,2,1,0:T(8,128)(2,1)} %get-tuple-element.38), channel_id=1, source_target_pairs={{4,0},{8,4},{12,8},{16,12},{20,16},{24,20},{28,24},{5,1},{9,5},{13... | collective-permute-start | bytes 1179656 | tf_op jit(solution)/shard_map/ppermute | solution.py:365
  211.5 0.9 copy-start.10
  228.1 91.5 %reduce-scatter.16.cloned.1.call-start = ((), (), s32[]{:S(2)}) async-start(), calls=%async_computation.13 | async-start | bytes 245760
  229.7 207.5 %all-reduce.3.cloned.1.call-start = ((), (), s32[]{:S(2)}) async-start(), calls=%async_computation.14 | async-start | bytes 5013504 | tf_op jit(solution)/shard_map/psum | solution.py:385
  437.2 4.4 copy-start.4
  439.1 3.5 copy-start.3
  (3 other events, 2.1 us)
Sparse Core Ops, SparseCore 0:
  9.6 33.4 all-gather.5
  44.6 17.4 all-gather.7
  63.7 20.7 all-gather.11
  85.9 30.7 all-gather.9
  152.2 25.7 reduce-scatter.9
  181.2 29.3 reduce-scatter.13
  213.2 40.4 reduce-scatter.11
  256.4 40.4 reduce-scatter.7
  299.9 19.7 reduce-scatter.15
  323.4 113.7 all-reduce.2

commit v2 on v1

--- a/solution.py
+++ b/solution.py
@@ -133,9 +133,39 @@
     dr_ref[0, 1] = va[WIN + count :].astype(bf16)
 
 
+def pack(dst, sources):
+    shares, depth, width = dst.shape
+    for f in range(shares):
+        at = 0
+        for src in sources:
+            n = src.shape[0] // shares
+            for j in range(src.shape[1] // width):
+                dst[f, at : at + n] = src[f * n : (f + 1) * n, j * width : (j + 1) * width].astype(bf16)
+                at += n
+        if at < depth:
+            dst[f, at:] = jnp.zeros((depth - at, width), bf16)
+
+
+def unpack(share, shapes):
+    width = share.shape[1]
+    outs, at = [], 0
+    for n, columns in shapes:
+        parts = []
+        for _ in range(columns // width):
+            parts.append(share[at : at + n])
+            at += n
+        outs.append(jnp.concatenate(parts, axis=1) if len(parts) > 1 else parts[0])
+    return outs
+
+
+def padded_rows(n, seq_size):
+    unit = 16 * seq_size
+    return -(-n // unit) * unit
+
+
 def mlp_kernel(
     tok_ref, att_ref, go_ref, gain_ref, wo_ref, win_ref, wout_ref,
-    out_ref, mg_ref, ag_ref, dwo_ref, dwin_ref, dwout_ref, dgain_ref,
+    out_ref, mg_ref, ag_ref, pack_ref, dgain_ref,
     awo, awin, awout, wg_buf, hid_buf,
 ):
     step = pl.program_id(0)
@@ -181,14 +211,12 @@
 
     @pl.when(step == pl.num_programs(0) - 1)
     def _():
-        dwo_ref[...] = awo[...].astype(bf16)
-        dwin_ref[...] = awin[...].astype(bf16)
-        dwout_ref[...] = awout[...].astype(bf16)
+        pack(pack_ref, (awin, awo, awout))
 
 
 def qkv_back_kernel(
     tok_ref, mg_ref, dq_ref, dk_ref, dv_ref, fl_ref, fr_ref, gain_ref, w_ref,
-    tg_ref, dw_ref, dgain_ref, acc, buf,
+    tg_ref, pack_ref, dgain_ref, acc, buf,
 ):
     step = pl.program_id(0)
 
@@ -220,7 +248,101 @@
 
     @pl.when(step == pl.num_programs(0) - 1)
     def _():
-        dw_ref[...] = acc[...].astype(bf16)
+        pack(pack_ref, (acc,))
+
+
+def gather_plan(shapes):
+    plan = []
+    for a, (n, columns) in enumerate(shapes):
+        half = n // 2
+        parts = 2 if half % 32 == 0 and n * columns > 300000 else 1
+        plan += [(a, k * half // parts, half // parts) for k in range(parts)]
+    return plan
+
+
+def gather_kernel(*refs):
+    ins, outs = refs[:4], refs[4:8]
+    own_sem, xs, xr, ys, yr, cs, cr = refs[8:]
+    plan = gather_plan([r.shape for r in ins])
+    count = len(plan)
+    seq, me = lax.axis_index("seq"), lax.axis_index("fsdp")
+    across = lax.rem(me + 2, 4)
+    core = me + 1 - 2 * lax.rem(me, 2)
+    side = lax.rem(seq, 2)
+    beside = {"seq": seq + 1 - 2 * side}
+    barrier = pltpu.get_barrier_semaphore()
+    for target in ({"fsdp": across}, {"fsdp": core}, beside):
+        pl.semaphore_signal(barrier, inc=1, device_id=target, device_id_type=pl.DeviceIdType.MESH)
+    pl.semaphore_wait(barrier, 3)
+
+    def send(src, dst, ss, rs, target):
+        copy = pltpu.make_async_remote_copy(
+            src_ref=src, dst_ref=dst, send_sem=ss, recv_sem=rs,
+            device_id=target, device_id_type=pl.DeviceIdType.MESH,
+        )
+        copy.start()
+        return copy
+
+    def place(a, owner, which, off, n):
+        rows = ins[a].shape[0]
+        at = owner * rows + which * (rows // 2) + off
+        return outs[a].at[pl.ds(pl.multiple_of(at, 16), n)]
+
+    def first_hop(k):
+        a, off, n = plan[k]
+        half = ins[a].shape[0] // 2
+        src = ins[a].at[pl.ds(pl.multiple_of(side * half + off, 16), n)]
+        return send(src, place(a, me, side, off, n), xs.at[k], xr.at[k], {"fsdp": across})
+
+    hops = [first_hop(k) for k in range(count)]
+    local, pairs = [], []
+    for a in range(4):
+        n = ins[a].shape[0]
+        spot = outs[a].at[pl.ds(pl.multiple_of(me * n, 16), n)]
+        copy = pltpu.make_async_copy(ins[a], spot, own_sem.at[a])
+        copy.start()
+        local.append(copy)
+        pairs.append(send(ins[a], spot, cs.at[a], cr.at[a], {"fsdp": core}))
+    seconds = []
+
+    def relay(k):
+        a, off, n = plan[k]
+        seconds[k].wait_recv()
+        spot = place(a, across, 1 - side, off, n)
+        i = 4 + count + k
+        pairs.append(send(spot, spot, cs.at[i], cr.at[i], {"fsdp": core}))
+
+    for k in range(count):
+        a, off, n = plan[k]
+        hops[k].wait_recv()
+        spot = place(a, across, side, off, n)
+        seconds.append(send(spot, spot, ys.at[k], yr.at[k], beside))
+        pairs.append(send(spot, spot, cs.at[4 + k], cr.at[4 + k], {"fsdp": core}))
+        if k:
+            relay(k - 1)
+    relay(count - 1)
+    for copy in local:
+        copy.wait()
+    for copy in hops + seconds:
+        copy.wait_send()
+    for copy in pairs:
+        copy.wait_send()
+        copy.wait_recv()
+
+
+def gather_weights(*weights):
+    count = len(gather_plan([w.shape for w in weights]))
+    sems = lambda n: pltpu.SemaphoreType.DMA((n,))
+    return pl.pallas_call(
+        gather_kernel,
+        in_specs=[pl.BlockSpec(memory_space=pl.ANY)] * 4,
+        out_specs=[pl.BlockSpec(memory_space=pl.ANY)] * 4,
+        out_shape=[sds((4 * w.shape[0], w.shape[1]), w.dtype) for w in weights],
+        scratch_shapes=[sems(4)] + [sems(count)] * 4 + [sems(4 + 2 * count)] * 2,
+        compiler_params=pltpu.CompilerParams(collective_id=0, has_side_effects=True),
+        cost_estimate=pl.CostEstimate(flops=0, bytes_accessed=2**26, transcendentals=0),
+        name="gather_weights",
+    )(*weights)
 
 
 def sds(shape, dtype):
@@ -251,14 +373,14 @@
     span = piece + 2 * WIN
     pairs = width // PAIR
     seq_size = lax.axis_size("seq")
+    shares = lax.axis_size("fsdp")
+    mlp_shapes = (mlp_in_weight.shape, attn_out_weight.shape, mlp_out_weight.shape)
+    mlp_rows = padded_rows(sum(n * m // width for n, m in mlp_shapes), seq_size)
+    qkv_rows = padded_rows(3 * qkv_weight.shape[0] + 16, seq_size)
     forward = [(i, i + 1) for i in range(seq_size - 1)]
     backward = [(j, i) for i, j in forward]
-    gather = lambda x: lax.all_gather(x, "fsdp", axis=0, tiled=True)
-    w_qkv = gather(qkv_weight)
     gains = lax.all_gather(jnp.stack([norm_gain_attn, norm_gain_mlp]), "fsdp", axis=1, tiled=True)
-    w_attn = gather(attn_out_weight)
-    w_in = gather(mlp_in_weight)
-    w_out = gather(mlp_out_weight)
+    w_qkv, w_attn, w_in, w_out = gather_weights(qkv_weight, attn_out_weight, mlp_in_weight, mlp_out_weight)
     gain_attn = gains[0:1].astype(f32)
     gain_mlp = gains[1:2].astype(f32)
     start = lax.axis_index("seq") * piece
@@ -319,15 +441,15 @@
         name="attend_forward",
     )(q, *kv_args, bias)
 
-    out, mg, ag, d_wo, d_win, d_wout, d_gain_mlp = pl.pallas_call(
+    out, mg, ag, d_mlp, d_gain_mlp = pl.pallas_call(
         mlp_kernel,
         grid=(rows // tile,),
         in_specs=[row_spec(width)] * 3 + [whole((1, width)), whole(w_attn.shape), whole(w_in.shape), whole(w_out.shape)],
         out_specs=[row_spec(width)] * 3
-        + [whole(w_attn.shape), whole(w_in.shape), whole(w_out.shape), whole((1, width))],
+        + [whole((shares, mlp_rows, width)), whole((1, width))],
         out_shape=[
             sds((rows, width), bf16), sds((rows, width), f32), sds((rows, width), bf16),
-            sds(w_attn.shape, bf16), sds(w_in.shape, bf16), sds(w_out.shape, bf16), sds((1, width), f32),
+            sds((shares, mlp_rows, width), bf16), sds((1, width), f32),
         ],
         scratch_shapes=[
             pltpu.VMEM(w_attn.shape, f32), pltpu.VMEM(w_in.shape, f32), pltpu.VMEM(w_out.shape, f32),
@@ -338,12 +460,12 @@
         name="mlp_both_ways",
     )(tok, flat(attended), flat(grad_out), gain_mlp, w_attn, w_in, w_out)
 
-    def reduce(x, dim=0):
-        mine = lax.psum_scatter(x, "fsdp", scatter_dimension=dim, tiled=True)
-        return mine
-
-    s_win, s_wout, s_wo = reduce(d_win), reduce(d_wout), reduce(d_wo)
-    s_win, s_wout, s_wo = lax.psum((s_win, s_wout, s_wo), "seq")
+    def reduce(x):
+        mine = lax.psum_scatter(x, "fsdp", scatter_dimension=0, tiled=True)[0]
+        part = lax.psum_scatter(mine, "seq", scatter_dimension=0, tiled=True)
+        return lax.all_gather(part, "seq", axis=0, tiled=True)
+
+    mlp_sum = reduce(d_mlp)
 
     table_full = pl.BlockSpec((span, PAIR), lambda s, p: (0, 0))
     edge = pl.BlockSpec((1, 2, WIN, PAIR), lambda s, p: (s, 0, 0, p))
@@ -370,19 +492,23 @@
         qkv_back_kernel,
         grid=(seqs,),
         in_specs=[seq_spec] * 5 + [edge_in] * 2 + [whole((1, width)), whole(w_qkv.shape)],
-        out_specs=[seq_spec, whole(w_qkv.shape), whole((1, width))],
-        out_shape=[sds((seqs, piece, width), f32), sds(w_qkv.shape, bf16), sds((1, width), f32)],
+        out_specs=[seq_spec, whole((shares, qkv_rows, width)), whole((1, width))],
+        out_shape=[sds((seqs, piece, width), f32), sds((shares, qkv_rows, width), bf16), sds((1, width), f32)],
         scratch_shapes=[pltpu.VMEM(w_qkv.shape, f32), pltpu.VMEM((piece, 3 * width), bf16)],
         compiler_params=params(1),
         cost_estimate=pl.CostEstimate(flops=12 * rows * width * width, bytes_accessed=20 * rows * width, transcendentals=0),
         name="qkv_backward",
     )(tokens, mg.reshape(seqs, piece, width), dq, dk, dv, from_left, from_right, gain_attn, w_qkv)
 
-    s_gains = lax.psum_scatter(
-        jnp.concatenate([d_gain_attn, d_gain_mlp]).astype(bf16), "fsdp", scatter_dimension=1, tiled=True
-    ).astype(f32)
-    s_wqkv = reduce(d_wqkv)
-    s_gains, s_wqkv = lax.psum((s_gains, s_wqkv), "seq")
+    gains_at = 3 * qkv_weight.shape[0]
+    both = jnp.concatenate([d_gain_attn, d_gain_mlp]).astype(bf16)
+    both = both.reshape(2, shares, width // shares).swapaxes(0, 1)
+    both = jnp.pad(both, ((0, 0), (0, 0), (0, width - width // shares)))
+    d_wqkv = lax.dynamic_update_slice(d_wqkv, both, (0, gains_at, 0))
+    qkv_sum = reduce(d_wqkv)
+    s_wqkv = unpack(qkv_sum, (qkv_weight.shape,))[0]
+    s_gains = qkv_sum[gains_at : gains_at + 2, : width // shares].astype(f32)
+    s_win, s_wo, s_wout = unpack(mlp_sum, mlp_shapes)
     return (
         out.reshape(seqs, piece, width),
         tokens_grad,

time: 451 us -> 502 us (1.11)
  Pallas kernels: 113 us -> 193 us
  waiting for transfers between devices: 265 us -> 223 us
  blocking collectives: 27.8 us -> 39.9 us
    reduce_scatter x4, waiting for transfers between devices: 67.1 us -> 178 us  [the longest x2 135 us: reduce(): part = lax.psum_scatter(mine, 'seq', scatter_dimension=0, tiled=True)]
    psum x1 -> x0, waiting for transfers between devices: 94.4 us -> none  [shards(): s_gains, s_wqkv = lax.psum((s_gains, s_wqkv), 'seq')]
    pallas_call x0 -> x1, Pallas kernels: none -> 79.7 us  [gather_weights(): pl.pallas_call(gather_kernel, in_specs=[pl.BlockSpec(memory_space=pl.ANY)...]
    all_gather x0 -> x1, blocking collectives: none -> 33.9 us  [reduce(): return lax.all_gather(part, 'seq', axis=0, tiled=True)]
    all_gather x4 -> x1, waiting for transfers between devices: 46.8 us -> 14.8 us  [reduce(): return lax.all_gather(part, 'seq', axis=0, tiled=True)]
    unnamed x11 -> x5, waiting for transfers between devices: 26.6 us -> 0.72 us
    psum x1 -> x0, blocking collectives: 21.8 us -> none  [shards(): s_gains, s_wqkv = lax.psum((s_gains, s_wqkv), 'seq')]
  transfers between devices with their start and end apart: 14 -> 9, of which waited for: 9 -> 7; matrix products, arithmetic and copies ran while one was open for 2% -> 1% of each run, Pallas kernels for 17% -> 11%
where the time goes in v2:
time: 502 us
  waiting for transfers between devices  223 us (44%)
  Pallas kernels  193 us (38%)
  blocking collectives  39.9 us (8%)
  between operations  14 us (3%)
  starting transfers between devices  12.1 us (2%)
  other arithmetic  11.4 us (2%)
  local copies, waits for them, and re-layouts  7.86 us (2%)
    reduce_scatter x2, waiting for transfers between devices, reduce(): part = lax.psum_scatter(mine, 'seq', scatter_dimension=0, tiled=True)  135 us
    pallas_call x1, Pallas kernels, gather_weights(): pl.pallas_call(gather_kernel, in_specs=[pl.BlockSpec(memory_space=pl.ANY)...  79.7 us
    reduce_scatter x2, waiting for transfers between devices, reduce(): mine = lax.psum_scatter(x, 'fsdp', scatter_dimension=0, tiled=True)[0]  42.8 us
    pallas_call x1, Pallas kernels, shards(): pl.pallas_call(attend_back_kernel, grid=(seqs, pairs), in_specs=[lanes(pi...  37.2 us
    pallas_call x1, Pallas kernels, shards(): pl.pallas_call(mlp_kernel, grid=(rows // tile,), in_specs=[row_spec(width...  35.5 us
    all_gather x1, blocking collectives, reduce(): return lax.all_gather(part, 'seq', axis=0, tiled=True)  33.9 us
    pallas_call x1, Pallas kernels, shards(): pl.pallas_call(attend_kernel, grid=(seqs, pairs), in_specs=[lanes(piece)]...  16.1 us
    pallas_call x1, Pallas kernels, shards(): pl.pallas_call(qkv_back_kernel, grid=(seqs,), in_specs=[seq_spec] * 5 + [...  16 us
  transfers between devices with their start and end apart: 9, of which 7 were waited for; matrix products, arithmetic and copies ran while one was open for 1% of the time, Pallas kernels for 11%

profile of v2, /device:TPU:0, one launch (start us, length us, event | category | flops | bytes accessed | tf_op | source)
XLA Modules:
  0.0 501.7 jit_solution(11456152696188877150)
XLA Ops:
  8.6 6.0 %all-gather = bf16[4,192,2]{1,2,0:T(2,128)(2,1)S(1)} all-gather(bf16[1,192,2]{1,2,0:T(2,128)(2,1)S(1)} %maximum_bitcast_fusion.1), channel_id=1, replica_groups=mesh['seq'=8,'fsdp'=4] {'fsdp'}, dimensions={0}, use_global_device_ids=true | all-gather | bytes 3840 | tf_op jit(solution)/shard_map/all_gather | solution.py:382
  15.3 1.2 multiply_sine_fusion
  19.6 79.7 %gather_weights.1 = (bf16[768,2304]{1,0:T(8,128)(2,1)}, bf16[768,768]{1,0:T(8,128)(2,1)}, bf16[768,2304]{1,0:T(8,128)(2,1)}, bf16[1152,768]{1,0:T(8,128)(2,1)}) custom-call(bf16[192,2304]{1,0:T(8,128)(2,1)} %refs_0_.1, bf16[192,768]{1,0:T(8,128)(2,1)} %refs_1_.1, bf16[192,2304]{1,0:T(8,128)(2,1)} %refs_2_.1, bf16[288,768]{1,0:T(8,128)(2,1)} %refs_3_.1), custom_call_target="tpu_custom_call" | custom-call | bytes 67108864 | tf_op jit(solution)/shard_map/gather_weights/pallas_call | solution.py:336
  99.3 8.8 %qkv_forward.1 = (bf16[1024,768]{1,0:T(8,128)(2,1)}, bf16[1024,1536]{1,0:T(8,128)(2,1)}) custom-call(bf16[1024,768]{1,0:T(8,128)(2,1)} %bitcast.32, f32[1,768]{1,0:T(1,128)} %get-tuple-element.65.gain_ref, bf16[768,2304]{1,0:T(8,128)(2,1)} %get-tuple-element.29.w_ref, f32[512,128]{1,0:T(8,128)} %slice.73.cos_ref, f32[512,128]{1,0:T(8,128)} %slice.74.low_ref, ...), custom_call_target="tpu_custom_call" | custom-call | flops 3623878656 | bytes 9437184 | tf_op jit(solution)/shard_map/qkv_forward/pallas_call | solution.py:405
  109.4 1.3 collective-permute-start.1
  110.7 4.8 collective-permute-start
  116.6 5.7 %collective-permute-done.1.rk_ref.rv_ref = bf16[2,64,1536]{2,1,0:T(8,128)(2,1)S(1)} collective-permute-done((bf16[2,64,1536]{2,1,0:T(8,128)(2,1)S(1)}, bf16[2,64,1536]{2,1,0:T(8,128)(2,1)S(1)}, u32[]{:S(2)}, u32[]{:S(2)}) %collective-permute-start.1) | collective-permute-done | bytes 393248 | tf_op jit(solution)/shard_map/ppermute | solution.py:418
  122.3 8.3 %collective-permute-done.lk_ref.lv_ref = bf16[2,64,1536]{2,1,0:T(8,128)(2,1)S(1)} collective-permute-done((bf16[2,64,1536]{2,1,0:T(8,128)(2,1)S(1)}, bf16[2,64,1536]{2,1,0:T(8,128)(2,1)S(1)}, u32[]{:S(2)}, u32[]{:S(2)}) %collective-permute-start) | collective-permute-done | bytes 393248 | tf_op jit(solution)/shard_map/ppermute | solution.py:417
  131.4 16.1 %attend_forward.1 = (bf16[2,512,768]{2,1,0:T(8,128)(2,1)}, bf16[2,12,512,256]{3,2,1,0:T(8,128)(2,1)}) custom-call(bf16[2,512,768]{2,1,0:T(8,128)(2,1)} %bitcast.36, bf16[2,512,1536]{2,1,0:T(8,128)(2,1)} %bitcast.24, bf16[2,512,1536]{2,1,0:T(8,128)(2,1)} %bitcast.25, bf16[2,64,1536]{2,1,0:T(8,128)(2,1)} %copy-done.5, bf16[2,64,1536]{2,1,0:T(8,128)(2,1)} %copy-done.5, ...), custom_call_target="tpu_custom_call" | custom-call | flops 3221225472 | bytes 12582912 | tf_op jit(solution)/shard_map/attend_forward/pallas_call | solution.py:432
  147.5 35.5 %mlp_both_ways.1 = (bf16[1024,768]{1,0:T(8,128)(2,1)}, f32[1024,768]{1,0:T(8,128)}, bf16[1024,768]{1,0:T(8,128)(2,1)}, bf16[4,1152,768]{2,1,0:T(8,128)(2,1)}, f32[1,768]{1,0:T(1,128)}) custom-call(bf16[1024,768]{1,0:T(8,128)(2,1)} %bitcast.33, bf16[1024,768]{1,0:T(8,128)(2,1)} %bitcast.39, bf16[1024,768]{1,0:T(8,128)(2,1)} %bitcast.31, ...), custom_call_target="tpu_custom_call" | custom-call | flops 19931332608 | bytes 41943040 | tf_op jit(solution)/shard_map/mlp_both_ways/pallas_call | solution.py:444
  183.1 37.2 %attend_backward.1 = (bf16[2,512,768]{2,1,0:T(8,128)(2,1)}, bf16[2,512,768]{2,1,0:T(8,128)(2,1)}, bf16[2,512,768]{2,1,0:T(8,128)(2,1)}, bf16[2,2,64,768]{3,2,1,0:T(8,128)(2,1)}, bf16[2,2,64,768]{3,2,1,0:T(8,128)(2,1)}) custom-call(bf16[2,512,768]{2,1,0:T(8,128)(2,1)} %bitcast.37, bf16[2,512,1536]{2,1,0:T(8,128)(2,1)} %bitcast.26, ...), custom_call_target="tpu_custom_call" | custom-call | flops 6442450944 | bytes 18874368 | tf_op jit(solution)/shard_map/attend_backward/pallas_call | solution.py:475
  220.2 4.4 collective-permute-start.2
  224.6 1.5 collective-permute-start.3
  226.3 15.6 %collective-permute-done.2.fl_ref = bf16[2,2,64,768]{3,2,1,0:T(8,128)(2,1)S(1)} collective-permute-done((bf16[2,2,64,768]{3,2,1,0:T(8,128)(2,1)}, bf16[2,2,64,768]{3,2,1,0:T(8,128)(2,1)S(1)}, u32[]{:S(2)}, u32[]{:S(2)}) %collective-permute-start.2) | collective-permute-done | bytes 393248 | tf_op jit(solution)/shard_map/ppermute | solution.py:486
  242.8 16.0 %qkv_backward.1 = (f32[2,512,768]{2,1,0:T(8,128)}, bf16[4,640,768]{2,1,0:T(8,128)(2,1)}, f32[1,768]{1,0:T(1,128)}) custom-call(bf16[2,512,768]{2,1,0:T(8,128)(2,1)} %tok_ref.1, f32[2,512,768]{2,1,0:T(8,128)} %bitcast.34, bf16[2,512,768]{2,1,0:T(8,128)(2,1)} %get-tuple-element.40.dq_ref, bf16[2,512,768]{2,1,0:T(8,128)(2,1)} %get-tuple-element.41.dk_ref, ...), custom_call_target="tpu_custom_call" | custom-call | flops 7247757312 | bytes 15728640 | tf_op jit(solution)/shard_map/qkv_backward/pallas_call | solution.py:491
  261.0 42.8 %reduce-scatter.5.cloned.1.call-done = bf16[1,640,768]{2,1,0:T(8,128)(2,1)} async-done(((bf16[4,640,768]{2,1,0:T(8,128)(2,1)}), bf16[1,640,768]{2,1,0:T(8,128)(2,1)}) %reduce-scatter.5.cloned.1.call-update) | async-done | bytes 983056 | tf_op jit(solution)/shard_map/reduce_scatter | solution.py:464
  303.9 69.3 %reduce-scatter.11.cloned.1.call-done = bf16[144,768]{1,0:T(8,128)(2,1)} async-done(((bf16[1152,768]{1,0:T(8,128)(2,1)}), bf16[144,768]{1,0:T(8,128)(2,1)}) %reduce-scatter.11.cloned.1.call-update) | async-done | bytes 221200 | tf_op jit(solution)/shard_map/reduce_scatter | solution.py:465
  373.2 65.8 %reduce-scatter.7.cloned.1.call-done = bf16[80,768]{1,0:T(8,128)(2,1)} async-done(((bf16[640,768]{1,0:T(8,128)(2,1)}), bf16[80,768]{1,0:T(8,128)(2,1)}) %reduce-scatter.7.cloned.1.call-update) | async-done | bytes 122896 | tf_op jit(solution)/shard_map/reduce_scatter | solution.py:465
  439.1 33.9 %all_gather.10 = bf16[640,768]{1,0:T(8,128)(2,1)S(1)} all-gather(bf16[80,768]{1,0:T(8,128)(2,1)} %reduce-scatter.7.cloned.1.call-done), channel_id=1, replica_groups=mesh['seq'=8,'fsdp'=4] {'seq'}, dimensions={0}, use_global_device_ids=true | all-gather | bytes 1105920 | tf_op jit(solution)/shard_map/all_gather | solution.py:466
  473.7 1.3 maximum_convert_fusion
  475.0 14.8 %all-gather.3.cloned.1.call-done = bf16[1152,768]{1,0:T(8,128)(2,1)} async-done(((bf16[144,768]{1,0:T(8,128)(2,1)}), bf16[1152,768]{1,0:T(8,128)(2,1)}) %all-gather.3.cloned.1.call-update) | async-done | bytes 1769488 | tf_op jit(solution)/shard_map/all_gather | solution.py:466
  489.7 2.1 fusion.7
  491.9 1.3 maximum_convert_fusion.1
  493.2 2.0 slice_convert_fusion
  (56 shorter events, 12.2 us)
Async XLA Ops:
  7.2 253.1 %reduce-scatter.9.cloned.1.call-start = ((), (), s32[]{:S(2)}) async-start(), calls=%async_computation.6 | async-start | bytes 8847360 | tf_op jit(solution)/shard_map/reduce_scatter | solution.py:464
  17.4 82.0 %copy-start = (f32[640,128]{1,0:T(8,128)}, f32[640,128]{1,0:T(8,128)S(1)}, u32[]{:S(2)}) copy-start(f32[640,128]{1,0:T(8,128)S(1)} %get-tuple-element.59.high_ref) | copy-start | bytes 983044
  17.4 82.0 %copy-start.1 = (f32[640,128]{1,0:T(8,128)}, f32[640,128]{1,0:T(8,128)S(1)}, u32[]{:S(2)}) copy-start(f32[640,128]{1,0:T(8,128)S(1)} %get-tuple-element.60.low_ref) | copy-start | bytes 983044
  17.4 82.0 %copy-start.2 = (f32[640,128]{1,0:T(8,128)}, f32[640,128]{1,0:T(8,128)S(1)}, u32[]{:S(2)}) copy-start(f32[640,128]{1,0:T(8,128)S(1)} %get-tuple-element.70.cos_ref) | copy-start | bytes 983044
  109.4 13.0 %collective-permute-start.1 = (bf16[2,64,1536]{2,1,0:T(8,128)(2,1)S(1)}, bf16[2,64,1536]{2,1,0:T(8,128)(2,1)S(1)}, u32[]{:S(2)}, u32[]{:S(2)}) collective-permute-start(bf16[2,64,1536]{2,1,0:T(8,128)(2,1)S(1)} %get-tuple-element.50), channel_id=1, source_target_pairs={{4,0},{8,4},{12,8},{16,12},{20,16},{24,20},{28,24},{5,1},{9,5},{13... | collective-permute-start | bytes 1179656 | tf_op jit(solution)/shard_map/ppermute | solution.py:418
  110.7 20.0 %collective-permute-start = (bf16[2,64,1536]{2,1,0:T(8,128)(2,1)S(1)}, bf16[2,64,1536]{2,1,0:T(8,128)(2,1)S(1)}, u32[]{:S(2)}, u32[]{:S(2)}) collective-permute-start(bf16[2,64,1536]{2,1,0:T(8,128)(2,1)S(1)} %get-tuple-element.51), channel_id=1, source_target_pairs={{0,4},{4,8},{8,12},{12,16},{16,20},{20,24},{24,28},{1,5},{5,9},{9,... | collective-permute-start | bytes 1179656 | tf_op jit(solution)/shard_map/ppermute | solution.py:417
  122.3 8.3 %copy-start.4 = (bf16[2,64,1536]{2,1,0:T(8,128)(2,1)}, bf16[2,64,1536]{2,1,0:T(8,128)(2,1)S(1)}, u32[]{:S(2)}) copy-start(bf16[2,64,1536]{2,1,0:T(8,128)(2,1)S(1)} %collective-permute-done.1.rk_ref.rv_ref) | copy-start | bytes 1179652
  130.6 0.7 copy-start.5
  183.0 120.8 %reduce-scatter.5.cloned.1.call-start = ((), (), s32[]{:S(2)}) async-start(), calls=%async_computation.4 | async-start | bytes 4915200 | tf_op jit(solution)/shard_map/reduce_scatter | solution.py:464
  183.1 43.1 %copy-start.3 = (f32[1,768]{1,0:T(1,128)S(1)}, f32[1,768]{1,0:T(1,128)}, u32[]{:S(2)}) copy-start(f32[1,768]{1,0:T(1,128)} %get-tuple-element.48) | copy-start | bytes 9220
  220.2 21.6 %collective-permute-start.2 = (bf16[2,2,64,768]{3,2,1,0:T(8,128)(2,1)}, bf16[2,2,64,768]{3,2,1,0:T(8,128)(2,1)S(1)}, u32[]{:S(2)}, u32[]{:S(2)}) collective-permute-start(bf16[2,2,64,768]{3,2,1,0:T(8,128)(2,1)} %get-tuple-element.43), channel_id=1, source_target_pairs={{0,4},{4,8},{8,12},{12,16},{16,20},{20,24},{24,28},{1,5},{5,9},{9,... | collective-permute-start | bytes 1179656 | tf_op jit(solution)/shard_map/ppermute | solution.py:486
  224.6 17.3 %collective-permute-start.3 = (bf16[2,2,64,768]{3,2,1,0:T(8,128)(2,1)}, bf16[2,2,64,768]{3,2,1,0:T(8,128)(2,1)S(1)}, u32[]{:S(2)}, u32[]{:S(2)}) collective-permute-start(bf16[2,2,64,768]{3,2,1,0:T(8,128)(2,1)} %get-tuple-element.44), channel_id=1, source_target_pairs={{4,0},{8,4},{12,8},{16,12},{20,16},{24,20},{28,24},{5,1},{9,5},{13... | collective-permute-start | bytes 1179656 | tf_op jit(solution)/shard_map/ppermute | solution.py:487
  241.9 0.7 copy-start.6
  241.9 0.9 copy-start.7
  260.2 113.0 %reduce-scatter.11.cloned.1.call-start = ((), (), s32[]{:S(2)}) async-start(), calls=%async_computation.7 | async-start | bytes 1990656 | tf_op jit(solution)/shard_map/reduce_scatter | solution.py:465
  261.0 178.1 %reduce-scatter.7.cloned.1.call-start = ((), (), s32[]{:S(2)}) async-start(), calls=%async_computation.5 | async-start | bytes 1105920 | tf_op jit(solution)/shard_map/reduce_scatter | solution.py:465
  303.9 185.9 %all-gather.3.cloned.1.call-start = ((), (), s32[]{:S(2)}) async-start(), calls=%async_computation.8 | async-start | bytes 1990656 | tf_op jit(solution)/shard_map/all_gather | solution.py:466
Sparse Core Ops, SparseCore 0:
  183.1 64.2 reduce-scatter.8
  260.4 43.4 reduce-scatter.4
  307.3 65.8 reduce-scatter.10
  376.8 62.2 reduce-scatter.6
  441.1 48.5 all-gather.2

commit v3 on v1

v3 whole, which is shorter than its diff:
```python
import functools
import math

import jax
import jax.numpy as jnp
from jax import lax
from jax.experimental import pallas as pl
from jax.experimental.pallas import tpu as pltpu
from jax.sharding import PartitionSpec as P

HEADS = 12
HEAD_DIM = 64
FF = 1152
WIN = 64
PAIR = 128
BLOCK = 128

epsilon = 1e-05
rope_base = 10000.0
negative = -1e30
f32 = jnp.float32
bf16 = jnp.bfloat16
LIMIT = 56 * 1024 * 1024

NN = (((1,), (0,)), ((), ()))
NT = (((1,), (1,)), ((), ()))
TN = (((0,), (0,)), ((), ()))


def mm(a, b, dims=NN):
    return lax.dot_general(a, b, dims, preferred_element_type=f32)


def unit_rows(x):
    center = x - jnp.mean(x, axis=-1, keepdims=True)
    inverse = lax.rsqrt(jnp.mean(center * center, axis=-1, keepdims=True) + epsilon)
    return center * inverse, inverse


def turn(x, cos, low, high):
    return x * cos + pltpu.roll(x, PAIR - 32, 1) * low + pltpu.roll(x, 32, 1) * high


def qkv_kernel(tok_ref, gain_ref, w_ref, cos_ref, low_ref, high_ref, q_ref, kv_ref):
    unit, _ = unit_rows(tok_ref[...].astype(f32))
    normed = (unit * gain_ref[...]).astype(bf16)
    cos, low, high = cos_ref[...], low_ref[...], high_ref[...]
    width = q_ref.shape[1]
    step = 2 * PAIR
    for j in range(3 * width // step):
        part = mm(normed, w_ref[:, j * step : (j + 1) * step])
        for h in range(2):
            at = j * step + h * PAIR
            piece = part[:, h * PAIR : (h + 1) * PAIR]
            if at < width:
                q_ref[:, at : at + PAIR] = (
                    turn(piece, cos, low, high) * (1.0 / math.sqrt(HEAD_DIM))
                ).astype(bf16)
            elif at < 2 * width:
                kv_ref[:, at - width : at - width + PAIR] = turn(piece, cos, low, high).astype(bf16)
            else:
                kv_ref[:, at - width : at - width + PAIR] = piece.astype(bf16)


def by_head(x):
    first = (lax.broadcasted_iota(jnp.int32, (1, PAIR), 1) < HEAD_DIM).astype(f32)
    return jnp.concatenate([x * first.astype(bf16), x * (1.0 - first).astype(bf16)], axis=0)


def own_heads(x):
    both = jnp.concatenate([x[:HEAD_DIM, :BLOCK], x[HEAD_DIM:, BLOCK:]], axis=0)
    return both.T


def fill(dst, left, mid, right):
    n = mid.shape[1]
    dst[0:WIN] = left[0]
    dst[WIN : WIN + n] = mid[0]
    dst[WIN + n : 2 * WIN + n] = right[0]


def attend_kernel(q_ref, k_ref, v_ref, lk_ref, lv_ref, rk_ref, rv_ref, bias_ref, att_ref, p_ref, ke, ve):
    fill(ke, lk_ref, k_ref, rk_ref)
    fill(ve, lv_ref, v_ref, rv_ref)
    vt = ve[...].T
    for i in range(q_ref.shape[1] // BLOCK):
        rows = slice(i * BLOCK, (i + 1) * BLOCK)
        span = slice(i * BLOCK, (i + 1) * BLOCK + 2 * WIN)
        scores = mm(ke[span], by_head(q_ref[0, rows]), NT)
        scores = scores + jnp.concatenate([bias_ref[i]] * 2, axis=1)
        raised = jnp.exp(scores - jnp.max(scores, axis=0, keepdims=True))
        total = jnp.sum(raised, axis=0, keepdims=True)
        probs = (raised * (1.0 / total)).astype(bf16)
        p_ref[0, 0, i] = probs
        att_ref[0, rows] = own_heads(mm(vt[:, span], probs)).astype(bf16)


def attend_back_kernel(
    q_ref, k_ref, v_ref, lk_ref, lv_ref, rk_ref, rv_ref, p_ref, ag_ref, cos_ref, low_ref, high_ref,
    dq_ref, dk_ref, dv_ref, dl_ref, dr_ref, ke, ve, ka, va,
):
    fill(ke, lk_ref, k_ref, rk_ref)
    fill(ve, lv_ref, v_ref, rv_ref)
    ka[...] = jnp.zeros_like(ka)
    va[...] = jnp.zeros_like(va)
    count = q_ref.shape[1]
    scale = 1.0 / math.sqrt(HEAD_DIM)
    kt = ke[...].T
    for i in range(count // BLOCK):
        rows = slice(i * BLOCK, (i + 1) * BLOCK)
        span = slice(i * BLOCK, (i + 1) * BLOCK + 2 * WIN)
        upstream = by_head(ag_ref[0, rows])
        low_probs = p_ref[0, 0, i]
        probs = low_probs.astype(f32)
        back = mm(ve[span], upstream, NT)
        delta = jnp.sum(probs * back, axis=0, keepdims=True)
        grad = (probs * (back - delta)).astype(bf16)
        dq = own_heads(mm(kt[:, span], grad)) * scale
        at = slice(WIN + i * BLOCK, WIN + (i + 1) * BLOCK)
        dq_ref[0, rows] = turn(dq, cos_ref[at], -low_ref[at], -high_ref[at]).astype(bf16)
        ka[span] += mm(grad, by_head(q_ref[0, rows]))
        va[span] += mm(low_probs, upstream)
    dk = turn(ka[...], cos_ref[...], -low_ref[...], -high_ref[...])
    dl_ref[0, 0] = dk[:WIN].astype(bf16)
    dk_ref[0] = dk[WIN : WIN + count].astype(bf16)
    dr_ref[0, 0] = dk[WIN + count :].astype(bf16)
    dl_ref[0, 1] = va[:WIN].astype(bf16)
    dv_ref[0] = va[WIN : WIN + count].astype(bf16)
    dr_ref[0, 1] = va[WIN + count :].astype(bf16)


def unpack(share, shapes):
    width = share.shape[1]
    outs, at = [], 0
    for n, columns in shapes:
        parts = []
        for _ in range(columns // width):
            parts.append(share[at : at + n])
            at += n
        outs.append(jnp.concatenate(parts, axis=1) if len(parts) > 1 else parts[0])
    return outs


def padded_rows(n, seq_size):
    unit = 16 * seq_size
    return -(-n // unit) * unit


def mlp_kernel(
    steps,
    tok_ref, att_ref, go_ref, gain_ref, wo_ref, win_ref, wout_ref,
    out_ref, mg_ref, ag_ref, pack_ref, dgain_ref,
    awo, awin, awout, wg_buf, hid_buf,
):
    step = pl.program_id(0)

    @pl.when(step == 0)
    def _():
        dgain_ref[...] = jnp.zeros_like(dgain_ref)

    attended, go = att_ref[...], go_ref[...]
    middle = tok_ref[...].astype(f32) + mm(attended, wo_ref[...])
    gain = gain_ref[...]
    unit, inverse = unit_rows(middle)
    normed = (unit * gain).astype(bf16)
    chunk = 384
    for c in range(FF // chunk):
        cols = slice(c * chunk, (c + 1) * chunk)
        gate = slice(FF + c * chunk, FF + (c + 1) * chunk)
        a = mm(normed, win_ref[:, cols])
        b = mm(normed, win_ref[:, gate])
        hg = mm(go, wout_ref[cols, :], NT)
        cdf = 0.5 * (1.0 + lax.erf(a * (1.0 / math.sqrt(2.0))))
        gelu = a * cdf
        slope = cdf + a * (jnp.exp(-0.5 * a * a) * (1.0 / math.sqrt(2.0 * math.pi)))
        hid_buf[:, cols] = (gelu * b).astype(bf16)
        wg_buf[:, cols] = (hg * b * slope).astype(bf16)
        wg_buf[:, gate] = (hg * gelu).astype(bf16)
    hidden, wg = hid_buf[...], wg_buf[...]
    out_ref[...] = (middle + mm(hidden, wout_ref[...])).astype(bf16)
    back = mm(wg, win_ref[...], NT)
    dgain_ref[...] += jnp.sum(back * unit, axis=0, keepdims=True)
    e = back * gain
    part = e - jnp.mean(e, axis=-1, keepdims=True) - unit * jnp.mean(e * unit, axis=-1, keepdims=True)
    mg = go.astype(f32) + inverse * part
    mg_ref[...] = mg
    low = mg.astype(bf16)
    ag_ref[...] = mm(low, wo_ref[...], NT).astype(bf16)
    products = ((awin, normed, wg), (awo, attended, low), (awout, hidden, go))
    last = steps - 1

    @pl.when(step == 0)
    def _():
        for acc, lhs, rhs in products:
            acc[...] = mm(lhs, rhs, TN)

    if steps > 2:

        @pl.when((step > 0) & (step < last))
        def _():
            for acc, lhs, rhs in products:
                acc[...] += mm(lhs, rhs, TN)

    @pl.when(step == last)
    def _():
        shares, depth, width = pack_ref.shape
        at = 0
        for acc, lhs, rhs in products:
            n = acc.shape[0] // shares
            for j in range(acc.shape[1] // width):
                cols = slice(j * width, (j + 1) * width)
                for f in range(shares):
                    mine = slice(f * n, (f + 1) * n)
                    piece = mm(lhs[:, mine], rhs[:, cols], TN) + acc[mine, cols]
                    pack_ref[f, at : at + n] = piece.astype(bf16)
                at += n
        if at < depth:
            for f in range(shares):
                pack_ref[f, at:] = jnp.zeros((depth - at, width), bf16)


def qkv_back_kernel(
    prior, kept, last, tok_ref, mg_ref, dq_ref, dk_ref, dv_ref, fl_ref, fr_ref, gain_ref, w_ref, *refs
):
    tg_ref, dw_ref, dgain_ref, buf = refs[prior + kept :]
    width = tok_ref.shape[2]
    count = tok_ref.shape[1]
    buf[:, :width] = dq_ref[0]
    for j, ref in enumerate((dk_ref, dv_ref)):
        cols = slice((j + 1) * width, (j + 2) * width)
        buf[:, cols] = ref[0]
        buf[:WIN, cols] = (ref[0, :WIN].astype(f32) + fl_ref[0, j].astype(f32)).astype(bf16)
        buf[count - WIN :, cols] = (
            ref[0, count - WIN :].astype(f32) + fr_ref[0, j].astype(f32)
        ).astype(bf16)
    gain = gain_ref[...]
    unit, inverse = unit_rows(tok_ref[0].astype(f32))
    normed = (unit * gain).astype(bf16)
    grads = buf[...]
    back = mm(grads, w_ref[...], NT)
    gain_grad = jnp.sum(back * unit, axis=0, keepdims=True)
    dgain_ref[...] = gain_grad + refs[1][...] if prior else gain_grad
    e = back * gain
    part = e - jnp.mean(e, axis=-1, keepdims=True) - unit * jnp.mean(e * unit, axis=-1, keepdims=True)
    tg_ref[0] = mg_ref[0] + inverse * part
    for j in range(3):
        cols = slice(j * width, (j + 1) * width)
        piece = mm(normed, grads[:, cols], TN)
        if prior:
            piece = piece + refs[0][:, cols].astype(f32)
        if not last:
            dw_ref[:, cols] = piece.astype(bf16)
            continue
        shares = dw_ref.shape[0]
        n = piece.shape[0] // shares
        for f in range(shares):
            dw_ref[f, j * n : (j + 1) * n] = piece[f * n : (f + 1) * n].astype(bf16)
    if last:
        at = 3 * w_ref.shape[0] // dw_ref.shape[0]
        dw_ref[:, at:] = jnp.zeros((dw_ref.shape[0], dw_ref.shape[1] - at, width), bf16)


def reduce_kernel(pack_ref, out_ref, mine, got, total, far, ls, cs, cr, xs, xr):
    me = lax.axis_index("fsdp")
    across = lax.rem(me + 2, 4)
    core = me + 1 - 2 * lax.rem(me, 2)
    barrier = pltpu.get_barrier_semaphore()
    for target in (across, core):
        pl.semaphore_signal(
            barrier, inc=1, device_id={"fsdp": target}, device_id_type=pl.DeviceIdType.MESH
        )
    pl.semaphore_wait(barrier, 2)
    parts = xs.shape[0]
    n = out_ref.shape[0] // parts
    rows = [pl.ds(k * n, n) for k in range(parts)]

    def send(src, dst, ss, rs, target):
        copy = pltpu.make_async_remote_copy(
            src_ref=src, dst_ref=dst, send_sem=ss, recv_sem=rs,
            device_id={"fsdp": target}, device_id_type=pl.DeviceIdType.MESH,
        )
        copy.start()
        return copy

    pairs, locals_ = {}, {}
    for slot, theirs, ours in ((0, lax.rem(core + 2, 4), across), (1, core, me)):
        for k in range(parts):
            i = slot * parts + k
            pairs[slot, k] = send(pack_ref.at[theirs, rows[k]], got.at[slot, rows[k]], cs.at[i], cr.at[i], core)
            copy = pltpu.make_async_copy(pack_ref.at[ours, rows[k]], mine.at[slot, rows[k]], ls.at[i])
            copy.start()
            locals_[slot, k] = copy
    hops = []
    for k in range(parts):
        locals_[0, k].wait()
        pairs[0, k].wait_recv()
        total[rows[k]] = (mine[0, rows[k]].astype(f32) + got[0, rows[k]].astype(f32)).astype(bf16)
        hops.append(send(total.at[rows[k]], far.at[rows[k]], xs.at[k], xr.at[k], across))
    for k in range(parts):
        locals_[1, k].wait()
        pairs[1, k].wait_recv()
        hops[k].wait_recv()
        out_ref[rows[k]] = (
            mine[1, rows[k]].astype(f32) + got[1, rows[k]].astype(f32) + far[rows[k]].astype(f32)
        ).astype(bf16)
    for copy in list(pairs.values()) + hops:
        copy.wait_send()


def reduce_fsdp(x, parts):
    shares, n, width = x.shape
    sems = lambda m: pltpu.SemaphoreType.DMA((m,))
    vmem = lambda *shape: pltpu.VMEM(shape, bf16)
    return pl.pallas_call(
        reduce_kernel,
        in_specs=[pl.BlockSpec(memory_space=pl.ANY)],
        out_specs=pl.BlockSpec(memory_space=pltpu.VMEM),
        out_shape=sds((n, width), bf16),
        scratch_shapes=[vmem(2, n, width), vmem(2, n, width), vmem(n, width), vmem(n, width)]
        + [sems(2 * parts)] * 3 + [sems(parts)] * 2,
        compiler_params=pltpu.CompilerParams(collective_id=1, has_side_effects=True, vmem_limit_bytes=LIMIT),
        cost_estimate=pl.CostEstimate(flops=0, bytes_accessed=2**26, transcendentals=0),
        name="reduce_fsdp",
    )(x)


def sds(shape, dtype):
    return jax.ShapeDtypeStruct(shape, dtype)


def whole(shape):
    return pl.BlockSpec(shape, lambda *_: (0,) * len(shape), pipeline_mode=pl.Buffered(1))


def tables(start, count):
    half = HEAD_DIM // 2
    freqs = rope_base ** (-(jnp.arange(half, dtype=f32) * 2.0 / HEAD_DIM))
    positions = (start + jnp.arange(count, dtype=jnp.int32)).astype(f32)
    angles = positions[:, None] * freqs[None, :]
    cos, sin = jnp.cos(angles), jnp.sin(angles)
    none = jnp.zeros_like(sin)
    return (
        jnp.concatenate([cos] * 4, axis=-1),
        jnp.concatenate([-sin, none] * 2, axis=-1),
        jnp.concatenate([none, sin] * 2, axis=-1),
    )


def shards(tokens, norm_gain_attn, qkv_weight, attn_out_weight, norm_gain_mlp, mlp_in_weight, mlp_out_weight, grad_out):
    seqs, piece, width = tokens.shape
    rows = seqs * piece
    span = piece + 2 * WIN
    pairs = width // PAIR
    seq_size = lax.axis_size("seq")
    shares = lax.axis_size("fsdp")
    mlp_shapes = (mlp_in_weight.shape, attn_out_weight.shape, mlp_out_weight.shape)
    mlp_rows = sum(n * m // width for n, m in mlp_shapes)
    qkv_rows = padded_rows(3 * qkv_weight.shape[0] + 16, seq_size)
    forward = [(i, i + 1) for i in range(seq_size - 1)]
    backward = [(j, i) for i, j in forward]
    gains = lax.all_gather(jnp.stack([norm_gain_attn, norm_gain_mlp]), "fsdp", axis=1, tiled=True)
    gather = lambda x: lax.all_gather(x, "fsdp", axis=0, tiled=True)
    w_qkv = gather(qkv_weight)
    w_attn = gather(attn_out_weight)
    w_in = gather(mlp_in_weight)
    w_out = gather(mlp_out_weight)
    gain_attn = gains[0:1].astype(f32)
    gain_mlp = gains[1:2].astype(f32)
    start = lax.axis_index("seq") * piece
    cos, low, high = tables(start - WIN, span)
    q_at = start + jnp.arange(piece, dtype=jnp.int32).reshape(-1, BLOCK)[:, None, :]
    k_at = (
        start - WIN
        + jnp.arange(piece // BLOCK, dtype=jnp.int32)[:, None, None] * BLOCK
        + jnp.arange(BLOCK + 2 * WIN, dtype=jnp.int32)[None, :, None]
    )
    inside = (jnp.abs(q_at - k_at) <= WIN) & (k_at >= 0) & (k_at < piece * seq_size)
    bias = jnp.where(inside, 0.0, negative).astype(f32)

    tile = 256
    per = piece // tile
    flat = lambda x: x.reshape(rows, x.shape[-1])
    row_spec = lambda w: pl.BlockSpec((tile, w), lambda i: (i, 0))
    table_spec = pl.BlockSpec((tile, PAIR), lambda i: (lax.rem(i, per), 0))
    params = lambda n: pltpu.CompilerParams(dimension_semantics=("arbitrary",) * n, vmem_limit_bytes=LIMIT)
    tok = flat(tokens)
    mid = slice(WIN, WIN + piece)
    def project(x, *rotary):
        count = x.shape[0]
        return pl.pallas_call(
            qkv_kernel,
            grid=(count // tile,),
            in_specs=[row_spec(width), whole((1, width)), whole(w_qkv.shape), table_spec, table_spec, table_spec],
            out_specs=[row_spec(width), row_spec(2 * width)],
            out_shape=[sds((count, width), bf16), sds((count, 2 * width), bf16)],
            compiler_params=params(1),
            cost_estimate=pl.CostEstimate(flops=6 * count * width * width, bytes_accessed=12 * count * width, transcendentals=0),
            name="qkv_forward",
        )(x, gain_attn, w_qkv, *rotary)

    borders = lambda x, n: jnp.concatenate([x[..., :WIN, :], x[..., n - WIN :, :]], axis=-2)
    _, kv_border = project(
        borders(tokens, piece).reshape(-1, width),
        *(jnp.tile(borders(t[mid], piece), (seqs, 1)) for t in (cos, low, high)),
    )
    kv_border = kv_border.reshape(seqs, 2 * WIN, 2 * width)
    left = lax.ppermute(kv_border[:, WIN:], "seq", forward)
    right = lax.ppermute(kv_border[:, :WIN], "seq", backward)
    q, kv = project(tok, cos[mid], low[mid], high[mid])
    q = q.reshape(seqs, piece, width)
    kv = kv.reshape(seqs, piece, 2 * width)

    def lanes(n, off=0):
        return pl.BlockSpec((1, n, PAIR), lambda s, p: (s, 0, p + off))

    kv_specs = [
        lanes(piece), lanes(piece, pairs), lanes(WIN), lanes(WIN, pairs), lanes(WIN), lanes(WIN, pairs),
    ]
    kv_args = (kv, kv, left, left, right, right)
    p_block = (1, 1, piece // BLOCK, BLOCK + 2 * WIN, 2 * BLOCK)
    p_spec = pl.BlockSpec(p_block, lambda s, p: (s, p, 0, 0, 0))
    p_shape = (seqs, pairs) + p_block[2:]
    ext = pltpu.VMEM((span, PAIR), bf16)
    unit_flops = 2 * seqs * HEADS * piece * (BLOCK + 2 * WIN) * HEAD_DIM
    p_bytes = 2 * math.prod(p_shape)
    attended, probs = pl.pallas_call(
        attend_kernel,
        grid=(seqs, pairs),
        in_specs=[lanes(piece)] + kv_specs + [whole(bias.shape)],
        out_specs=[lanes(piece), p_spec],
        out_shape=[sds((seqs, piece, width), bf16), sds(p_shape, bf16)],
        scratch_shapes=[ext, ext],
        compiler_params=params(2),
        cost_estimate=pl.CostEstimate(flops=8 * unit_flops, bytes_accessed=p_bytes + 8 * rows * width, transcendentals=p_bytes // 2),
        name="attend_forward",
    )(q, *kv_args, bias)

    wide = piece
    wide_spec = pl.BlockSpec((wide, width), lambda i: (i, 0))
    out, mg, ag, d_mlp, d_gain_mlp = pl.pallas_call(
        functools.partial(mlp_kernel, rows // wide),
        grid=(rows // wide,),
        in_specs=[wide_spec] * 3 + [whole((1, width)), whole(w_attn.shape), whole(w_in.shape), whole(w_out.shape)],
        out_specs=[wide_spec] * 3
        + [whole((shares, mlp_rows, width)), whole((1, width))],
        out_shape=[
            sds((rows, width), bf16), sds((rows, width), f32), sds((rows, width), bf16),
            sds((shares, mlp_rows, width), bf16), sds((1, width), f32),
        ],
        scratch_shapes=[
            pltpu.VMEM(w_attn.shape, f32), pltpu.VMEM(w_in.shape, f32), pltpu.VMEM(w_out.shape, f32),
            pltpu.VMEM((wide, 2 * FF), bf16), pltpu.VMEM((wide, FF), bf16),
        ],
        compiler_params=params(1),
        cost_estimate=pl.CostEstimate(flops=6 * rows * width * (width + 3 * FF), bytes_accessed=40 * 2**20, transcendentals=0),
        name="mlp_both_ways",
    )(tok, flat(attended), flat(grad_out), gain_mlp, w_attn, w_in, w_out)

    mlp_sum = lax.psum(lax.psum_scatter(d_mlp, "fsdp", scatter_dimension=0, tiled=True)[0], "seq")

    table_full = pl.BlockSpec((span, PAIR), lambda p: (0, 0))
    edge_shape = sds((1, 2, WIN, width), bf16)
    own = sds((1, piece, width), bf16)
    total = pltpu.VMEM((span, PAIR), f32)
    ag = ag.reshape(seqs, piece, width)
    mg = mg.reshape(seqs, piece, width)

    def attend_back(s):
        def at(n, off=0):
            return pl.BlockSpec((1, n, PAIR), lambda p: (s, 0, p + off))

        here = pl.BlockSpec((1, piece, PAIR), lambda p: (0, 0, p))
        edge = pl.BlockSpec((1, 2, WIN, PAIR), lambda p: (0, 0, 0, p))
        return pl.pallas_call(
            attend_back_kernel,
            grid=(pairs,),
            in_specs=[at(piece), at(piece), at(piece, pairs), at(WIN), at(WIN, pairs), at(WIN), at(WIN, pairs)]
            + [pl.BlockSpec(p_block, lambda p: (s, p, 0, 0, 0)), at(piece)]
            + [table_full] * 3,
            out_specs=[here] * 3 + [edge, edge],
            out_shape=[own] * 3 + [edge_shape] * 2,
            scratch_shapes=[ext, ext, total, total],
            compiler_params=params(1),
            cost_estimate=pl.CostEstimate(flops=8 * unit_flops, bytes_accessed=p_bytes // 2 + 8 * rows * width, transcendentals=0),
            name="attend_backward",
        )(q, *kv_args, probs, ag, cos, low, high)

    one = pl.BlockSpec((1, piece, width), lambda i: (0, 0, 0))
    edge_in = pl.BlockSpec((1, 2, WIN, width), lambda i: (0, 0, 0, 0))

    def qkv_back(s, grads, before, tokens_grad):
        this = pl.BlockSpec((1, piece, width), lambda i: (s, 0, 0))
        last = s == seqs - 1
        prior = [] if before is None else list(before)
        to = (shares, qkv_rows, width) if last else w_qkv.shape
        kept = [] if tokens_grad is None else [tokens_grad]
        args = [tokens, mg, *grads, gain_attn, w_qkv, *prior, *kept]
        return pl.pallas_call(
            functools.partial(qkv_back_kernel, len(prior), len(kept), last),
            grid=(1,),
            in_specs=[this] * 2 + [one] * 3 + [edge_in] * 2 + [whole((1, width)), whole(w_qkv.shape)]
            + [whole(p.shape) for p in prior] + [pl.BlockSpec(memory_space=pl.ANY)] * len(kept),
            out_specs=[this, whole(to), whole((1, width))],
            out_shape=[sds(tokens.shape, f32), sds(to, bf16), sds((1, width), f32)],
            scratch_shapes=[pltpu.VMEM((piece, 3 * width), bf16)],
            input_output_aliases={len(args) - 1: 0} if kept else {},
            compiler_params=params(1),
            cost_estimate=pl.CostEstimate(flops=12 * piece * width * width, bytes_accessed=20 * piece * width, transcendentals=0),
            name="qkv_backward",
        )(*args)

    grads = []
    for s in range(seqs):
        dq, dk, dv, dl, dr = attend_back(s)
        grads.append((dq, dk, dv, lax.ppermute(dr, "seq", forward), lax.ppermute(dl, "seq", backward)))
    before = tokens_grad = None
    for s in range(seqs):
        tokens_grad, *before = qkv_back(s, grads[s], before, tokens_grad)
    d_wqkv, d_gain_attn = before

    gains_at = 3 * qkv_weight.shape[0]
    both = jnp.concatenate([d_gain_attn, d_gain_mlp]).astype(bf16)
    both = both.reshape(2, shares, width // shares).swapaxes(0, 1)
    both = jnp.pad(both, ((0, 0), (0, 0), (0, width - width // shares)))
    d_wqkv = lax.dynamic_update_slice(d_wqkv, both, (0, gains_at, 0))
    qkv_share, mlp_sum = lax.optimization_barrier((reduce_fsdp(d_wqkv, 4), mlp_sum))
    qkv_sum = lax.psum(qkv_share, "seq")
    s_wqkv = unpack(qkv_sum, (qkv_weight.shape,))[0]
    s_gains = qkv_sum[gains_at : gains_at + 2, : width // shares].astype(f32)
    s_win, s_wo, s_wout = unpack(mlp_sum, mlp_shapes)
    return (
        out.reshape(seqs, piece, width),
        tokens_grad,
        s_gains[0],
        s_wqkv.astype(f32),
        s_wo.astype(f32),
        s_gains[1],
        s_win.astype(f32),
        s_wout.astype(f32),
    )


def solution(mesh):
    return jax.shard_map(
        shards,
        mesh=mesh,
        in_specs=(
            P("fsdp", "seq", None),
            P("fsdp"),
            P("fsdp", None),
            P("fsdp", None),
            P("fsdp"),
            P("fsdp", None),
            P("fsdp", None),
            P("fsdp", "seq", None),
        ),
        out_specs=(
            P("fsdp", "seq", None),
            P("fsdp", "seq", None),
            P("fsdp"),
            P("fsdp", None),
            P("fsdp", None),
            P("fsdp"),
            P("fsdp", None),
            P("fsdp", None),
        ),
        check_vma=False,
    )
```

time: 451 us -> 406 us (0.900)
  waiting for transfers between devices: 265 us -> 200 us
  Pallas kernels: 113 us -> 144 us
  blocking collectives: 27.8 us -> 5.98 us
  starting transfers between devices: 11.3 us -> 16.7 us
    ppermute x4 -> x6, waiting for transfers between devices: 30.4 us -> 3.27 us  [the longest x1 3.25 us: shards(): left = lax.ppermute(kv_border[:, WIN:], 'seq', forward)]
    pallas_call x4 -> x8, Pallas kernels: 97 us -> 123 us  [the longest x1 34.8 us: shards(): pl.pallas_call(functools.partial(mlp_kernel, rows // wide), grid=(rows //...]
    unnamed x11 -> x7, waiting for transfers between devices: 26.6 us -> 2.63 us
    psum x1 -> x0, blocking collectives: 21.8 us -> none  [shards(): s_gains, s_wqkv = lax.psum((s_gains, s_wqkv), 'seq')]
    reduce_scatter x4 -> x1, waiting for transfers between devices: 67.1 us -> 59.8 us  [shards(): lax.psum_scatter(d_mlp, 'fsdp', scatter_dimension=0, tiled=True)[0]]
    ppermute x4 -> x6, starting transfers between devices: 11 us -> 16.4 us  [the longest x2 7.97 us: shards(): lax.ppermute(dr, 'seq', forward)]
    pallas_call x1, Pallas kernels: 16.2 us -> 21.6 us  [shards(): pl.pallas_call(attend_kernel, grid=(seqs, pairs), in_specs=[lanes(piece)]...]
    psum x1 -> x2, waiting for transfers between devices: 94.4 us -> 90.6 us  [the longest x1 76 us: shards(): qkv_sum = lax.psum(qkv_share, 'seq')]
  transfers between devices with their start and end apart: 14 -> 13, of which waited for: 9 -> 6; matrix products, arithmetic and copies ran while one was open for 2% -> 4% of each run, Pallas kernels for 17% -> 27%
where the time goes in v3:
time: 406 us; the launch traced here: 405 us
  waiting for transfers between devices  200 us (49%)
  Pallas kernels  144 us (35%)
  starting transfers between devices  16.7 us (4%)
  between operations  14.5 us (4%)
  other arithmetic  12.1 us (3%)
  local copies, waits for them, and re-layouts  11.5 us (3%)
  blocking collectives  5.98 us (1%)
    psum x1, waiting for transfers between devices, shards(): qkv_sum = lax.psum(qkv_share, 'seq')  76 us
    reduce_scatter x1, waiting for transfers between devices, shards(): lax.psum_scatter(d_mlp, 'fsdp', scatter_dimension=0, tiled=True)[0]  59.8 us
    all_gather x4, waiting for transfers between devices, shards(): gather = lambda x: lax.all_gather(x, 'fsdp', axis=0, tiled=True)  44.1 us
    pallas_call x1, Pallas kernels, shards(): pl.pallas_call(functools.partial(mlp_kernel, rows // wide), grid=(rows //...  34.8 us
    pallas_call x2, Pallas kernels, attend_back(): pl.pallas_call(attend_back_kernel, grid=(pairs,), in_specs=[at(piece), at...  27.7 us
    pallas_call x1, Pallas kernels, reduce_fsdp(): pl.pallas_call(reduce_kernel, in_specs=[pl.BlockSpec(memory_space=pl.ANY)...  26.9 us
    pallas_call x1, Pallas kernels, shards(): pl.pallas_call(attend_kernel, grid=(seqs, pairs), in_specs=[lanes(piece)]...  21.6 us
    pallas_call x2, Pallas kernels, qkv_back(): pl.pallas_call(functools.partial(qkv_back_kernel, len(prior), len(kept),...  20 us
  transfers between devices with their start and end apart: 13, of which 6 were waited for; matrix products, arithmetic and copies ran while one was open for 4% of the time, Pallas kernels for 27%

profile of v3, /device:TPU:0, one launch (start us, length us, event | category | flops | bytes accessed | tf_op | source)
XLA Modules:
  0.0 405.4 jit_solution(16978273197931343192)
XLA Ops:
  10.1 6.0 %all-gather = bf16[4,192,2]{1,2,0:T(2,128)(2,1)S(1)} all-gather(bf16[1,192,2]{1,2,0:T(2,128)(2,1)S(1)} %maximum_bitcast_fusion.1), channel_id=1, replica_groups=mesh['seq'=8,'fsdp'=4] {'fsdp'}, dimensions={0}, use_global_device_ids=true | all-gather | bytes 3840 | tf_op jit(solution)/shard_map/all_gather | solution.py:361
  21.2 21.9 %all-gather.6.cloned.1.call-done.w_ref = bf16[768,2304]{1,0:T(8,128)(2,1)} async-done(((bf16[192,2304]{1,0:T(8,128)(2,1)}), bf16[768,2304]{1,0:T(8,128)(2,1)}) %all-gather.6.cloned.1.call-update) | async-done | bytes 3538960 | tf_op jit(solution)/shard_map/all_gather | solution.py:362
  45.1 4.4 %qkv_forward.3 = (bf16[256,768]{1,0:T(8,128)(2,1)}, bf16[256,1536]{1,0:T(8,128)(2,1)}) custom-call(bf16[256,768]{1,0:T(8,128)(2,1)} %bitcast.41, f32[1,768]{1,0:T(1,128)} %get-tuple-element.87.gain_ref, bf16[768,2304]{1,0:T(8,128)(2,1)} %all-gather.6.cloned.1.call-done.w_ref, f32[256,128]{1,0:T(8,128)} %bitcast.45, f32[256,128]{1,0:T(8,128)} %bitcast.44, ...), custom_call_target="tpu_custom_call" | custom-call | flops 905969664 | bytes 2359296 | tf_op jit(solution)/shard_map/qkv_forward/pallas_call | solution.py:390
  50.7 1.3 collective-permute-start.1
  52.0 4.6 %collective-permute-start = (bf16[2,64,1536]{2,1,0:T(8,128)(2,1)S(1)}, bf16[2,64,1536]{2,1,0:T(8,128)(2,1)S(1)}, u32[]{:S(2)}, u32[]{:S(2)}) collective-permute-start(bf16[2,64,1536]{2,1,0:T(8,128)(2,1)S(1)} %get-tuple-element.74), channel_id=1, source_target_pairs={{0,4},{4,8},{8,12},{12,16},{16,20},{20,24},{24,28},{1,5},{5,9},{9,... | collective-permute-start | bytes 1179656 | tf_op jit(solution)/shard_map/ppermute | solution.py:407
  60.1 8.8 %qkv_forward.2 = (bf16[1024,768]{1,0:T(8,128)(2,1)}, bf16[1024,1536]{1,0:T(8,128)(2,1)}) custom-call(bf16[1024,768]{1,0:T(8,128)(2,1)} %bitcast.38, f32[1,768]{1,0:T(1,128)} %get-tuple-element.87.gain_ref, bf16[768,2304]{1,0:T(8,128)(2,1)} %all-gather.6.cloned.1.call-done.w_ref, f32[512,128]{1,0:T(8,128)} %slice.114.cos_ref, f32[512,128]{1,0:T(8,128)} %slice.115.low_ref, ...), custom_call_target="tpu_custom_call" | custom-call | flops 3623878656 | bytes 9437184 | tf_op jit(solution)/shard_map/qkv_forward/pallas_call | solution.py:390
  68.9 3.3 collective-permute-done.lk_ref.lv_ref
  72.9 21.6 %attend_forward.1 = (bf16[2,512,768]{2,1,0:T(8,128)(2,1)}, bf16[2,6,4,256,256]{4,3,2,1,0:T(8,128)(2,1)}) custom-call(bf16[2,512,768]{2,1,0:T(8,128)(2,1)} %bitcast.31, bf16[2,512,1536]{2,1,0:T(8,128)(2,1)} %bitcast.25, bf16[2,512,1536]{2,1,0:T(8,128)(2,1)} %bitcast.26, bf16[2,64,1536]{2,1,0:T(8,128)(2,1)} %copy-done.1, bf16[2,64,1536]{2,1,0:T(8,128)(2,1)} %copy-done.1, ...), custom_call_target="tpu_custom_call" | custom-call | flops 3221225472 | bytes 12582912 | tf_op jit(solution)/shard_map/attend_forward/pallas_call | solution.py:426
  94.6 22.2 %all-gather.10.cloned.1.call-done.win_ref = bf16[768,2304]{1,0:T(8,128)(2,1)} async-done(((bf16[192,2304]{1,0:T(8,128)(2,1)}), bf16[768,2304]{1,0:T(8,128)(2,1)}) %all-gather.10.cloned.1.call-update) | async-done | bytes 3538960 | tf_op jit(solution)/shard_map/all_gather | solution.py:362
  116.7 34.8 %mlp_both_ways.1 = (bf16[1024,768]{1,0:T(8,128)(2,1)}, f32[1024,768]{1,0:T(8,128)}, bf16[1024,768]{1,0:T(8,128)(2,1)}, bf16[4,1056,768]{2,1,0:T(8,128)(2,1)}, f32[1,768]{1,0:T(1,128)}) custom-call(bf16[1024,768]{1,0:T(8,128)(2,1)} %bitcast.39, bf16[1024,768]{1,0:T(8,128)(2,1)} %bitcast.51, bf16[1024,768]{1,0:T(8,128)(2,1)} %bitcast.49, ...), custom_call_target="tpu_custom_call" | custom-call | flops 19931332608 | bytes 41943040 | tf_op jit(solution)/shard_map/mlp_both_ways/pallas_call | solution.py:440
  151.6 59.8 %reduce-scatter.2.cloned.1.call-done = bf16[1,1056,768]{2,1,0:T(8,128)(2,1)} async-done(((bf16[4,1056,768]{2,1,0:T(8,128)(2,1)}), bf16[1,1056,768]{2,1,0:T(8,128)(2,1)}) %reduce-scatter.2.cloned.1.call-update) | async-done | bytes 1622032 | tf_op jit(solution)/shard_map/reduce_scatter | solution.py:459
  211.6 13.9 %attend_backward.3 = (bf16[1,512,768]{2,1,0:T(8,128)(2,1)}, bf16[1,512,768]{2,1,0:T(8,128)(2,1)}, bf16[1,512,768]{2,1,0:T(8,128)(2,1)}, bf16[1,2,64,768]{3,2,1,0:T(8,128)(2,1)}, bf16[1,2,64,768]{3,2,1,0:T(8,128)(2,1)}) custom-call(bf16[2,512,768]{2,1,0:T(8,128)(2,1)} %bitcast.32, bf16[2,512,1536]{2,1,0:T(8,128)(2,1)} %bitcast.27, ...), custom_call_target="tpu_custom_call" | custom-call | flops 3221225472 | bytes 9437184 | tf_op jit(solution)/shard_map/attend_backward/pallas_call | solution.py:474
  225.4 3.4 collective-permute-start.4
  228.8 1.3 collective-permute-start.5
  230.1 13.8 %attend_backward.2 = (bf16[1,512,768]{2,1,0:T(8,128)(2,1)}, bf16[1,512,768]{2,1,0:T(8,128)(2,1)}, bf16[1,512,768]{2,1,0:T(8,128)(2,1)}, bf16[1,2,64,768]{3,2,1,0:T(8,128)(2,1)}, bf16[1,2,64,768]{3,2,1,0:T(8,128)(2,1)}) custom-call(bf16[2,512,768]{2,1,0:T(8,128)(2,1)} %bitcast.33, bf16[2,512,1536]{2,1,0:T(8,128)(2,1)} %bitcast.29, ...), custom_call_target="tpu_custom_call" | custom-call | flops 3221225472 | bytes 9437184 | tf_op jit(solution)/shard_map/attend_backward/pallas_call | solution.py:474
  244.0 4.6 %collective-permute-start.2 = (bf16[1,2,64,768]{3,2,1,0:T(8,128)(2,1)}, bf16[1,2,64,768]{3,2,1,0:T(8,128)(2,1)S(1)}, u32[]{:S(2)}, u32[]{:S(2)}) collective-permute-start(bf16[1,2,64,768]{3,2,1,0:T(8,128)(2,1)} %get-tuple-element.47), channel_id=1, source_target_pairs={{0,4},{4,8},{8,12},{12,16},{16,20},{20,24},{24,28},{1,5},{5,9},{9,... | collective-permute-start | bytes 589832 | tf_op jit(solution)/shard_map/ppermute | solution.py:515
  250.6 9.4 %qkv_backward.2 = (f32[2,512,768]{2,1,0:T(8,128)}, bf16[768,2304]{1,0:T(8,128)(2,1)}, f32[1,768]{1,0:T(1,128)}) custom-call(bf16[2,512,768]{2,1,0:T(8,128)(2,1)} %tok_ref.3, f32[2,512,768]{2,1,0:T(8,128)} %bitcast.36, bf16[1,512,768]{2,1,0:T(8,128)(2,1)} %get-tuple-element.49.dq_ref, bf16[1,512,768]{2,1,0:T(8,128)(2,1)} %get-tuple-element.50.dk_ref, ...), custom_call_target="tpu_custom_call" | custom-call | flops 3623878656 | bytes 7864320 | tf_op jit(solution)/shard_map/qkv_backward/pallas_call | solution.py:498
  260.8 10.6 %qkv_backward.3 = (f32[2,512,768]{2,1,0:T(8,128)}, bf16[4,640,768]{2,1,0:T(8,128)(2,1)}, f32[1,768]{1,0:T(1,128)}) custom-call(bf16[2,512,768]{2,1,0:T(8,128)(2,1)} %tok_ref.3, f32[2,512,768]{2,1,0:T(8,128)} %bitcast.37, bf16[1,512,768]{2,1,0:T(8,128)(2,1)} %get-tuple-element.44.dq_ref, ...), custom_call_target="tpu_custom_call", output_to_operand_aliasing={{0}: (11, {})} | custom-call | flops 3623878656 | bytes 7864320 | tf_op jit(solution)/shard_map/qkv_backward/pallas_call | solution.py:498
  272.9 26.9 %reduce_fsdp.1 = bf16[640,768]{1,0:T(8,128)(2,1)} custom-call(bf16[4,640,768]{2,1,0:T(8,128)(2,1)} %pad_dynamic-update-slice_fusion.pack_ref), custom_call_target="tpu_custom_call" | custom-call | bytes 67108864 | tf_op jit(solution)/shard_map/reduce_fsdp/pallas_call | solution.py:314
  299.8 14.6 %all-reduce.4.cloned.1.call-done = bf16[1056,768]{1,0:T(8,128)(2,1)} async-done(((bf16[1056,768]{1,0:T(8,128)(2,1)}), bf16[1056,768]{1,0:T(8,128)(2,1)}) %all-reduce.4.cloned.1.call-update) | async-done | bytes 1622032 | tf_op jit(solution)/shard_map/psum | solution.py:459
  314.5 2.1 slice_convert_fusion
  317.5 1.3 maximum_convert_fusion.1
  318.8 76.0 %all-reduce.6.cloned.1.call-done = bf16[640,768]{1,0:T(8,128)(2,1)} async-done(((bf16[640,768]{1,0:T(8,128)(2,1)}), bf16[640,768]{1,0:T(8,128)(2,1)}) %all-reduce.6.cloned.1.call-update) | async-done | bytes 983056 | tf_op jit(solution)/shard_map/psum | solution.py:527
  397.3 1.3 maximum_convert_fusion
  (89 shorter events, 23.0 us)
Async XLA Ops:
  7.2 2.9 copy-start.11
  7.2 2.9 copy-start.12
  7.2 35.9 %all-gather.6.cloned.1.call-start = ((), (), s32[]{:S(2)}) async-start(), calls=%async_computation.1 | async-start | bytes 4423680 | tf_op jit(solution)/shard_map/all_gather | solution.py:362
  7.9 86.6 %all-gather.8.cloned.1.call-start = ((), (), s32[]{:S(2)}) async-start(), calls=%async_computation.2 | async-start | bytes 1474560 | tf_op jit(solution)/shard_map/all_gather | solution.py:362
  8.7 85.9 %all-gather.12.cloned.1.call-start = ((), (), s32[]{:S(2)}) async-start(), calls=%async_computation.4 | async-start | bytes 2211840 | tf_op jit(solution)/shard_map/all_gather | solution.py:362
  9.4 107.3 %all-gather.10.cloned.1.call-start = ((), (), s32[]{:S(2)}) async-start(), calls=%async_computation.3 | async-start | bytes 4423680 | tf_op jit(solution)/shard_map/all_gather | solution.py:362
  10.0 201.4 %reduce-scatter.2.cloned.1.call-start = ((), (), s32[]{:S(2)}) async-start(), calls=%async_computation.5 | async-start | bytes 8110080 | tf_op jit(solution)/shard_map/reduce_scatter | solution.py:459
  18.1 39.8 %copy-start.3 = (f32[640,128]{1,0:T(8,128)}, f32[640,128]{1,0:T(8,128)S(1)}, u32[]{:S(2)}) copy-start(f32[640,128]{1,0:T(8,128)S(1)} %get-tuple-element.81.high_ref) | copy-start | bytes 983044
  18.1 40.6 %copy-start.4 = (f32[640,128]{1,0:T(8,128)}, f32[640,128]{1,0:T(8,128)S(1)}, u32[]{:S(2)}) copy-start(f32[640,128]{1,0:T(8,128)S(1)} %get-tuple-element.82.low_ref) | copy-start | bytes 983044
  18.4 40.9 %copy-start.2 = (f32[640,128]{1,0:T(8,128)}, f32[640,128]{1,0:T(8,128)S(1)}, u32[]{:S(2)}) copy-start(f32[640,128]{1,0:T(8,128)S(1)} %pad_maximum_fusion.1.cos_ref) | copy-start | bytes 983044
  50.7 18.2 %collective-permute-start.1 = (bf16[2,64,1536]{2,1,0:T(8,128)(2,1)S(1)}, bf16[2,64,1536]{2,1,0:T(8,128)(2,1)S(1)}, u32[]{:S(2)}, u32[]{:S(2)}) collective-permute-start(bf16[2,64,1536]{2,1,0:T(8,128)(2,1)S(1)} %get-tuple-element.73), channel_id=1, source_target_pairs={{4,0},{8,4},{12,8},{16,12},{20,16},{24,20},{28,24},{5,1},{9,5},{13... | collective-permute-start | bytes 1179656 | tf_op jit(solution)/shard_map/ppermute | solution.py:408
  52.0 20.1 %collective-permute-start = (bf16[2,64,1536]{2,1,0:T(8,128)(2,1)S(1)}, bf16[2,64,1536]{2,1,0:T(8,128)(2,1)S(1)}, u32[]{:S(2)}, u32[]{:S(2)}) collective-permute-start(bf16[2,64,1536]{2,1,0:T(8,128)(2,1)S(1)} %get-tuple-element.74), channel_id=1, source_target_pairs={{0,4},{4,8},{8,12},{12,16},{16,20},{20,24},{24,28},{1,5},{5,9},{9,... | collective-permute-start | bytes 1179656 | tf_op jit(solution)/shard_map/ppermute | solution.py:407
  68.9 3.3 copy-start
  72.2 0.7 copy-start.1
  151.5 59.9 %copy-start.8 = (f32[1,768]{1,0:T(1,128)S(1)}, f32[1,768]{1,0:T(1,128)}, u32[]{:S(2)}) copy-start(f32[1,768]{1,0:T(1,128)} %get-tuple-element.60) | copy-start | bytes 9220
  151.6 162.9 %all-reduce.4.cloned.1.call-start = ((), (), s32[]{:S(2)}) async-start(), calls=%async_computation.6 | async-start | bytes 3244032 | tf_op jit(solution)/shard_map/psum | solution.py:459
  211.4 183.4 %all-reduce.6.cloned.1.call-start = ((), (), s32[]{:S(2)}) async-start(), calls=%async_computation.7 | async-start | bytes 1966080 | tf_op jit(solution)/shard_map/psum | solution.py:527
  225.4 24.4 %collective-permute-start.4 = (bf16[1,2,64,768]{3,2,1,0:T(8,128)(2,1)}, bf16[1,2,64,768]{3,2,1,0:T(8,128)(2,1)S(1)}, u32[]{:S(2)}, u32[]{:S(2)}) collective-permute-start(bf16[1,2,64,768]{3,2,1,0:T(8,128)(2,1)} %get-tuple-element.52), channel_id=1, source_target_pairs={{0,4},{4,8},{8,12},{12,16},{16,20},{20,24},{24,28},{1,5},{5,9},{9,... | collective-permute-start | bytes 589832 | tf_op jit(solution)/shard_map/ppermute | solution.py:515
  228.8 21.1 %collective-permute-start.5 = (bf16[1,2,64,768]{3,2,1,0:T(8,128)(2,1)}, bf16[1,2,64,768]{3,2,1,0:T(8,128)(2,1)S(1)}, u32[]{:S(2)}, u32[]{:S(2)}) collective-permute-start(bf16[1,2,64,768]{3,2,1,0:T(8,128)(2,1)} %get-tuple-element.53), channel_id=1, source_target_pairs={{4,0},{8,4},{12,8},{16,12},{20,16},{24,20},{28,24},{5,1},{9,5},{13... | collective-permute-start | bytes 589832 | tf_op jit(solution)/shard_map/ppermute | solution.py:515
  244.0 16.1 %collective-permute-start.2 = (bf16[1,2,64,768]{3,2,1,0:T(8,128)(2,1)}, bf16[1,2,64,768]{3,2,1,0:T(8,128)(2,1)S(1)}, u32[]{:S(2)}, u32[]{:S(2)}) collective-permute-start(bf16[1,2,64,768]{3,2,1,0:T(8,128)(2,1)} %get-tuple-element.47), channel_id=1, source_target_pairs={{0,4},{4,8},{8,12},{12,16},{16,20},{20,24},{24,28},{1,5},{5,9},{9,... | collective-permute-start | bytes 589832 | tf_op jit(solution)/shard_map/ppermute | solution.py:515
  248.6 11.5 %collective-permute-start.3 = (bf16[1,2,64,768]{3,2,1,0:T(8,128)(2,1)}, bf16[1,2,64,768]{3,2,1,0:T(8,128)(2,1)S(1)}, u32[]{:S(2)}, u32[]{:S(2)}) collective-permute-start(bf16[1,2,64,768]{3,2,1,0:T(8,128)(2,1)} %get-tuple-element.48), channel_id=1, source_target_pairs={{4,0},{8,4},{12,8},{16,12},{20,16},{24,20},{28,24},{5,1},{9,5},{13... | collective-permute-start | bytes 589832 | tf_op jit(solution)/shard_map/ppermute | solution.py:515
  249.9 0.7 copy-start.10
  260.1 0.7 copy-start.7
  314.4 2.1 copy-start.5
  (2 other events, 1.4 us)
Sparse Core Ops, SparseCore 0:
  9.6 33.4 all-gather.5
  44.6 17.4 all-gather.7
  63.7 20.7 all-gather.11
  85.9 30.7 all-gather.9
  151.7 59.6 reduce-scatter.1
  215.2 99.1 all-reduce.3
  318.3 76.4 all-reduce.5

commit v4 on v3

--- a/solution.py
+++ b/solution.py
@@ -260,24 +260,122 @@
         dw_ref[:, at:] = jnp.zeros((dw_ref.shape[0], dw_ref.shape[1] - at, width), bf16)
 
 
-def reduce_kernel(pack_ref, out_ref, mine, got, total, far, ls, cs, cr, xs, xr):
+def gather_plan(shapes):
+    plan = []
+    for a, (n, columns) in enumerate(shapes):
+        half = n // 2
+        parts = 2 if half % 32 == 0 and n * columns > 300000 else 1
+        plan += [(a, k * half // parts, half // parts) for k in range(parts)]
+    return plan
+
+
+def gather_kernel(*refs):
+    many = (len(refs) - 7) // 2
+    ins, outs = refs[:many], refs[many : 2 * many]
+    own_sem, xs, xr, ys, yr, cs, cr = refs[2 * many :]
+    plan = gather_plan([r.shape for r in ins])
+    count = len(plan)
+    seq, me = lax.axis_index("seq"), lax.axis_index("fsdp")
+    across = lax.rem(me + 2, 4)
+    core = me + 1 - 2 * lax.rem(me, 2)
+    side = lax.rem(seq, 2)
+    beside = {"seq": seq + 1 - 2 * side}
+    barrier = pltpu.get_barrier_semaphore()
+    for target in ({"fsdp": across}, {"fsdp": core}, beside):
+        pl.semaphore_signal(barrier, inc=1, device_id=target, device_id_type=pl.DeviceIdType.MESH)
+    pl.semaphore_wait(barrier, 3)
+
+    def send(src, dst, ss, rs, target):
+        copy = pltpu.make_async_remote_copy(
+            src_ref=src, dst_ref=dst, send_sem=ss, recv_sem=rs,
+            device_id=target, device_id_type=pl.DeviceIdType.MESH,
+        )
+        copy.start()
+        return copy
+
+    def place(a, owner, which, off, n):
+        rows = ins[a].shape[0]
+        at = owner * rows + which * (rows // 2) + off
+        return outs[a].at[pl.ds(pl.multiple_of(at, 16), n)]
+
+    def first_hop(k):
+        a, off, n = plan[k]
+        half = ins[a].shape[0] // 2
+        src = ins[a].at[pl.ds(pl.multiple_of(side * half + off, 16), n)]
+        return send(src, place(a, me, side, off, n), xs.at[k], xr.at[k], {"fsdp": across})
+
+    hops = [first_hop(k) for k in range(count)]
+    local, pairs = [], []
+    for a in range(many):
+        n = ins[a].shape[0]
+        spot = outs[a].at[pl.ds(pl.multiple_of(me * n, 16), n)]
+        copy = pltpu.make_async_copy(ins[a], spot, own_sem.at[a])
+        copy.start()
+        local.append(copy)
+        pairs.append(send(ins[a], spot, cs.at[a], cr.at[a], {"fsdp": core}))
+    seconds = []
+
+    def relay(k):
+        a, off, n = plan[k]
+        seconds[k].wait_recv()
+        spot = place(a, across, 1 - side, off, n)
+        i = many + count + k
+        pairs.append(send(spot, spot, cs.at[i], cr.at[i], {"fsdp": core}))
+
+    for k in range(count):
+        a, off, n = plan[k]
+        hops[k].wait_recv()
+        spot = place(a, across, side, off, n)
+        seconds.append(send(spot, spot, ys.at[k], yr.at[k], beside))
+        pairs.append(send(spot, spot, cs.at[many + k], cr.at[many + k], {"fsdp": core}))
+        if k:
+            relay(k - 1)
+    relay(count - 1)
+    for copy in local:
+        copy.wait()
+    for copy in hops + seconds:
+        copy.wait_send()
+    for copy in pairs:
+        copy.wait_send()
+        copy.wait_recv()
+
+
+def gather_weights(*weights):
+    count, many = len(gather_plan([w.shape for w in weights])), len(weights)
+    sems = lambda n: pltpu.SemaphoreType.DMA((n,))
+    return pl.pallas_call(
+        gather_kernel,
+        in_specs=[pl.BlockSpec(memory_space=pl.ANY)] * many,
+        out_specs=[pl.BlockSpec(memory_space=pl.ANY)] * many,
+        out_shape=[sds((4 * w.shape[0], w.shape[1]), w.dtype) for w in weights],
+        scratch_shapes=[sems(many)] + [sems(count)] * 4 + [sems(many + 2 * count)] * 2,
+        compiler_params=pltpu.CompilerParams(collective_id=0, has_side_effects=True),
+        cost_estimate=pl.CostEstimate(flops=0, bytes_accessed=2**26, transcendentals=0),
+        name="gather_weights",
+    )(*weights)
+
+
+def reduce_kernel(seq_size, pack_ref, out_ref, mine, got, total, far, work, back, done, ls, cs, cr, xs, xr, ss, sr, gs, gr):
     me = lax.axis_index("fsdp")
     across = lax.rem(me + 2, 4)
     core = me + 1 - 2 * lax.rem(me, 2)
     barrier = pltpu.get_barrier_semaphore()
-    for target in (across, core):
-        pl.semaphore_signal(
-            barrier, inc=1, device_id={"fsdp": target}, device_id_type=pl.DeviceIdType.MESH
-        )
-    pl.semaphore_wait(barrier, 2)
+    seq = lax.axis_index("seq")
+    hops_count = seq_size.bit_length() - 1
+    bits = [lax.rem(lax.div(seq, 2**b), 2) for b in range(hops_count)]
+    partners = [{"seq": seq + (1 - 2 * bits[b]) * 2**b} for b in range(hops_count)]
+    for target in [{"fsdp": across}, {"fsdp": core}] + partners:
+        pl.semaphore_signal(barrier, inc=1, device_id=target, device_id_type=pl.DeviceIdType.MESH)
+    pl.semaphore_wait(barrier, 2 + hops_count)
     parts = xs.shape[0]
+    lanes = out_ref.shape[1] // 2
     n = out_ref.shape[0] // parts
     rows = [pl.ds(k * n, n) for k in range(parts)]
 
     def send(src, dst, ss, rs, target):
         copy = pltpu.make_async_remote_copy(
             src_ref=src, dst_ref=dst, send_sem=ss, recv_sem=rs,
-            device_id={"fsdp": target}, device_id_type=pl.DeviceIdType.MESH,
+            device_id=target, device_id_type=pl.DeviceIdType.MESH,
         )
         copy.start()
         return copy
@@ -286,7 +384,7 @@
     for slot, theirs, ours in ((0, lax.rem(core + 2, 4), across), (1, core, me)):
         for k in range(parts):
             i = slot * parts + k
-            pairs[slot, k] = send(pack_ref.at[theirs, rows[k]], got.at[slot, rows[k]], cs.at[i], cr.at[i], core)
+            pairs[slot, k] = send(pack_ref.at[theirs, rows[k]], got.at[slot, rows[k]], cs.at[i], cr.at[i], {"fsdp": core})
             copy = pltpu.make_async_copy(pack_ref.at[ours, rows[k]], mine.at[slot, rows[k]], ls.at[i])
             copy.start()
             locals_[slot, k] = copy
@@ -295,32 +393,76 @@
         locals_[0, k].wait()
         pairs[0, k].wait_recv()
         total[rows[k]] = (mine[0, rows[k]].astype(f32) + got[0, rows[k]].astype(f32)).astype(bf16)
-        hops.append(send(total.at[rows[k]], far.at[rows[k]], xs.at[k], xr.at[k], across))
+        hops.append(send(total.at[rows[k]], far.at[rows[k]], xs.at[k], xr.at[k], {"fsdp": across}))
     for k in range(parts):
         locals_[1, k].wait()
         pairs[1, k].wait_recv()
         hops[k].wait_recv()
-        out_ref[rows[k]] = (
+        share = (
             mine[1, rows[k]].astype(f32) + got[1, rows[k]].astype(f32) + far[rows[k]].astype(f32)
         ).astype(bf16)
-    for copy in list(pairs.values()) + hops:
+        work[0, rows[k]] = share[:, :lanes]
+        work[1, rows[k]] = share[:, lanes:]
+    orders = [list(range(hops_count)), list(range(1, hops_count)) + [0]]
+    low = [0, 0]
+    size = out_ref.shape[0]
+    offset = 0
+    copies = []
+    span = lambda at, n: pl.ds(pl.multiple_of(at, 16), n)
+    for t in range(hops_count):
+        size //= 2
+        started = []
+        for h in range(2):
+            b = orders[h][t]
+            spot = back.at[h, pl.ds(offset, size)]
+            gone = work.at[h, span(low[h] + (1 - bits[b]) * size, size)]
+            i = 2 * t + h
+            started.append(send(gone, spot, ss.at[i], sr.at[i], partners[b]))
+            low[h] = low[h] + bits[b] * size
+        for h in range(2):
+            started[h].wait_recv()
+            here = span(low[h], size)
+            value = work[h, here].astype(f32) + back[h, pl.ds(offset, size)].astype(f32)
+            if t < hops_count - 1:
+                work[h, here] = value.astype(bf16)
+            else:
+                done[h, here] = value.astype(bf16)
+        copies += started
+        offset += size
+    for t in reversed(range(hops_count)):
+        started = []
+        for h in range(2):
+            b = orders[h][t]
+            here = done.at[h, span(low[h], size)]
+            i = 2 * t + h
+            started.append(send(here, here, gs.at[i], gr.at[i], partners[b]))
+        for h in range(2):
+            started[h].wait_recv()
+            low[h] = low[h] - bits[orders[h][t]] * size
+        copies += started
+        size *= 2
+    for copy in list(pairs.values()) + hops + copies:
         copy.wait_send()
-
-
-def reduce_fsdp(x, parts):
+    out_ref[:, :lanes] = done[0]
+    out_ref[:, lanes:] = done[1]
+
+
+def reduce_all(x, parts, seq_size):
     shares, n, width = x.shape
     sems = lambda m: pltpu.SemaphoreType.DMA((m,))
     vmem = lambda *shape: pltpu.VMEM(shape, bf16)
+    hops = 2 * (seq_size.bit_length() - 1)
     return pl.pallas_call(
-        reduce_kernel,
+        functools.partial(reduce_kernel, seq_size),
         in_specs=[pl.BlockSpec(memory_space=pl.ANY)],
         out_specs=pl.BlockSpec(memory_space=pltpu.VMEM),
         out_shape=sds((n, width), bf16),
         scratch_shapes=[vmem(2, n, width), vmem(2, n, width), vmem(n, width), vmem(n, width)]
-        + [sems(2 * parts)] * 3 + [sems(parts)] * 2,
+        + [vmem(2, n, width // 2)] * 3
+        + [sems(2 * parts)] * 3 + [sems(parts)] * 2 + [sems(hops)] * 4,
         compiler_params=pltpu.CompilerParams(collective_id=1, has_side_effects=True, vmem_limit_bytes=LIMIT),
         cost_estimate=pl.CostEstimate(flops=0, bytes_accessed=2**26, transcendentals=0),
-        name="reduce_fsdp",
+        name="reduce_all",
     )(x)
 
 
@@ -358,9 +500,12 @@
     qkv_rows = padded_rows(3 * qkv_weight.shape[0] + 16, seq_size)
     forward = [(i, i + 1) for i in range(seq_size - 1)]
     backward = [(j, i) for i, j in forward]
-    gains = lax.all_gather(jnp.stack([norm_gain_attn, norm_gain_mlp]), "fsdp", axis=1, tiled=True)
     gather = lambda x: lax.all_gather(x, "fsdp", axis=0, tiled=True)
-    w_qkv = gather(qkv_weight)
+    gains = jnp.stack([norm_gain_attn, norm_gain_mlp])
+    own_gains = gains.shape[1]
+    gains = jnp.pad(gains, ((0, 30), (0, -own_gains % PAIR)))
+    w_qkv, gains = gather_weights(qkv_weight, gains)
+    gains = gains.reshape(shares, 32, -1)[:, :2, :own_gains].swapaxes(0, 1).reshape(2, width)
     w_attn = gather(attn_out_weight)
     w_in = gather(mlp_in_weight)
     w_out = gather(mlp_out_weight)
@@ -523,8 +668,7 @@
     both = both.reshape(2, shares, width // shares).swapaxes(0, 1)
     both = jnp.pad(both, ((0, 0), (0, 0), (0, width - width // shares)))
     d_wqkv = lax.dynamic_update_slice(d_wqkv, both, (0, gains_at, 0))
-    qkv_share, mlp_sum = lax.optimization_barrier((reduce_fsdp(d_wqkv, 4), mlp_sum))
-    qkv_sum = lax.psum(qkv_share, "seq")
+    qkv_sum = reduce_all(d_wqkv, 4, seq_size)
     s_wqkv = unpack(qkv_sum, (qkv_weight.shape,))[0]
     s_gains = qkv_sum[gains_at : gains_at + 2, : width // shares].astype(f32)
     s_win, s_wo, s_wout = unpack(mlp_sum, mlp_shapes)

time: 406 us -> 307 us (0.76)
  waiting for transfers between devices: 200 us -> 17.4 us
  Pallas kernels: 144 us -> 228 us
  blocking collectives: 5.98 us -> 0 us
    pallas_call x1 -> x2, Pallas kernels: 26.9 us -> 110 us  [the longest x1 78.1 us: reduce_all(): pl.pallas_call(functools.partial(reduce_kernel, seq_size), in_specs=[pl.B...]
    psum x1 -> x0, waiting for transfers between devices: 76 us -> none  [shards(): qkv_sum = lax.psum(qkv_share, 'seq')]
    reduce_scatter x1, waiting for transfers between devices: 59.8 us -> 9.25 us  [shards(): lax.psum_scatter(d_mlp, 'fsdp', scatter_dimension=0, tiled=True)[0]]
    all_gather x4 -> x3, waiting for transfers between devices: 44.1 us -> 0.05 us  [shards(): gather = lambda x: lax.all_gather(x, 'fsdp', axis=0, tiled=True)]
    psum x1, waiting for transfers between devices: 14.6 us -> 4.35 us  [shards(): lax.psum(lax.psum_scatter(d_mlp, 'fsdp', scatter_dimension=0, tiled=True)...]
    all_gather x1 -> x0, blocking collectives: 5.98 us -> none  [shards(): lax.all_gather(jnp.stack([norm_gain_attn, norm_gain_mlp]), 'fsdp', axis=1...]
  transfers between devices with their start and end apart: 13 -> 11, of which waited for: 6 -> 3; matrix products, arithmetic and copies ran while one was open for 4% -> 7% of each run, Pallas kernels for 27% -> 63%
where the time goes in v4:
time: 307 us; the launch traced here: 306 us
  Pallas kernels  228 us (74%)
  starting transfers between devices  18.2 us (6%)
  waiting for transfers between devices  17.4 us (6%)
  local copies, waits for them, and re-layouts  15.3 us (5%)
  between operations  14.1 us (5%)
  other arithmetic  13.2 us (4%)
    pallas_call x1, Pallas kernels, reduce_all(): pl.pallas_call(functools.partial(reduce_kernel, seq_size), in_specs=[pl.B...  78.1 us
    pallas_call x1, Pallas kernels, shards(): pl.pallas_call(functools.partial(mlp_kernel, rows // wide), grid=(rows //...  35 us
    pallas_call x1, Pallas kernels, gather_weights(): pl.pallas_call(gather_kernel, in_specs=[pl.BlockSpec(memory_space=pl.ANY)...  31.7 us
    pallas_call x2, Pallas kernels, attend_back(): pl.pallas_call(attend_back_kernel, grid=(pairs,), in_specs=[at(piece), at...  27.9 us
    pallas_call x1, Pallas kernels, shards(): pl.pallas_call(attend_kernel, grid=(seqs, pairs), in_specs=[lanes(piece)]...  21.6 us
    pallas_call x2, Pallas kernels, qkv_back(): pl.pallas_call(functools.partial(qkv_back_kernel, len(prior), len(kept),...  20.2 us
    pallas_call x2, Pallas kernels, project(): pl.pallas_call(qkv_kernel, grid=(count // tile,), in_specs=[row_spec(widt...  13.4 us
    ppermute x2, starting transfers between devices, shards(): lax.ppermute(dr, 'seq', forward)  9.56 us
  transfers between devices with their start and end apart: 11, of which 3 were waited for; matrix products, arithmetic and copies ran while one was open for 7% of the time, Pallas kernels for 63%

profile of v4, /device:TPU:0, one launch (start us, length us, event | category | flops | bytes accessed | tf_op | source)
XLA Modules:
  0.0 306.0 jit_solution(6426305280350994076)
XLA Ops:
  11.4 31.7 %gather_weights.1 = (bf16[768,2304]{1,0:T(8,128)(2,1)}, bf16[128,256]{1,0:T(8,128)(2,1)}) custom-call(bf16[192,2304]{1,0:T(8,128)(2,1)} %refs_0_.1, bf16[32,256]{1,0:T(8,128)(2,1)} %fusion.9.refs_1_), custom_call_target="tpu_custom_call" | custom-call | bytes 67108864 | tf_op jit(solution)/shard_map/gather_weights/pallas_call | solution.py:346
  50.7 4.5 %qkv_forward.3 = (bf16[256,768]{1,0:T(8,128)(2,1)}, bf16[256,1536]{1,0:T(8,128)(2,1)}) custom-call(bf16[256,768]{1,0:T(8,128)(2,1)} %bitcast.38, f32[1,768]{1,0:T(1,128)} %reshape.205.gain_ref, bf16[768,2304]{1,0:T(8,128)(2,1)} %get-tuple-element.37.w_ref, f32[256,128]{1,0:T(8,128)} %bitcast.42, f32[256,128]{1,0:T(8,128)} %bitcast.41, f32[256,128]{1,0:T(8,128)} %bitcast.40), custom_call_target="tpu_custom_call" | custom-call | flops 905969664 | bytes 2359296 | tf_op jit(solution)/shard_map/qkv_forward/pallas_call | solution.py:535
  56.3 1.3 collective-permute-start.1
  57.6 4.6 %collective-permute-start = (bf16[2,64,1536]{2,1,0:T(8,128)(2,1)S(1)}, bf16[2,64,1536]{2,1,0:T(8,128)(2,1)S(1)}, u32[]{:S(2)}, u32[]{:S(2)}) collective-permute-start(bf16[2,64,1536]{2,1,0:T(8,128)(2,1)S(1)} %get-tuple-element.74), channel_id=1, source_target_pairs={{0,4},{4,8},{8,12},{12,16},{16,20},{20,24},{24,28},{1,5},{5,9},{9,... | collective-permute-start | bytes 1179656 | tf_op jit(solution)/shard_map/ppermute | solution.py:552
  62.4 1.3 fusion.2.bias_ref
  66.5 9.0 %qkv_forward.2 = (bf16[1024,768]{1,0:T(8,128)(2,1)}, bf16[1024,1536]{1,0:T(8,128)(2,1)}) custom-call(bf16[1024,768]{1,0:T(8,128)(2,1)} %bitcast.35, f32[1,768]{1,0:T(1,128)} %reshape.205.gain_ref, bf16[768,2304]{1,0:T(8,128)(2,1)} %get-tuple-element.37.w_ref, f32[512,128]{1,0:T(8,128)} %slice.121.cos_ref, f32[512,128]{1,0:T(8,128)} %slice.122.low_ref, ...), custom_call_target="tpu_custom_call" | custom-call | flops 3623878656 | bytes 9437184 | tf_op jit(solution)/shard_map/qkv_forward/pallas_call | solution.py:535
  75.5 1.6 collective-permute-done.lk_ref.lv_ref
  77.9 21.6 %attend_forward.1 = (bf16[2,512,768]{2,1,0:T(8,128)(2,1)}, bf16[2,6,4,256,256]{4,3,2,1,0:T(8,128)(2,1)}) custom-call(bf16[2,512,768]{2,1,0:T(8,128)(2,1)} %bitcast.28, bf16[2,512,1536]{2,1,0:T(8,128)(2,1)} %bitcast.22, bf16[2,512,1536]{2,1,0:T(8,128)(2,1)} %bitcast.23, bf16[2,64,1536]{2,1,0:T(8,128)(2,1)} %copy-done.1, bf16[2,64,1536]{2,1,0:T(8,128)(2,1)} %copy-done.1, ...), custom_call_target="tpu_custom_call" | custom-call | flops 3221225472 | bytes 12582912 | tf_op jit(solution)/shard_map/attend_forward/pallas_call | solution.py:571
  99.5 35.0 %mlp_both_ways.1 = (bf16[1024,768]{1,0:T(8,128)(2,1)}, f32[1024,768]{1,0:T(8,128)}, bf16[1024,768]{1,0:T(8,128)(2,1)}, bf16[4,1056,768]{2,1,0:T(8,128)(2,1)}, f32[1,768]{1,0:T(1,128)}) custom-call(bf16[1024,768]{1,0:T(8,128)(2,1)} %bitcast.36, bf16[1024,768]{1,0:T(8,128)(2,1)} %bitcast.49, bf16[1024,768]{1,0:T(8,128)(2,1)} %bitcast.47, ...), custom_call_target="tpu_custom_call" | custom-call | flops 19931332608 | bytes 41943040 | tf_op jit(solution)/shard_map/mlp_both_ways/pallas_call | solution.py:585
  135.3 13.8 %attend_backward.3 = (bf16[1,512,768]{2,1,0:T(8,128)(2,1)}, bf16[1,512,768]{2,1,0:T(8,128)(2,1)}, bf16[1,512,768]{2,1,0:T(8,128)(2,1)}, bf16[1,2,64,768]{3,2,1,0:T(8,128)(2,1)}, bf16[1,2,64,768]{3,2,1,0:T(8,128)(2,1)}) custom-call(bf16[2,512,768]{2,1,0:T(8,128)(2,1)} %bitcast.29, bf16[2,512,1536]{2,1,0:T(8,128)(2,1)} %bitcast.24, ...), custom_call_target="tpu_custom_call" | custom-call | flops 3221225472 | bytes 9437184 | tf_op jit(solution)/shard_map/attend_backward/pallas_call | solution.py:619
  149.1 4.4 %collective-permute-start.4 = (bf16[1,2,64,768]{3,2,1,0:T(8,128)(2,1)}, bf16[1,2,64,768]{3,2,1,0:T(8,128)(2,1)S(1)}, u32[]{:S(2)}, u32[]{:S(2)}) collective-permute-start(bf16[1,2,64,768]{3,2,1,0:T(8,128)(2,1)} %get-tuple-element.54), channel_id=1, source_target_pairs={{0,4},{4,8},{8,12},{12,16},{16,20},{20,24},{24,28},{1,5},{5,9},{9,... | collective-permute-start | bytes 589832 | tf_op jit(solution)/shard_map/ppermute | solution.py:660
  153.6 1.3 collective-permute-start.5
  154.9 14.1 %attend_backward.2 = (bf16[1,512,768]{2,1,0:T(8,128)(2,1)}, bf16[1,512,768]{2,1,0:T(8,128)(2,1)}, bf16[1,512,768]{2,1,0:T(8,128)(2,1)}, bf16[1,2,64,768]{3,2,1,0:T(8,128)(2,1)}, bf16[1,2,64,768]{3,2,1,0:T(8,128)(2,1)}) custom-call(bf16[2,512,768]{2,1,0:T(8,128)(2,1)} %bitcast.30, bf16[2,512,1536]{2,1,0:T(8,128)(2,1)} %bitcast.26, ...), custom_call_target="tpu_custom_call" | custom-call | flops 3221225472 | bytes 9437184 | tf_op jit(solution)/shard_map/attend_backward/pallas_call | solution.py:619
  168.9 5.2 %collective-permute-start.2 = (bf16[1,2,64,768]{3,2,1,0:T(8,128)(2,1)}, bf16[1,2,64,768]{3,2,1,0:T(8,128)(2,1)S(1)}, u32[]{:S(2)}, u32[]{:S(2)}) collective-permute-start(bf16[1,2,64,768]{3,2,1,0:T(8,128)(2,1)} %get-tuple-element.49), channel_id=1, source_target_pairs={{0,4},{4,8},{8,12},{12,16},{16,20},{20,24},{24,28},{1,5},{5,9},{9,... | collective-permute-start | bytes 589832 | tf_op jit(solution)/shard_map/ppermute | solution.py:660
  174.1 1.3 collective-permute-start.3
  176.2 9.7 %qkv_backward.2 = (f32[2,512,768]{2,1,0:T(8,128)}, bf16[768,2304]{1,0:T(8,128)(2,1)}, f32[1,768]{1,0:T(1,128)}) custom-call(bf16[2,512,768]{2,1,0:T(8,128)(2,1)} %tok_ref.3, f32[2,512,768]{2,1,0:T(8,128)} %bitcast.33, bf16[1,512,768]{2,1,0:T(8,128)(2,1)} %get-tuple-element.51.dq_ref, bf16[1,512,768]{2,1,0:T(8,128)(2,1)} %get-tuple-element.52.dk_ref, ...), custom_call_target="tpu_custom_call" | custom-call | flops 3623878656 | bytes 7864320 | tf_op jit(solution)/shard_map/qkv_backward/pallas_call | solution.py:643
  185.8 9.2 %reduce-scatter.2.cloned.1.call-done = bf16[1,1056,768]{2,1,0:T(8,128)(2,1)} async-done(((bf16[4,1056,768]{2,1,0:T(8,128)(2,1)}), bf16[1,1056,768]{2,1,0:T(8,128)(2,1)}) %reduce-scatter.2.cloned.1.call-update) | async-done | bytes 1622032 | tf_op jit(solution)/shard_map/reduce_scatter | solution.py:604
  195.8 10.6 %qkv_backward.3 = (f32[2,512,768]{2,1,0:T(8,128)}, bf16[4,640,768]{2,1,0:T(8,128)(2,1)}, f32[1,768]{1,0:T(1,128)}) custom-call(bf16[2,512,768]{2,1,0:T(8,128)(2,1)} %tok_ref.3, f32[2,512,768]{2,1,0:T(8,128)} %bitcast.34, bf16[1,512,768]{2,1,0:T(8,128)(2,1)} %get-tuple-element.46.dq_ref, ...), custom_call_target="tpu_custom_call", output_to_operand_aliasing={{0}: (11, {})} | custom-call | flops 3623878656 | bytes 7864320 | tf_op jit(solution)/shard_map/qkv_backward/pallas_call | solution.py:643
  207.8 78.1 %reduce_all.1 = bf16[640,768]{1,0:T(8,128)(2,1)} custom-call(bf16[4,640,768]{2,1,0:T(8,128)(2,1)} %pad_dynamic-update-slice_fusion.pack_ref), custom_call_target="tpu_custom_call" | custom-call | bytes 67108864 | tf_op jit(solution)/shard_map/reduce_all/pallas_call | solution.py:455
  288.4 1.3 maximum_convert_fusion
  289.7 4.4 %all-reduce.4.cloned.1.call-done = bf16[1056,768]{1,0:T(8,128)(2,1)} async-done(((bf16[1056,768]{1,0:T(8,128)(2,1)}), bf16[1056,768]{1,0:T(8,128)(2,1)}) %all-reduce.4.cloned.1.call-update) | async-done | bytes 1622032 | tf_op jit(solution)/shard_map/psum | solution.py:604
  294.0 2.1 fusion.12
  296.2 1.3 maximum_convert_fusion.1
  297.5 2.0 slice_convert_fusion
  (79 shorter events, 22.8 us)
Async XLA Ops:
  7.2 92.3 %all-gather.4.cloned.1.call-start = ((), (), s32[]{:S(2)}) async-start(), calls=%async_computation.1 | async-start | bytes 1474560 | tf_op jit(solution)/shard_map/all_gather | solution.py:503
  7.9 91.6 %all-gather.8.cloned.1.call-start = ((), (), s32[]{:S(2)}) async-start(), calls=%async_computation.3 | async-start | bytes 2211840 | tf_op jit(solution)/shard_map/all_gather | solution.py:503
  8.7 90.9 %all-gather.6.cloned.1.call-start = ((), (), s32[]{:S(2)}) async-start(), calls=%async_computation.2 | async-start | bytes 4423680 | tf_op jit(solution)/shard_map/all_gather | solution.py:503
  9.4 185.7 %reduce-scatter.2.cloned.1.call-start = ((), (), s32[]{:S(2)}) async-start(), calls=%async_computation.4 | async-start | bytes 8110080 | tf_op jit(solution)/shard_map/reduce_scatter | solution.py:604
  46.3 17.3 %copy-start.3 = (f32[640,128]{1,0:T(8,128)}, f32[640,128]{1,0:T(8,128)S(1)}, u32[]{:S(2)}) copy-start(f32[640,128]{1,0:T(8,128)S(1)} %get-tuple-element.81.high_ref) | copy-start | bytes 983044
  46.3 18.0 %copy-start.4 = (f32[640,128]{1,0:T(8,128)}, f32[640,128]{1,0:T(8,128)S(1)}, u32[]{:S(2)}) copy-start(f32[640,128]{1,0:T(8,128)S(1)} %get-tuple-element.82.low_ref) | copy-start | bytes 983044
  46.7 18.4 %copy-start.2 = (f32[640,128]{1,0:T(8,128)}, f32[640,128]{1,0:T(8,128)S(1)}, u32[]{:S(2)}) copy-start(f32[640,128]{1,0:T(8,128)S(1)} %pad_maximum_fusion.1.cos_ref) | copy-start | bytes 983044
  56.3 19.1 %collective-permute-start.1 = (bf16[2,64,1536]{2,1,0:T(8,128)(2,1)S(1)}, bf16[2,64,1536]{2,1,0:T(8,128)(2,1)S(1)}, u32[]{:S(2)}, u32[]{:S(2)}) collective-permute-start(bf16[2,64,1536]{2,1,0:T(8,128)(2,1)S(1)} %get-tuple-element.73), channel_id=1, source_target_pairs={{4,0},{8,4},{12,8},{16,12},{20,16},{24,20},{28,24},{5,1},{9,5},{13... | collective-permute-start | bytes 1179656 | tf_op jit(solution)/shard_map/ppermute | solution.py:553
  57.6 19.5 %collective-permute-start = (bf16[2,64,1536]{2,1,0:T(8,128)(2,1)S(1)}, bf16[2,64,1536]{2,1,0:T(8,128)(2,1)S(1)}, u32[]{:S(2)}, u32[]{:S(2)}) collective-permute-start(bf16[2,64,1536]{2,1,0:T(8,128)(2,1)S(1)} %get-tuple-element.74), channel_id=1, source_target_pairs={{0,4},{4,8},{8,12},{12,16},{16,20},{20,24},{24,28},{1,5},{5,9},{9,... | collective-permute-start | bytes 1179656 | tf_op jit(solution)/shard_map/ppermute | solution.py:552
  75.5 1.7 copy-start
  77.1 0.7 copy-start.1
  134.5 0.7 copy-start.7
  134.6 159.5 %all-reduce.4.cloned.1.call-start = ((), (), s32[]{:S(2)}) async-start(), calls=%async_computation.5 | async-start | bytes 3244032 | tf_op jit(solution)/shard_map/psum | solution.py:604
  149.1 26.3 %collective-permute-start.4 = (bf16[1,2,64,768]{3,2,1,0:T(8,128)(2,1)}, bf16[1,2,64,768]{3,2,1,0:T(8,128)(2,1)S(1)}, u32[]{:S(2)}, u32[]{:S(2)}) collective-permute-start(bf16[1,2,64,768]{3,2,1,0:T(8,128)(2,1)} %get-tuple-element.54), channel_id=1, source_target_pairs={{0,4},{4,8},{8,12},{12,16},{16,20},{20,24},{24,28},{1,5},{5,9},{9,... | collective-permute-start | bytes 589832 | tf_op jit(solution)/shard_map/ppermute | solution.py:660
  153.6 21.9 %collective-permute-start.5 = (bf16[1,2,64,768]{3,2,1,0:T(8,128)(2,1)}, bf16[1,2,64,768]{3,2,1,0:T(8,128)(2,1)S(1)}, u32[]{:S(2)}, u32[]{:S(2)}) collective-permute-start(bf16[1,2,64,768]{3,2,1,0:T(8,128)(2,1)} %get-tuple-element.55), channel_id=1, source_target_pairs={{4,0},{8,4},{12,8},{16,12},{20,16},{24,20},{28,24},{5,1},{9,5},{13... | collective-permute-start | bytes 589832 | tf_op jit(solution)/shard_map/ppermute | solution.py:660
  168.9 26.1 %collective-permute-start.2 = (bf16[1,2,64,768]{3,2,1,0:T(8,128)(2,1)}, bf16[1,2,64,768]{3,2,1,0:T(8,128)(2,1)S(1)}, u32[]{:S(2)}, u32[]{:S(2)}) collective-permute-start(bf16[1,2,64,768]{3,2,1,0:T(8,128)(2,1)} %get-tuple-element.49), channel_id=1, source_target_pairs={{0,4},{4,8},{8,12},{12,16},{16,20},{20,24},{24,28},{1,5},{5,9},{9,... | collective-permute-start | bytes 589832 | tf_op jit(solution)/shard_map/ppermute | solution.py:660
  174.1 21.0 %collective-permute-start.3 = (bf16[1,2,64,768]{3,2,1,0:T(8,128)(2,1)}, bf16[1,2,64,768]{3,2,1,0:T(8,128)(2,1)S(1)}, u32[]{:S(2)}, u32[]{:S(2)}) collective-permute-start(bf16[1,2,64,768]{3,2,1,0:T(8,128)(2,1)} %get-tuple-element.50), channel_id=1, source_target_pairs={{4,0},{8,4},{12,8},{16,12},{20,16},{24,20},{28,24},{5,1},{9,5},{13... | collective-permute-start | bytes 589832 | tf_op jit(solution)/shard_map/ppermute | solution.py:660
  175.4 0.7 copy-start.8
  175.4 0.7 copy-start.9
  195.1 0.7 copy-start.5
  195.1 0.7 copy-start.6
Sparse Core Ops, SparseCore 0:
  9.6 24.2 all-gather.3
  35.5 21.0 all-gather.7
  58.1 30.7 all-gather.5
  134.7 60.3 reduce-scatter.1
  198.9 95.0 all-reduce.3

commit v5 on v4

--- a/solution.py
+++ b/solution.py
@@ -13,7 +13,7 @@
 FF = 1152
 WIN = 64
 PAIR = 128
-BLOCK = 128
+BLOCK = 64
 
 epsilon = 1e-05
 rope_base = 10000.0
@@ -68,8 +68,18 @@
 
 
 def own_heads(x):
-    both = jnp.concatenate([x[:HEAD_DIM, :BLOCK], x[HEAD_DIM:, BLOCK:]], axis=0)
-    return both.T
+    turned = x.T
+    first = lax.broadcasted_iota(jnp.int32, (1, PAIR), 1) < HEAD_DIM
+    return jnp.where(first, turned[:BLOCK], turned[BLOCK:])
+
+
+def columns(x):
+    return x.T, x[BLOCK:].T
+
+
+def span_of(pair, i):
+    at = (i - i % 2) * BLOCK
+    return pair[i % 2][:, at : at + BLOCK + 2 * WIN]
 
 
 def fill(dst, left, mid, right):
@@ -82,17 +92,17 @@
 def attend_kernel(q_ref, k_ref, v_ref, lk_ref, lv_ref, rk_ref, rv_ref, bias_ref, att_ref, p_ref, ke, ve):
     fill(ke, lk_ref, k_ref, rk_ref)
     fill(ve, lv_ref, v_ref, rv_ref)
-    vt = ve[...].T
+    vt = columns(ve[...])
     for i in range(q_ref.shape[1] // BLOCK):
         rows = slice(i * BLOCK, (i + 1) * BLOCK)
         span = slice(i * BLOCK, (i + 1) * BLOCK + 2 * WIN)
         scores = mm(ke[span], by_head(q_ref[0, rows]), NT)
-        scores = scores + jnp.concatenate([bias_ref[i]] * 2, axis=1)
+        scores = scores + bias_ref[i]
         raised = jnp.exp(scores - jnp.max(scores, axis=0, keepdims=True))
         total = jnp.sum(raised, axis=0, keepdims=True)
         probs = (raised * (1.0 / total)).astype(bf16)
         p_ref[0, 0, i] = probs
-        att_ref[0, rows] = own_heads(mm(vt[:, span], probs)).astype(bf16)
+        att_ref[0, rows] = own_heads(mm(span_of(vt, i), probs)).astype(bf16)
 
 
 def attend_back_kernel(
@@ -105,7 +115,7 @@
     va[...] = jnp.zeros_like(va)
     count = q_ref.shape[1]
     scale = 1.0 / math.sqrt(HEAD_DIM)
-    kt = ke[...].T
+    kt = columns(ke[...])
     for i in range(count // BLOCK):
         rows = slice(i * BLOCK, (i + 1) * BLOCK)
         span = slice(i * BLOCK, (i + 1) * BLOCK + 2 * WIN)
@@ -115,7 +125,7 @@
         back = mm(ve[span], upstream, NT)
         delta = jnp.sum(probs * back, axis=0, keepdims=True)
         grad = (probs * (back - delta)).astype(bf16)
-        dq = own_heads(mm(kt[:, span], grad)) * scale
+        dq = own_heads(mm(span_of(kt, i), grad)) * scale
         at = slice(WIN + i * BLOCK, WIN + (i + 1) * BLOCK)
         dq_ref[0, rows] = turn(dq, cos_ref[at], -low_ref[at], -high_ref[at]).astype(bf16)
         ka[span] += mm(grad, by_head(q_ref[0, rows]))
@@ -520,7 +530,7 @@
         + jnp.arange(BLOCK + 2 * WIN, dtype=jnp.int32)[None, :, None]
     )
     inside = (jnp.abs(q_at - k_at) <= WIN) & (k_at >= 0) & (k_at < piece * seq_size)
-    bias = jnp.where(inside, 0.0, negative).astype(f32)
+    bias = jnp.tile(jnp.where(inside, 0.0, negative).astype(f32), (1, 1, 2))
 
     tile = 256
     per = piece // tile
@@ -601,7 +611,7 @@
         name="mlp_both_ways",
     )(tok, flat(attended), flat(grad_out), gain_mlp, w_attn, w_in, w_out)
 
-    mlp_sum = lax.psum(lax.psum_scatter(d_mlp, "fsdp", scatter_dimension=0, tiled=True)[0], "seq")
+    mlp_share = lax.psum_scatter(d_mlp, "fsdp", scatter_dimension=0, tiled=True)[0]
 
     table_full = pl.BlockSpec((span, PAIR), lambda p: (0, 0))
     edge_shape = sds((1, 2, WIN, width), bf16)
@@ -668,6 +678,8 @@
     both = both.reshape(2, shares, width // shares).swapaxes(0, 1)
     both = jnp.pad(both, ((0, 0), (0, 0), (0, width - width // shares)))
     d_wqkv = lax.dynamic_update_slice(d_wqkv, both, (0, gains_at, 0))
+    mlp_share, d_wqkv = lax.optimization_barrier((mlp_share, d_wqkv))
+    mlp_sum = lax.psum(mlp_share, "seq")
     qkv_sum = reduce_all(d_wqkv, 4, seq_size)
     s_wqkv = unpack(qkv_sum, (qkv_weight.shape,))[0]
     s_gains = qkv_sum[gains_at : gains_at + 2, : width // shares].astype(f32)

time: 307 us -> 316 us (1.029)
  Pallas kernels: 228 us -> 235 us
    psum x1, waiting for transfers between devices: 4.35 us -> 16.1 us  [shards(): mlp_sum = lax.psum(mlp_share, 'seq')]
    reduce_scatter x1, waiting for transfers between devices: 9.25 us -> 0.01 us  [shards(): lax.psum_scatter(d_mlp, 'fsdp', scatter_dimension=0, tiled=True)[0]]
    pallas_call x1, Pallas kernels: 21.6 us -> 30.7 us  [shards(): pl.pallas_call(attend_kernel, grid=(seqs, pairs), in_specs=[lanes(piece)]...]
    pallas_call x1, Pallas kernels: 78.1 us -> 74.5 us  [reduce_all(): pl.pallas_call(functools.partial(reduce_kernel, seq_size), in_specs=[pl.B...]
  transfers between devices with their start and end apart: 11 -> 11, of which waited for: 3 -> 2; matrix products, arithmetic and copies ran while one was open for 7% -> 7% of each run, Pallas kernels for 63% -> 63%
where the time goes in v5:
time: 316 us; the launch traced here: 315 us
  Pallas kernels  235 us (74%)
  waiting for transfers between devices  19.7 us (6%)
  starting transfers between devices  17.6 us (6%)
  local copies, waits for them, and re-layouts  16.6 us (5%)
  between operations  14.1 us (4%)
  other arithmetic  12.1 us (4%)
    pallas_call x1, Pallas kernels, reduce_all(): pl.pallas_call(functools.partial(reduce_kernel, seq_size), in_specs=[pl.B...  74.5 us
    pallas_call x1, Pallas kernels, shards(): pl.pallas_call(functools.partial(mlp_kernel, rows // wide), grid=(rows //...  35 us
    pallas_call x1, Pallas kernels, gather_weights(): pl.pallas_call(gather_kernel, in_specs=[pl.BlockSpec(memory_space=pl.ANY)...  31.7 us
    pallas_call x1, Pallas kernels, shards(): pl.pallas_call(attend_kernel, grid=(seqs, pairs), in_specs=[lanes(piece)]...  30.7 us
    pallas_call x2, Pallas kernels, attend_back(): pl.pallas_call(attend_back_kernel, grid=(pairs,), in_specs=[at(piece), at...  29.2 us
    pallas_call x2, Pallas kernels, qkv_back(): pl.pallas_call(functools.partial(qkv_back_kernel, len(prior), len(kept),...  20.2 us
    psum x1, waiting for transfers between devices, shards(): mlp_sum = lax.psum(mlp_share, 'seq')  16.1 us
    pallas_call x2, Pallas kernels, project(): pl.pallas_call(qkv_kernel, grid=(count // tile,), in_specs=[row_spec(widt...  13.4 us
  transfers between devices with their start and end apart: 11, of which 2 were waited for; matrix products, arithmetic and copies ran while one was open for 7% of the time, Pallas kernels for 63%

profile of v5, /device:TPU:0, one launch (start us, length us, event | category | flops | bytes accessed | tf_op | source)
XLA Modules:
  0.0 314.8 jit_solution(4113482307881495432)
XLA Ops:
  11.4 31.7 %gather_weights.1 = (bf16[768,2304]{1,0:T(8,128)(2,1)}, bf16[128,256]{1,0:T(8,128)(2,1)}) custom-call(bf16[192,2304]{1,0:T(8,128)(2,1)} %refs_0_.1, bf16[32,256]{1,0:T(8,128)(2,1)} %fusion.9.refs_1_), custom_call_target="tpu_custom_call" | custom-call | bytes 67108864 | tf_op jit(solution)/shard_map/gather_weights/pallas_call | solution.py:356
  44.5 1.2 multiply_sine_fusion
  50.7 4.5 %qkv_forward.3 = (bf16[256,768]{1,0:T(8,128)(2,1)}, bf16[256,1536]{1,0:T(8,128)(2,1)}) custom-call(bf16[256,768]{1,0:T(8,128)(2,1)} %bitcast.40, f32[1,768]{1,0:T(1,128)} %reshape.214.gain_ref, bf16[768,2304]{1,0:T(8,128)(2,1)} %get-tuple-element.39.w_ref, f32[256,128]{1,0:T(8,128)} %bitcast.44, f32[256,128]{1,0:T(8,128)} %bitcast.43, f32[256,128]{1,0:T(8,128)} %bitcast.42), custom_call_target="tpu_custom_call" | custom-call | flops 905969664 | bytes 2359296 | tf_op jit(solution)/shard_map/qkv_forward/pallas_call | solution.py:545
  56.3 1.3 collective-permute-start.1
  57.6 4.6 %collective-permute-start = (bf16[2,64,1536]{2,1,0:T(8,128)(2,1)S(1)}, bf16[2,64,1536]{2,1,0:T(8,128)(2,1)S(1)}, u32[]{:S(2)}, u32[]{:S(2)}) collective-permute-start(bf16[2,64,1536]{2,1,0:T(8,128)(2,1)S(1)} %get-tuple-element.78), channel_id=1, source_target_pairs={{0,4},{4,8},{8,12},{12,16},{16,20},{20,24},{24,28},{1,5},{5,9},{9,... | collective-permute-start | bytes 1179656 | tf_op jit(solution)/shard_map/ppermute | solution.py:562
  66.8 8.9 %qkv_forward.2 = (bf16[1024,768]{1,0:T(8,128)(2,1)}, bf16[1024,1536]{1,0:T(8,128)(2,1)}) custom-call(bf16[1024,768]{1,0:T(8,128)(2,1)} %bitcast.37, f32[1,768]{1,0:T(1,128)} %reshape.214.gain_ref, bf16[768,2304]{1,0:T(8,128)(2,1)} %get-tuple-element.39.w_ref, f32[512,128]{1,0:T(8,128)} %slice.121.cos_ref, f32[512,128]{1,0:T(8,128)} %slice.122.low_ref, ...), custom_call_target="tpu_custom_call" | custom-call | flops 3623878656 | bytes 9437184 | tf_op jit(solution)/shard_map/qkv_forward/pallas_call | solution.py:545
  75.7 1.4 collective-permute-done.lk_ref.lv_ref
  77.9 30.7 %attend_forward.1 = (bf16[2,512,768]{2,1,0:T(8,128)(2,1)}, bf16[2,6,8,192,128]{4,3,2,1,0:T(8,128)(2,1)}) custom-call(bf16[2,512,768]{2,1,0:T(8,128)(2,1)} %bitcast.29, bf16[2,512,1536]{2,1,0:T(8,128)(2,1)} %bitcast.23, bf16[2,512,1536]{2,1,0:T(8,128)(2,1)} %bitcast.24, bf16[2,64,1536]{2,1,0:T(8,128)(2,1)} %copy-done.1, bf16[2,64,1536]{2,1,0:T(8,128)(2,1)} %copy-done.1, ...), custom_call_target="tpu_custom_call" | custom-call | flops 2415919104 | bytes 11010048 | tf_op jit(solution)/shard_map/attend_forward/pallas_call | solution.py:581
  108.6 35.0 %mlp_both_ways.1 = (bf16[1024,768]{1,0:T(8,128)(2,1)}, f32[1024,768]{1,0:T(8,128)}, bf16[1024,768]{1,0:T(8,128)(2,1)}, bf16[4,1056,768]{2,1,0:T(8,128)(2,1)}, f32[1,768]{1,0:T(1,128)}) custom-call(bf16[1024,768]{1,0:T(8,128)(2,1)} %bitcast.38, bf16[1024,768]{1,0:T(8,128)(2,1)} %bitcast.50, bf16[1024,768]{1,0:T(8,128)(2,1)} %bitcast.49, ...), custom_call_target="tpu_custom_call" | custom-call | flops 19931332608 | bytes 41943040 | tf_op jit(solution)/shard_map/mlp_both_ways/pallas_call | solution.py:595
  144.4 14.3 %attend_backward.3 = (bf16[1,512,768]{2,1,0:T(8,128)(2,1)}, bf16[1,512,768]{2,1,0:T(8,128)(2,1)}, bf16[1,512,768]{2,1,0:T(8,128)(2,1)}, bf16[1,2,64,768]{3,2,1,0:T(8,128)(2,1)}, bf16[1,2,64,768]{3,2,1,0:T(8,128)(2,1)}) custom-call(bf16[2,512,768]{2,1,0:T(8,128)(2,1)} %bitcast.30, bf16[2,512,1536]{2,1,0:T(8,128)(2,1)} %bitcast.25, ...), custom_call_target="tpu_custom_call" | custom-call | flops 2415919104 | bytes 8650752 | tf_op jit(solution)/shard_map/attend_backward/pallas_call | solution.py:629
  158.7 4.4 %collective-permute-start.4 = (bf16[1,2,64,768]{3,2,1,0:T(8,128)(2,1)}, bf16[1,2,64,768]{3,2,1,0:T(8,128)(2,1)S(1)}, u32[]{:S(2)}, u32[]{:S(2)}) collective-permute-start(bf16[1,2,64,768]{3,2,1,0:T(8,128)(2,1)} %get-tuple-element.56), channel_id=1, source_target_pairs={{0,4},{4,8},{8,12},{12,16},{16,20},{20,24},{24,28},{1,5},{5,9},{9,... | collective-permute-start | bytes 589832 | tf_op jit(solution)/shard_map/ppermute | solution.py:670
  163.1 1.3 collective-permute-start.5
  164.4 14.9 %attend_backward.2 = (bf16[1,512,768]{2,1,0:T(8,128)(2,1)}, bf16[1,512,768]{2,1,0:T(8,128)(2,1)}, bf16[1,512,768]{2,1,0:T(8,128)(2,1)}, bf16[1,2,64,768]{3,2,1,0:T(8,128)(2,1)}, bf16[1,2,64,768]{3,2,1,0:T(8,128)(2,1)}) custom-call(bf16[2,512,768]{2,1,0:T(8,128)(2,1)} %bitcast.31, bf16[2,512,1536]{2,1,0:T(8,128)(2,1)} %bitcast.27, ...), custom_call_target="tpu_custom_call" | custom-call | flops 2415919104 | bytes 8650752 | tf_op jit(solution)/shard_map/attend_backward/pallas_call | solution.py:629
  179.3 4.6 %collective-permute-start.2 = (bf16[1,2,64,768]{3,2,1,0:T(8,128)(2,1)}, bf16[1,2,64,768]{3,2,1,0:T(8,128)(2,1)S(1)}, u32[]{:S(2)}, u32[]{:S(2)}) collective-permute-start(bf16[1,2,64,768]{3,2,1,0:T(8,128)(2,1)} %get-tuple-element.51), channel_id=1, source_target_pairs={{0,4},{4,8},{8,12},{12,16},{16,20},{20,24},{24,28},{1,5},{5,9},{9,... | collective-permute-start | bytes 589832 | tf_op jit(solution)/shard_map/ppermute | solution.py:670
  183.9 1.3 collective-permute-start.3
  186.0 9.6 %qkv_backward.2 = (f32[2,512,768]{2,1,0:T(8,128)}, bf16[768,2304]{1,0:T(8,128)(2,1)}, f32[1,768]{1,0:T(1,128)}) custom-call(bf16[2,512,768]{2,1,0:T(8,128)(2,1)} %tok_ref.3, f32[2,512,768]{2,1,0:T(8,128)} %bitcast.35, bf16[1,512,768]{2,1,0:T(8,128)(2,1)} %get-tuple-element.53.dq_ref, bf16[1,512,768]{2,1,0:T(8,128)(2,1)} %get-tuple-element.54.dk_ref, ...), custom_call_target="tpu_custom_call" | custom-call | flops 3623878656 | bytes 7864320 | tf_op jit(solution)/shard_map/qkv_backward/pallas_call | solution.py:653
  196.4 10.6 %qkv_backward.3 = (f32[2,512,768]{2,1,0:T(8,128)}, bf16[4,640,768]{2,1,0:T(8,128)(2,1)}, f32[1,768]{1,0:T(1,128)}) custom-call(bf16[2,512,768]{2,1,0:T(8,128)(2,1)} %tok_ref.3, f32[2,512,768]{2,1,0:T(8,128)} %bitcast.36, bf16[1,512,768]{2,1,0:T(8,128)(2,1)} %get-tuple-element.48.dq_ref, ...), custom_call_target="tpu_custom_call", output_to_operand_aliasing={{0}: (11, {})} | custom-call | flops 3623878656 | bytes 7864320 | tf_op jit(solution)/shard_map/qkv_backward/pallas_call | solution.py:653
  208.4 74.5 %reduce_all.1 = bf16[640,768]{1,0:T(8,128)(2,1)} custom-call(bf16[4,640,768]{2,1,0:T(8,128)(2,1)} %pad_dynamic-update-slice_fusion.pack_ref), custom_call_target="tpu_custom_call" | custom-call | bytes 67108864 | tf_op jit(solution)/shard_map/reduce_all/pallas_call | solution.py:465
  284.2 1.2 fusion.14
  285.4 1.3 maximum_convert_fusion
  286.7 16.1 %all-reduce.4.cloned.1.call-done = bf16[1056,768]{1,0:T(8,128)(2,1)} async-done(((bf16[1056,768]{1,0:T(8,128)(2,1)}), bf16[1056,768]{1,0:T(8,128)(2,1)}) %all-reduce.4.cloned.1.call-update) | async-done | bytes 1622032 | tf_op jit(solution)/shard_map/psum | solution.py:682
  302.9 2.1 fusion.12
  305.0 1.3 maximum_convert_fusion.1
  306.3 2.0 slice_convert_fusion
  (81 shorter events, 21.9 us)
Async XLA Ops:
  7.2 101.4 %all-gather.4.cloned.1.call-start = ((), (), s32[]{:S(2)}) async-start(), calls=%async_computation.1 | async-start | bytes 1474560 | tf_op jit(solution)/shard_map/all_gather | solution.py:513
  7.9 100.7 %all-gather.8.cloned.1.call-start = ((), (), s32[]{:S(2)}) async-start(), calls=%async_computation.3 | async-start | bytes 2211840 | tf_op jit(solution)/shard_map/all_gather | solution.py:513
  8.7 100.0 %all-gather.6.cloned.1.call-start = ((), (), s32[]{:S(2)}) async-start(), calls=%async_computation.2 | async-start | bytes 4423680 | tf_op jit(solution)/shard_map/all_gather | solution.py:513
  9.4 198.9 %reduce-scatter.2.cloned.1.call-start = ((), (), s32[]{:S(2)}) async-start(), calls=%async_computation.4 | async-start | bytes 8110080 | tf_op jit(solution)/shard_map/reduce_scatter | solution.py:614
  46.3 16.3 %copy-start.3 = (f32[640,128]{1,0:T(8,128)}, f32[640,128]{1,0:T(8,128)S(1)}, u32[]{:S(2)}) copy-start(f32[640,128]{1,0:T(8,128)S(1)} %get-tuple-element.85.high_ref) | copy-start | bytes 983044
  46.3 17.0 %copy-start.4 = (f32[640,128]{1,0:T(8,128)}, f32[640,128]{1,0:T(8,128)S(1)}, u32[]{:S(2)}) copy-start(f32[640,128]{1,0:T(8,128)S(1)} %get-tuple-element.86.low_ref) | copy-start | bytes 983044
  46.7 17.4 %copy-start.2 = (f32[640,128]{1,0:T(8,128)}, f32[640,128]{1,0:T(8,128)S(1)}, u32[]{:S(2)}) copy-start(f32[640,128]{1,0:T(8,128)S(1)} %pad_maximum_fusion.1.cos_ref) | copy-start | bytes 983044
  56.3 19.4 %collective-permute-start.1 = (bf16[2,64,1536]{2,1,0:T(8,128)(2,1)S(1)}, bf16[2,64,1536]{2,1,0:T(8,128)(2,1)S(1)}, u32[]{:S(2)}, u32[]{:S(2)}) collective-permute-start(bf16[2,64,1536]{2,1,0:T(8,128)(2,1)S(1)} %get-tuple-element.77), channel_id=1, source_target_pairs={{4,0},{8,4},{12,8},{16,12},{20,16},{24,20},{28,24},{5,1},{9,5},{13... | collective-permute-start | bytes 1179656 | tf_op jit(solution)/shard_map/ppermute | solution.py:563
  57.6 19.5 %collective-permute-start = (bf16[2,64,1536]{2,1,0:T(8,128)(2,1)S(1)}, bf16[2,64,1536]{2,1,0:T(8,128)(2,1)S(1)}, u32[]{:S(2)}, u32[]{:S(2)}) collective-permute-start(bf16[2,64,1536]{2,1,0:T(8,128)(2,1)S(1)} %get-tuple-element.78), channel_id=1, source_target_pairs={{0,4},{4,8},{8,12},{12,16},{16,20},{20,24},{24,28},{1,5},{5,9},{9,... | collective-permute-start | bytes 1179656 | tf_op jit(solution)/shard_map/ppermute | solution.py:562
  75.7 1.4 copy-start
  77.1 0.7 copy-start.1
  143.6 0.7 copy-start.7
  143.6 159.2 %all-reduce.4.cloned.1.call-start = ((), (), s32[]{:S(2)}) async-start(), calls=%async_computation.5 | async-start | bytes 3244032 | tf_op jit(solution)/shard_map/psum | solution.py:682
  158.7 26.5 %collective-permute-start.4 = (bf16[1,2,64,768]{3,2,1,0:T(8,128)(2,1)}, bf16[1,2,64,768]{3,2,1,0:T(8,128)(2,1)S(1)}, u32[]{:S(2)}, u32[]{:S(2)}) collective-permute-start(bf16[1,2,64,768]{3,2,1,0:T(8,128)(2,1)} %get-tuple-element.56), channel_id=1, source_target_pairs={{0,4},{4,8},{8,12},{12,16},{16,20},{20,24},{24,28},{1,5},{5,9},{9,... | collective-permute-start | bytes 589832 | tf_op jit(solution)/shard_map/ppermute | solution.py:670
  163.1 22.1 %collective-permute-start.5 = (bf16[1,2,64,768]{3,2,1,0:T(8,128)(2,1)}, bf16[1,2,64,768]{3,2,1,0:T(8,128)(2,1)S(1)}, u32[]{:S(2)}, u32[]{:S(2)}) collective-permute-start(bf16[1,2,64,768]{3,2,1,0:T(8,128)(2,1)} %get-tuple-element.57), channel_id=1, source_target_pairs={{4,0},{8,4},{12,8},{16,12},{20,16},{24,20},{28,24},{5,1},{9,5},{13... | collective-permute-start | bytes 589832 | tf_op jit(solution)/shard_map/ppermute | solution.py:670
  179.3 16.3 %collective-permute-start.2 = (bf16[1,2,64,768]{3,2,1,0:T(8,128)(2,1)}, bf16[1,2,64,768]{3,2,1,0:T(8,128)(2,1)S(1)}, u32[]{:S(2)}, u32[]{:S(2)}) collective-permute-start(bf16[1,2,64,768]{3,2,1,0:T(8,128)(2,1)} %get-tuple-element.51), channel_id=1, source_target_pairs={{0,4},{4,8},{8,12},{12,16},{16,20},{20,24},{24,28},{1,5},{5,9},{9,... | collective-permute-start | bytes 589832 | tf_op jit(solution)/shard_map/ppermute | solution.py:670
  183.9 11.7 %collective-permute-start.3 = (bf16[1,2,64,768]{3,2,1,0:T(8,128)(2,1)}, bf16[1,2,64,768]{3,2,1,0:T(8,128)(2,1)S(1)}, u32[]{:S(2)}, u32[]{:S(2)}) collective-permute-start(bf16[1,2,64,768]{3,2,1,0:T(8,128)(2,1)} %get-tuple-element.52), channel_id=1, source_target_pairs={{4,0},{8,4},{12,8},{16,12},{20,16},{24,20},{28,24},{5,1},{9,5},{13... | collective-permute-start | bytes 589832 | tf_op jit(solution)/shard_map/ppermute | solution.py:670
  185.2 0.7 copy-start.8
  185.2 0.7 copy-start.9
  195.6 0.7 copy-start.5
  195.6 0.7 copy-start.6
Sparse Core Ops, SparseCore 0:
  9.6 24.2 all-gather.3
  35.5 21.0 all-gather.7
  58.1 30.7 all-gather.5
  143.8 60.3 reduce-scatter.1
  208.5 94.3 all-reduce.3
